TPU v7x, 32 devices: a whole 2x2x4 slice. The times are simulated.
32 devices in a mesh: section: 2 (over core), fsdp: 16 (over z, y, x).
Axes of the slice: x: 2, y: 2, z: 4, core: 2. Of those that a mesh axis runs over, the one named last changes fastest.
Arguments:
- token_ids: int32 [2, 16, 128], P('section', 'fsdp'), may hold values from 0 to 50303
- target_ids: int32 [2, 16, 128], P('section', 'fsdp'), may hold values from 0 to 50303
- true_counts: int32 [2, 16], replicated, may hold values from 32 to 128, as said below
- embed_table: float32 [50304, 768], P('fsdp')
- embed_m: float32 [50304, 768], P('fsdp'), may hold values from -1.9073486e-06 to 1.9073486e-06
- embed_v: float32 [50304, 768], P('fsdp'), may hold values from 6.3649325e-12 to 2.5535503e-11
- pos_table: float32 [128, 768], P(None, 'fsdp'), may hold values from -1.75 to 1.75
- pos_m: float32 [128, 768], P(None, 'fsdp'), may hold values from -1.9073486e-06 to 1.9073486e-06
- pos_v: float32 [128, 768], P(None, 'fsdp'), may hold values from 3.98566e-13 to 1.594264e-12
- w_qkv: float32 [2, 768, 2304], P('section', None, 'fsdp'), may hold values from -0.21875 to 0.21875
- w_proj: float32 [2, 768, 768], P('section', None, 'fsdp'), may hold values from -0.4375 to 0.4375
- w_fc: float32 [2, 768, 3072], P('section', None, 'fsdp'), may hold values from -0.21875 to 0.21875
- w_down: float32 [2, 768, 3072], P('section', None, 'fsdp'), may hold values from -0.109375 to 0.109375
- mom_qkv: float32 [2, 768, 2304], P('section', None, 'fsdp'), may hold values from -1.5258789e-05 to 1.5258789e-05
- mom_proj: float32 [2, 768, 768], P('section', None, 'fsdp'), may hold values from -1.5258789e-05 to 1.5258789e-05
- mom_fc: float32 [2, 768, 3072], P('section', None, 'fsdp'), may hold values from -1.5258789e-05 to 1.5258789e-05
- mom_down: float32 [2, 768, 3072], P('section', None, 'fsdp'), may hold values from -1.5258789e-05 to 1.5258789e-05
- layer_vecs: float32 [2, 12, 768], P('section', None, 'fsdp')
- vecs_m: float32 [2, 12, 768], P('section', None, 'fsdp'), may hold values from -9.536743e-06 to 9.536743e-06
- vecs_v: float32 [2, 12, 768], P('section', None, 'fsdp'), may hold values from 9.96415e-12 to 3.98566e-11
- final_norm: float32 [2, 768], P(None, 'fsdp')
- norm_m: float32 [2, 768], P(None, 'fsdp'), may hold values from -9.536743e-06 to 9.536743e-06
- norm_v: float32 [2, 768], P(None, 'fsdp'), may hold values from 9.96415e-12 to 3.98566e-11
Outputs:
- loss_sum: float32 [], replicated
- clip_norm: float32 [], replicated
- embed_new: float32 [50304, 768], P('fsdp')
- embed_low: bfloat16 [50304, 768], P('fsdp')
- embed_m_new: float32 [50304, 768], P('fsdp')
- embed_v_new: float32 [50304, 768], P('fsdp')
- pos_new: float32 [128, 768], P(None, 'fsdp')
- pos_m_new: float32 [128, 768], P(None, 'fsdp')
- pos_v_new: float32 [128, 768], P(None, 'fsdp')
- qkv_new: float32 [2, 768, 2304], P('section', None, 'fsdp')
- qkv_low: bfloat16 [2, 768, 2304], P('section', None, 'fsdp')
- qkv_mom: float32 [2, 768, 2304], P('section', None, 'fsdp')
- proj_new: float32 [2, 768, 768], P('section', None, 'fsdp')
- proj_low: bfloat16 [2, 768, 768], P('section', None, 'fsdp')
- proj_mom: float32 [2, 768, 768], P('section', None, 'fsdp')
- fc_new: float32 [2, 768, 3072], P('section', None, 'fsdp')
- fc_low: bfloat16 [2, 768, 3072], P('section', None, 'fsdp')
- fc_mom: float32 [2, 768, 3072], P('section', None, 'fsdp')
- down_new: float32 [2, 768, 3072], P('section', None, 'fsdp')
- down_low: bfloat16 [2, 768, 3072], P('section', None, 'fsdp')
- down_mom: float32 [2, 768, 3072], P('section', None, 'fsdp')
- vecs_new: float32 [2, 12, 768], P('section', None, 'fsdp')
- vecs_m_new: float32 [2, 12, 768], P('section', None, 'fsdp')
- vecs_v_new: float32 [2, 12, 768], P('section', None, 'fsdp')
- norm_new: float32 [2, 768], P(None, 'fsdp')
- norm_m_new: float32 [2, 768], P(None, 'fsdp')
- norm_v_new: float32 [2, 768], P(None, 'fsdp')
Inputs may be any that keep to these rules, and one draw needn't show every extreme that they name: `true_counts`: leading positions of a sequence that count in the loss; the last sequence of each micro-batch counts all 128.
All inputs are finite; a program needn't handle non-finite values.
Results may differ from a plain program's by a relative error of at most 0.0075.
The roundings to bfloat16 on the way count: a program that leaves them out, or rounds other values in their place, can miss the bound.
Values may be sent and summed in bfloat16 or wider, within the bound.
No kernel may reach another device: no remote copies, remote signals or barrier semaphores. Data moves between devices by JAX's collectives and lax.ppermute only.
A program may use at most 168 MiB of HBM per device.

v0:
```python
import math

import jax
import jax.numpy as jnp
from jax import lax
from jax.sharding import PartitionSpec as P

HD = 64
STEP = 10


LN_EPS = 1e-05
NEG_FILL = -1e30
Z_WEIGHT = 0.01
CLIP_NORM = 0.02
MOMENTUM = 0.5
MUON_RATE = 0.7
MUON_DECAY = 0.01
ADAM_ONE = 0.9
ADAM_TWO = 0.95
ADAM_EPS = 1e-08
ADAM_DECAY = 0.1
RATE_EMBED = 0.12
RATE_POS = 0.1
RATE_VEC = 0.2
NEWTON_COEFS = (3.4445, -4.775, 2.0315)
PRECISE = lax.Precision.HIGHEST


def from_behind(block, axis, distance):
    devices = range(lax.axis_size(axis))
    route = [((i - distance) % len(devices), i) for i in devices]
    return lax.ppermute(block, axis, route)


def combined_all(part, axis, combine):
    gathered = jax.tree.map(lambda a: lax.all_gather(a, axis), part)

    def take(source):
        return jax.tree.map(lambda a: lax.dynamic_index_in_dim(a, source, 0, False), gathered)

    return lax.fori_loop(
        1, lax.axis_size(axis), lambda source, state: combine(state, take(source)), take(0)
    )


def layer_norm(values, gain_row, bias_row):
    average = jnp.mean(values, -1, keepdims=True)
    centered = values - average
    variance = jnp.mean(centered * centered, -1, keepdims=True)
    return centered * lax.rsqrt(variance + LN_EPS) * gain_row + bias_row


def split_vectors(vectors):
    return (
        vectors[0],
        vectors[1],
        vectors[2],
        vectors[3],
        vectors[4],
        vectors[5],
        vectors[6],
        vectors[7:11].reshape(-1),
        vectors[11],
    )


def contract_rows(left_mat, right_mat):
    return lax.dot_general(
        left_mat, right_mat, (((0,), (0,)), ((), ())), preferred_element_type=jnp.float32
    )


def contract_cols(left_mat, right_mat):
    return lax.dot_general(
        left_mat, right_mat, (((1,), (1,)), ((), ())), preferred_element_type=jnp.float32
    )


def gelu_tanh(values):
    return jax.nn.gelu(values, approximate=True)


def precise_mul(left_mat, right_mat):
    return jnp.matmul(left_mat, right_mat, precision=PRECISE)


def layer_forward(inputs, weights):
    w_qkv, w_proj, w_fc, w_down, vectors = weights
    g_one, b_one, q_bias, v_bias, p_bias, g_two, b_two, f_bias, d_bias = split_vectors(vectors)
    seq_len, model_width = inputs.shape
    head_count = model_width // HD
    factor = HD ** (-0.5)
    normed_a = layer_norm(inputs, g_one, b_one).astype(jnp.bfloat16)
    bias_qkv = jnp.concatenate([q_bias, jnp.zeros_like(q_bias), v_bias])
    qkv_rows = (jnp.dot(normed_a, w_qkv, preferred_element_type=jnp.float32) + bias_qkv).astype(
        jnp.bfloat16
    )
    queries = qkv_rows[:, :model_width].reshape(seq_len, head_count, HD)
    keys_all = qkv_rows[:, model_width : 2 * model_width].reshape(seq_len, head_count, HD)
    values_all = qkv_rows[:, 2 * model_width :].reshape(seq_len, head_count, HD)
    scores = (
        jnp.einsum("qhd,khd->hqk", queries, keys_all, preferred_element_type=jnp.float32) * factor
    )
    causal = lax.broadcasted_iota(jnp.int32, (seq_len, seq_len), 0) >= lax.broadcasted_iota(
        jnp.int32, (seq_len, seq_len), 1
    )
    attn_probs = jax.nn.softmax(jnp.where(causal, scores, NEG_FILL), axis=-1)
    probs_low = attn_probs.astype(jnp.bfloat16)
    attended = jnp.einsum("hqk,khd->qhd", probs_low, values_all, preferred_element_type=jnp.float32)
    attended = attended.reshape(seq_len, model_width).astype(jnp.bfloat16)
    after_attn = inputs + jnp.dot(attended, w_proj, preferred_element_type=jnp.float32) + p_bias
    normed_b = layer_norm(after_attn, g_two, b_two).astype(jnp.bfloat16)
    hidden_pre = jnp.dot(normed_b, w_fc, preferred_element_type=jnp.float32) + f_bias
    hidden_low = gelu_tanh(hidden_pre).astype(jnp.bfloat16)
    outputs = after_attn + contract_cols(hidden_low, w_down) + d_bias
    saved = (
        normed_a,
        queries,
        keys_all,
        values_all,
        attn_probs,
        probs_low,
        attended,
        after_attn,
        normed_b,
        hidden_pre,
        hidden_low,
    )
    return (outputs, saved)


def layer_backward(inputs, grad_out, weights):
    w_qkv, w_proj, w_fc, w_down, vectors = weights
    g_one, b_one, q_bias, v_bias, p_bias, g_two, b_two, f_bias, d_bias = split_vectors(vectors)
    seq_len, model_width = inputs.shape
    factor = HD ** (-0.5)
    unused, saved = layer_forward(inputs, weights)
    (
        normed_a,
        queries,
        keys_all,
        values_all,
        attn_probs,
        probs_low,
        attended,
        after_attn,
        normed_b,
        hidden_pre,
        hidden_low,
    ) = saved
    grad_mlp = grad_out.astype(jnp.bfloat16)
    d_dbias = jnp.sum(grad_mlp, 0, dtype=jnp.float32)
    d_down = contract_rows(grad_mlp, hidden_low)
    grad_hidden = jnp.dot(grad_mlp, w_down, preferred_element_type=jnp.float32)
    grad_pre = jax.vjp(gelu_tanh, hidden_pre)[1](grad_hidden)[0].astype(jnp.bfloat16)
    d_fbias = jnp.sum(grad_pre, 0, dtype=jnp.float32)
    d_fc = contract_rows(normed_b, grad_pre)
    grad_nb = contract_cols(grad_pre, w_fc)
    ln_two = jax.vjp(layer_norm, after_attn, g_two, b_two)[1](grad_nb)
    grad_mid = grad_out + ln_two[0]
    grad_attn = grad_mid.astype(jnp.bfloat16)
    d_pbias = jnp.sum(grad_attn, 0, dtype=jnp.float32)
    d_proj = contract_rows(attended, grad_attn)
    grad_att = contract_cols(grad_attn, w_proj).reshape(queries.shape).astype(jnp.bfloat16)
    grad_probs = jnp.einsum(
        "qhd,khd->hqk", grad_att, values_all, preferred_element_type=jnp.float32
    )
    grad_vals = jnp.einsum("hqk,qhd->khd", probs_low, grad_att, preferred_element_type=jnp.float32)
    grad_scores = attn_probs * (grad_probs - jnp.sum(grad_probs * attn_probs, -1, keepdims=True))
    grad_scores = grad_scores.astype(jnp.bfloat16)
    grad_q = (
        jnp.einsum("hqk,khd->qhd", grad_scores, keys_all, preferred_element_type=jnp.float32)
        * factor
    )
    grad_k = (
        jnp.einsum("hqk,qhd->khd", grad_scores, queries, preferred_element_type=jnp.float32)
        * factor
    )
    grad_qkv = jnp.concatenate(
        [
            grad_q.reshape(seq_len, model_width),
            grad_k.reshape(seq_len, model_width),
            grad_vals.reshape(seq_len, model_width),
        ],
        -1,
    ).astype(jnp.bfloat16)
    qkv_sums = jnp.sum(grad_qkv, 0, dtype=jnp.float32)
    d_qkv = contract_rows(normed_a, grad_qkv)
    grad_na = contract_cols(grad_qkv, w_qkv)
    ln_one = jax.vjp(layer_norm, inputs, g_one, b_one)[1](grad_na)
    grad_in = grad_mid + ln_one[0]
    d_vectors = jnp.concatenate(
        [
            jnp.stack(
                [
                    ln_one[1],
                    ln_one[2],
                    qkv_sums[:model_width],
                    qkv_sums[2 * model_width :],
                    d_pbias,
                    ln_two[1],
                    ln_two[2],
                ]
            ),
            d_fbias.reshape(4, model_width),
            d_dbias[None],
        ],
        0,
    )
    return (grad_in, (d_qkv, d_proj, d_fc, d_down, d_vectors))


def adam_step(weights_in, gradient, first_mom, second_mom, step_rate):
    first_new = ADAM_ONE * first_mom + (1.0 - ADAM_ONE) * gradient
    second_new = ADAM_TWO * second_mom + (1.0 - ADAM_TWO) * gradient * gradient
    first_hat = first_new / (1.0 - ADAM_ONE**STEP)
    second_hat = second_new / (1.0 - ADAM_TWO**STEP)
    weights_new = weights_in - step_rate * (
        first_hat / (jnp.sqrt(second_hat) + ADAM_EPS) + ADAM_DECAY * weights_in
    )
    return (weights_new, first_new, second_new)


def combine_parts(earlier, latter):
    highest = jnp.maximum(earlier[0], latter[0])
    merged_sum = earlier[1] * jnp.exp(earlier[0] - highest) + latter[1] * jnp.exp(
        latter[0] - highest
    )
    return (highest, merged_sum, earlier[2] + latter[2])


def gram_halves(iterates, half_width):
    gram_parts = [precise_mul(iterate, iterate.T) for iterate in iterates]
    return (
        jnp.stack([gram_part[:, :half_width] for gram_part in gram_parts]),
        jnp.stack([gram_part[half_width:, half_width:] for gram_part in gram_parts]),
    )


def assemble_gram(summed, number, half_width):
    left_half = summed[0][number]
    right_half = jnp.concatenate([left_half[half_width:].T, summed[1][number]], 0)
    return jnp.concatenate([left_half, right_half], 1)


def shards(
    token_ids,
    target_ids,
    true_counts,
    embed_table,
    embed_m,
    embed_v,
    pos_table,
    pos_m,
    pos_v,
    w_qkv,
    w_proj,
    w_fc,
    w_down,
    mom_qkv,
    mom_proj,
    mom_fc,
    mom_down,
    layer_vecs,
    vecs_m,
    vecs_v,
    final_norm,
    norm_m,
    norm_v,
):
    section_index = lax.axis_index("section")
    shard_rows = embed_table.shape[0]
    vocab_start = lax.axis_index("fsdp") * shard_rows
    table_low = embed_table.astype(jnp.bfloat16)

    def fetch_layer():
        pieces = (
            lax.all_gather(w_qkv.astype(jnp.bfloat16), "fsdp", axis=2, tiled=True),
            lax.all_gather(w_proj.astype(jnp.bfloat16), "fsdp", axis=2, tiled=True),
            lax.all_gather(w_fc.astype(jnp.bfloat16), "fsdp", axis=2, tiled=True),
            lax.all_gather(w_down.astype(jnp.bfloat16), "fsdp", axis=2, tiled=True),
            lax.all_gather(layer_vecs.astype(jnp.bfloat16), "fsdp", axis=2, tiled=True),
            lax.all_gather(pos_table.astype(jnp.bfloat16), "fsdp", axis=1, tiled=True),
            lax.all_gather(final_norm.astype(jnp.bfloat16), "fsdp", axis=1, tiled=True),
        )
        layer_set = (
            pieces[0][0],
            pieces[1][0],
            pieces[2][0],
            pieces[3][0],
            pieces[4][0].astype(jnp.float32),
        )
        return (layer_set, pieces[5].astype(jnp.float32), pieces[6].astype(jnp.float32))

    first_set, positions, head_norm = fetch_layer()

    def layer_now():
        return fetch_layer()[0]

    ids_all, targets_all = (
        lax.all_gather(token_ids[0], "fsdp", axis=0, tiled=True),
        lax.all_gather(target_ids[0], "fsdp", axis=0, tiled=True),
    )
    seq_count, seq_len = ids_all.shape
    local_ids = ids_all - vocab_start
    inside = (local_ids >= 0) & (local_ids < shard_rows)
    safe_ids = jnp.clip(local_ids, 0, shard_rows - 1)
    contrib = jnp.where(
        inside[..., None], jnp.take(table_low, safe_ids, axis=0), jnp.zeros((), jnp.bfloat16)
    )
    received = lax.all_to_all(contrib, "fsdp", split_axis=0, concat_axis=0, tiled=True)
    embedded = jnp.sum(received, 0, dtype=jnp.float32) + positions
    kept_inputs = []
    arrived = embedded
    for clock_tick in range(3):
        weights = first_set if clock_tick == 0 else layer_now()
        current = embedded if clock_tick == 0 else arrived
        kept_inputs.append(current)
        outputs, unused = layer_forward(current, weights)
        if clock_tick < 2:
            payload = (
                jnp.where(section_index == 0, outputs, embedded) if clock_tick == 0 else outputs
            )
            arrived = from_behind(payload, "section", 1)
    final_rows = jnp.where(section_index == 0, arrived, outputs)
    normed_low = layer_norm(final_rows, head_norm[0], head_norm[1]).astype(jnp.bfloat16)
    rows_all = lax.all_gather(normed_low, "fsdp", axis=0, tiled=True)
    token_rows = rows_all.shape[0]
    block_rows = min(1024, token_rows)
    block_count = token_rows // block_rows
    counts_row = jnp.take(true_counts, section_index, axis=0)
    counted = lax.broadcasted_iota(jnp.int32, (seq_count, seq_len), 1) < counts_row[:, None]
    counted = counted.astype(jnp.float32).reshape(-1)
    token_total = jnp.sum(true_counts).astype(jnp.float32)
    local_targets = targets_all.reshape(-1) - vocab_start
    vocab_cols = lax.broadcasted_iota(jnp.int32, (block_rows, shard_rows), 1)

    def block_logits(block_idx):
        start = block_idx * block_rows
        row_block = lax.dynamic_slice_in_dim(rows_all, start, block_rows, 0)
        target_block = lax.dynamic_slice_in_dim(local_targets, start, block_rows, 0)
        return (row_block, target_block, contract_cols(row_block, table_low))

    def block_stats(block_idx):
        row_block, target_block, logits = block_logits(block_idx)
        block_max = jnp.max(logits, -1)
        exp_total = jnp.sum(jnp.exp(logits - block_max[:, None]), -1)
        target_logit = jnp.sum(jnp.where(vocab_cols == target_block[:, None], logits, 0.0), -1)
        return (block_max, exp_total, target_logit)

    stats = lax.map(block_stats, jnp.arange(block_count, dtype=jnp.int32))
    merged = combined_all(
        (stats[0].reshape(-1), stats[1].reshape(-1), stats[2].reshape(-1)), "fsdp", combine_parts
    )
    partition = merged[0] + jnp.log(merged[1])
    loss_part = jnp.sum(counted * (partition - merged[2] + Z_WEIGHT * partition * partition))
    token_weight = counted / token_total

    def block_back(table_grad, block_idx):
        row_block, target_block, logits = block_logits(block_idx)
        part_block = lax.dynamic_slice_in_dim(partition, block_idx * block_rows, block_rows, 0)
        weight_block = lax.dynamic_slice_in_dim(token_weight, block_idx * block_rows, block_rows, 0)
        soft_max = (
            jnp.exp(logits - part_block[:, None]) * (1.0 + 2.0 * Z_WEIGHT * part_block)[:, None]
        )
        onehot = (vocab_cols == target_block[:, None]).astype(jnp.float32)
        grad_logit = (weight_block[:, None] * (soft_max - onehot)).astype(jnp.bfloat16)
        table_grad = table_grad + contract_rows(grad_logit, row_block)
        return (table_grad, jnp.dot(grad_logit, table_low, preferred_element_type=jnp.float32))

    table_grad, grad_blocks = lax.scan(
        block_back,
        jnp.zeros(embed_table.shape, jnp.float32),
        jnp.arange(block_count, dtype=jnp.int32),
    )
    grad_normed = lax.psum_scatter(
        grad_blocks.reshape(token_rows, -1), "fsdp", scatter_dimension=0, tiled=True
    )
    grad_final, d_fgain, d_fbias = jax.vjp(layer_norm, final_rows, head_norm[0], head_norm[1])[1](
        grad_normed
    )
    totals = jax.tree.map(lambda item: jnp.zeros(item.shape, jnp.float32), first_set)
    arrived = grad_final
    for back_tick in range(3):
        clock_tick = 2 - back_tick
        weights = layer_now()
        grad_out = grad_final if back_tick == 0 else arrived
        grad_in, grads = layer_backward(kept_inputs[clock_tick], grad_out, weights)
        live = ((clock_tick - section_index >= 0) & (clock_tick - section_index <= 1)).astype(
            jnp.float32
        )
        totals = jax.tree.map(
            lambda total_item, grad_item: total_item + live * grad_item, totals, grads
        )
        if back_tick < 2:
            payload = (
                jnp.where(section_index == 1, grad_in, grad_final) if back_tick == 0 else grad_in
            )
            arrived = from_behind(payload, "section", 1)
    grad_embedded = jnp.where(section_index == 0, grad_in, arrived)
    gathered = lax.all_gather(grad_embedded, "fsdp", axis=0, tiled=True)
    flat_inside = inside.reshape(-1)
    table_grad = table_grad.at[safe_ids.reshape(-1)].add(
        jnp.where(flat_inside[:, None], gathered, 0.0)
    )
    norm_grad = jnp.stack([d_fgain, d_fbias])
    flushed = (
        lax.psum_scatter(totals[0], "fsdp", scatter_dimension=1, tiled=True),
        lax.psum_scatter(totals[1], "fsdp", scatter_dimension=1, tiled=True),
        lax.psum_scatter(totals[2], "fsdp", scatter_dimension=1, tiled=True),
        lax.psum_scatter(totals[3], "fsdp", scatter_dimension=1, tiled=True),
        lax.psum_scatter(totals[4], "fsdp", scatter_dimension=1, tiled=True),
        lax.psum_scatter(grad_embedded, "fsdp", scatter_dimension=1, tiled=True),
        lax.psum_scatter(norm_grad, "fsdp", scatter_dimension=1, tiled=True),
    )
    shared = lax.psum((table_grad, flushed[5], flushed[6], loss_part), "section")
    own_squares = sum((jnp.sum(item * item) for item in flushed[:5]))
    shared_squares = sum((jnp.sum(item * item) for item in shared[:3]))
    square_sum = lax.psum(
        own_squares + jnp.where(section_index == 0, shared_squares, 0.0), ("section", "fsdp")
    )
    clip_norm = jnp.sqrt(square_sum)
    factor = jnp.minimum(1.0, CLIP_NORM / (clip_norm + 1e-06))
    embed_new, embed_m_new, embed_v_new = adam_step(
        embed_table, factor * shared[0], embed_m, embed_v, RATE_EMBED
    )
    pos_new, pos_m_new, pos_v_new = adam_step(pos_table, factor * shared[1], pos_m, pos_v, RATE_POS)
    norm_new, norm_m_new, norm_v_new = adam_step(
        final_norm, factor * shared[2], norm_m, norm_v, RATE_VEC
    )
    vecs_new, vecs_m_new, vecs_v_new = adam_step(
        layer_vecs, factor * flushed[4][None], vecs_m, vecs_v, RATE_VEC
    )
    masters = (w_qkv[0], w_proj[0], w_fc[0], w_down[0])
    moments = (mom_qkv[0], mom_proj[0], mom_fc[0], mom_down[0])
    new_moms = [MOMENTUM * moments[number] + factor * flushed[number] for number in range(4)]
    model_width = masters[0].shape[0]
    half_width = model_width // 2
    summed = lax.psum(gram_halves(new_moms, half_width), "fsdp")
    identity = jnp.eye(model_width, dtype=jnp.float32)
    iterates = []
    for number in range(4):
        full_gram = assemble_gram(summed, number, half_width)
        inverse = 1.0 / (jnp.sqrt(jnp.trace(full_gram)) + 1e-07)
        gram_now = full_gram * (inverse * inverse)
        product = identity
        for iteration in range(5):
            squared = precise_mul(gram_now, gram_now)
            poly = (
                NEWTON_COEFS[0] * identity + NEWTON_COEFS[1] * gram_now + NEWTON_COEFS[2] * squared
            )
            product = precise_mul(poly, product)
            if iteration < 4:
                gram_now = precise_mul(poly, precise_mul(gram_now, poly))
        iterates.append(precise_mul(product, new_moms[number] * inverse))
    results = []
    for number in range(4):
        column_factor = math.sqrt(masters[number].shape[1] * lax.axis_size("fsdp") / model_width)
        new_master = masters[number] - MUON_RATE * (
            column_factor * iterates[number] + MUON_DECAY * masters[number]
        )
        results.append(
            (new_master[None], new_master[None].astype(jnp.bfloat16), new_moms[number][None])
        )
    return (
        shared[3],
        clip_norm,
        embed_new,
        embed_new.astype(jnp.bfloat16),
        embed_m_new,
        embed_v_new,
        pos_new,
        pos_m_new,
        pos_v_new,
        results[0][0],
        results[0][1],
        results[0][2],
        results[1][0],
        results[1][1],
        results[1][2],
        results[2][0],
        results[2][1],
        results[2][2],
        results[3][0],
        results[3][1],
        results[3][2],
        vecs_new,
        vecs_m_new,
        vecs_v_new,
        norm_new,
        norm_m_new,
        norm_v_new,
    )


def solution(mesh):
    in_specs = (
        P("section", "fsdp", None),
        P("section", "fsdp", None),
        P(),
        P("fsdp", None),
        P("fsdp", None),
        P("fsdp", None),
        P(None, "fsdp"),
        P(None, "fsdp"),
        P(None, "fsdp"),
        P("section", None, "fsdp"),
        P("section", None, "fsdp"),
        P("section", None, "fsdp"),
        P("section", None, "fsdp"),
        P("section", None, "fsdp"),
        P("section", None, "fsdp"),
        P("section", None, "fsdp"),
        P("section", None, "fsdp"),
        P("section", None, "fsdp"),
        P("section", None, "fsdp"),
        P("section", None, "fsdp"),
        P(None, "fsdp"),
        P(None, "fsdp"),
        P(None, "fsdp"),
    )
    out_specs = (
        P(),
        P(),
        P("fsdp", None),
        P("fsdp", None),
        P("fsdp", None),
        P("fsdp", None),
        P(None, "fsdp"),
        P(None, "fsdp"),
        P(None, "fsdp"),
        P("section", None, "fsdp"),
        P("section", None, "fsdp"),
        P("section", None, "fsdp"),
        P("section", None, "fsdp"),
        P("section", None, "fsdp"),
        P("section", None, "fsdp"),
        P("section", None, "fsdp"),
        P("section", None, "fsdp"),
        P("section", None, "fsdp"),
        P("section", None, "fsdp"),
        P("section", None, "fsdp"),
        P("section", None, "fsdp"),
        P("section", None, "fsdp"),
        P("section", None, "fsdp"),
        P("section", None, "fsdp"),
        P(None, "fsdp"),
        P(None, "fsdp"),
        P(None, "fsdp"),
    )
    return jax.shard_map(shards, mesh=mesh, in_specs=in_specs, out_specs=out_specs, check_vma=False)
```

profile of v0, /device:TPU:0, one launch (start us, length us, event | category | flops | bytes accessed | tf_op | source)
XLA Modules:
  0.0 2874.4 jit_solution(12900640312838739202)
XLA Ops:
  19.0 42.2 %all-gather = s32[16,1,128]{2,1,0:T(1,128)S(1)} all-gather(s32[1,1,128]{2,1,0:T(1,128)S(1)} %copy-done.286), channel_id=2, replica_groups=mesh['section'=2,'fsdp'=16] {'fsdp'}, dimensions={0}, use_global_device_ids=true | all-gather | bytes 8704 | tf_op jit(solution)/shard_map/all_gather | solution.py:302
  61.8 11.4 gather_fusion
  81.3 88.4 %all_gather.30 = bf16[1,12,768]{1,0,2:T(2,128)(2,1)S(1)} all-gather(bf16[1,12,48]{1,0,2:T(2,128)(2,1)S(1)} %copy.248), channel_id=1, replica_groups=mesh['section'=2,'fsdp'=16] {'fsdp'}, dimensions={2}, use_global_device_ids=true | all-gather | bytes 19584 | tf_op jit(solution)/shard_map/all_gather | solution.py:283
  172.4 52.1 %all_gather.29 = bf16[128,768]{0,1:T(8,128)(2,1)} all-gather(bf16[128,48]{0,1:T(8,128)(2,1)S(1)} %convert_element_type.300), channel_id=1, replica_groups=mesh['section'=2,'fsdp'=16] {'fsdp'}, dimensions={1}, use_global_device_ids=true | all-gather | bytes 208896 | tf_op jit(solution)/shard_map/all_gather | solution.py:284
  228.0 20.4 slice_reduce_fusion.2
  265.3 76.8 %all-gather.19.cloned.1.call-done = bf16[1,768,3072]{1,2,0:T(8,128)(2,1)} async-done(((bf16[1,768,192]{1,2,0:T(8,128)(2,1)}), bf16[1,768,3072]{1,2,0:T(8,128)(2,1)}) %all-gather.19.cloned.1.call-update) | async-done | bytes 4718608 | tf_op jit(solution)/shard_map/all_gather | solution.py:282
  377.5 38.2 %all-gather.2 = bf16[16,48,2]{1,2,0:T(2,128)(2,1)S(1)} all-gather(bf16[1,48,2]{1,2,0:T(2,128)(2,1)S(1)} %convert_bitcast_fusion.4), channel_id=1, replica_groups=mesh['section'=2,'fsdp'=16] {'fsdp'}, dimensions={0}, use_global_device_ids=true | all-gather | bytes 3264 | tf_op jit(solution)/shard_map/all_gather | solution.py:285
  443.2 35.3 %all-gather.1 = s32[16,1,128]{2,1,0:T(1,128)S(1)} all-gather(s32[1,1,128]{2,1,0:T(1,128)S(1)} %copy-done.287), channel_id=3, replica_groups=mesh['section'=2,'fsdp'=16] {'fsdp'}, dimensions={0}, use_global_device_ids=true | all-gather | bytes 8704 | tf_op jit(solution)/shard_map/all_gather | solution.py:303
  478.5 27.4 all-gather.21.cloned.1.call-done
  505.9 25.3 while.49
  507.2 7.8 fusion.911
  519.8 7.8 fusion.911
  531.3 38.9 %all-gather.4 = f32[16,1,2048]{2,1,0:T(1,128)S(1)} all-gather(f32[1,1,2048]{2,1,0:T(1,128)S(1)} %reshape.612), channel_id=1, replica_groups=mesh['section'=2,'fsdp'=16] {'fsdp'}, dimensions={0}, use_global_device_ids=true | all-gather | bytes 139264 | tf_op jit(solution)/shard_map/all_gather | solution.py:37
  570.2 36.2 %all-gather.3 = f32[16,1,2048]{2,1,0:T(1,128)S(1)} all-gather(f32[1,1,2048]{2,1,0:T(1,128)S(1)} %reshape.610), channel_id=1, replica_groups=mesh['section'=2,'fsdp'=16] {'fsdp'}, dimensions={0}, use_global_device_ids=true | all-gather | bytes 139264 | tf_op jit(solution)/shard_map/all_gather | solution.py:37
  606.4 38.4 %all-gather.5 = f32[16,1,2048]{2,1,0:T(1,128)S(1)} all-gather(f32[1,1,2048]{2,1,0:T(1,128)S(1)} %reshape.614), channel_id=1, replica_groups=mesh['section'=2,'fsdp'=16] {'fsdp'}, dimensions={0}, use_global_device_ids=true | all-gather | bytes 139264 | tf_op jit(solution)/shard_map/all_gather | solution.py:37
  647.1 72.0 %while.50 = (s32[]{:T(128)}, f32[3144,768]{1,0:T(8,128)}, f32[2,1024,768]{2,1,0:T(8,128)}, s32[2]{0:T(128)S(1)}, f32[2048]{0:T(1024)S(1)}, /*index=5*/bf16[2048,...) while((s32[]{:T(128)}, f32[3144,768]{1,0:T(8,128)}, ...), condition=%wide.region_32.33_spmd.clone, body=%wide.region_31.32_spmd.clone.sunk | while | flops 14862620672 | bytes 204468656 | solution.py:372
  648.4 12.4 multiply_convert_fusion.14
  660.8 7.9 bitcast_dynamic-update-slice_fusion.2
  668.7 10.5 select_add_fusion.22
  684.4 12.4 multiply_convert_fusion.14
  696.8 7.9 bitcast_dynamic-update-slice_fusion.2
  704.8 10.5 select_add_fusion.22
  721.4 139.1 %reduce-scatter.15.cloned.1.call-done = f32[128,768]{1,0:T(8,128)} async-done(((f32[2048,768]{1,0:T(8,128)}), f32[128,768]{1,0:T(8,128)}) %reduce-scatter.15.cloned.1.call-update) | async-done | bytes 393232 | tf_op jit(solution)/shard_map/reduce_scatter | solution.py:377
  959.0 54.8 %all-gather.23.cloned.1.call-done = f32[2048,768]{1,0:T(8,128)} async-done(((f32[128,768]{1,0:T(8,128)}), f32[2048,768]{1,0:T(8,128)}) %all-gather.23.cloned.1.call-update) | async-done | bytes 6291472 | tf_op jit(solution)/shard_map/all_gather | solution.py:402
  1013.8 23.4 scatter_custom_fusion
  1037.2 101.1 %reduce-scatter.29.cloned.1.call-done = f32[48,2]{1,0:T(8,128)} async-done(((f32[768,2]{1,0:T(8,128)}), f32[48,2]{1,0:T(8,128)}) %reduce-scatter.29.cloned.1.call-update) | async-done | bytes 400
  1139.2 125.2 %reduce-scatter.25.cloned.1.call-done = f32[48,12]{1,0:T(8,128)} async-done(((f32[768,12]{1,0:T(8,128)}), f32[48,12]{1,0:T(8,128)}) %reduce-scatter.25.cloned.1.call-update) | async-done | bytes 2320
  1265.8 123.8 %reduce-scatter.27.cloned.1.call-done = f32[48,128]{1,0:T(8,128)} async-done(((f32[768,128]{1,0:T(8,128)}), f32[48,128]{1,0:T(8,128)}) %reduce-scatter.27.cloned.1.call-update) | async-done | bytes 24592
  1395.4 127.2 %reduce-scatter.19.cloned.1.call-done = f32[768,48]{0,1:T(8,128)} async-done(((f32[768,768]{0,1:T(8,128)}), f32[768,48]{0,1:T(8,128)}) %reduce-scatter.19.cloned.1.call-update) | async-done | bytes 147472 | tf_op jit(solution)/shard_map/reduce_scatter | solution.py:410
  1524.2 154.0 %reduce-scatter.17.cloned.1.call-done = f32[768,144]{0,1:T(8,128)} async-done(((f32[768,2304]{0,1:T(8,128)}), f32[768,144]{0,1:T(8,128)}) %reduce-scatter.17.cloned.1.call-update) | async-done | bytes 442384 | tf_op jit(solution)/shard_map/reduce_scatter | solution.py:409
  1681.2 172.9 %reduce-scatter.21.cloned.1.call-done = f32[768,192]{0,1:T(8,128)} async-done(((f32[768,3072]{0,1:T(8,128)}), f32[768,192]{0,1:T(8,128)}) %reduce-scatter.21.cloned.1.call-update) | async-done | bytes 589840 | tf_op jit(solution)/shard_map/reduce_scatter | solution.py:411
  1856.5 174.5 %reduce-scatter.23.cloned.1.call-done = f32[768,192]{0,1:T(8,128)} async-done(((f32[768,3072]{0,1:T(8,128)}), f32[768,192]{0,1:T(8,128)}) %reduce-scatter.23.cloned.1.call-update) | async-done | bytes 589840 | tf_op jit(solution)/shard_map/reduce_scatter | solution.py:412
  2034.2 39.9 %all-reduce.5.cloned.1.call-done = f32[3144,768]{1,0:T(8,128)} async-done(((f32[3144,768]{1,0:T(8,128)}), f32[3144,768]{1,0:T(8,128)}) %all-reduce.5.cloned.1.call-update) | async-done | bytes 9658384 | tf_op jit(solution)/shard_map/psum | solution.py:417
  2074.0 6.8 multiply_reduce_fusion
  2082.8 40.6 %psum.53 = f32[]{:T(128)} all-reduce(f32[]{:T(128)S(6)} %add.850), channel_id=1, replica_groups=mesh['section'=2,'fsdp'=16] {'section','fsdp'}, use_global_device_ids=true, to_apply=%region_96.97 | all-reduce | flops 1 | bytes 8 | tf_op jit(solution)/shard_map/psum | solution.py:420
  2153.9 27.5 fusion.680
  2181.4 196.4 %all-reduce.7.cloned.1.call-done = (f32[4,384,384]{2,1,0:T(8,128)}, f32[4,768,384]{1,2,0:T(8,128)}) async-done(((f32[4,384,384]{2,1,0:T(8,128)}, f32[4,768,384]{1,2,0:T(8,128)}), (f32[4,384,384]{2,1,0:T(8,128)}, f32[4,768,384]{1,2,0:T(8,128)})) %all-reduce.7.cloned.1.call-update) | async-done | bytes 7077904 | tf_op jit(solution)/shard_map/psum | solution.py:440
  2387.7 8.2 fusion.64
  2396.0 7.3 fusion.122
  2412.1 8.6 fusion.71
  2420.7 7.6 fusion.116
  2437.1 8.4 fusion.78
  2445.6 7.7 fusion.110
  2462.0 8.5 fusion.85
  2579.8 6.5 fusion.142
  2623.2 6.5 fusion.128
  2713.5 6.5 fusion.83
  2838.1 6.5 fusion.182
  (1079 shorter events, 670.5 us)
Async XLA Ops:
  7.2 244.2 %all-gather.13.cloned.1.call-start = ((), (), s32[]{:S(2)}) async-start(), calls=%async_computation.9 | async-start | bytes 3760128 | tf_op jit(solution)/shard_map/all_gather | solution.py:279
  9.0 248.8 %all-gather.15.cloned.1.call-start = ((), (), s32[]{:S(2)}) async-start(), calls=%async_computation.10 | async-start | bytes 1253376 | tf_op jit(solution)/shard_map/all_gather | solution.py:280
  10.6 249.4 %all-gather.17.cloned.1.call-start = ((), (), s32[]{:S(2)}) async-start(), calls=%async_computation.11 | async-start | bytes 5013504 | tf_op jit(solution)/shard_map/all_gather | solution.py:281
  61.2 12.1 copy-start.171
  75.3 174.3 %all-to-all-start = ((bf16[16,128,768]{2,1,0:T(8,128)(2,1)}), bf16[16,128,768]{2,1,0:T(8,128)(2,1)S(1)}, u32[]{:S(2)}, u32[]{:S(2)}) async-start(bf16[16,128,768]{2,1,0:T(8,128)(2,1)} %select_select_fusion), calls=%async_computation | async-start | bytes 6291456 | tf_op jit(solution)/shard_map/all_to_all | solution.py:312
  79.2 262.8 %all-gather.19.cloned.1.call-start = ((), (), s32[]{:S(2)}) async-start(), calls=%async_computation.12 | async-start | bytes 5013504 | tf_op jit(solution)/shard_map/all_gather | solution.py:282
  81.1 424.8 %all-gather.21.cloned.1.call-start = ((), (), s32[]{:S(2)}) async-start(), calls=%async_computation.13 | async-start | bytes 3342336 | tf_op jit(solution)/shard_map/all_gather | solution.py:328
  248.4 174.9 %copy-start.154 = (f32[768]{0:T(1024)}, f32[768]{0:T(1024)S(1)}, u32[]{:S(2)}) copy-start(f32[768]{0:T(1024)S(1)} %get-tuple-element.541) | copy-start | bytes 9220
  248.4 174.9 %copy-start.162 = (f32[768]{0:T(1024)}, f32[768]{0:T(1024)S(1)}, u32[]{:S(2)}) copy-start(f32[768]{0:T(1024)S(1)} %get-tuple-element.540) | copy-start | bytes 9220
  248.4 182.9 %copy-start.96 = (f32[768]{0:T(1024)}, f32[768]{0:T(1024)S(1)}, u32[]{:S(2)}) copy-start(f32[768]{0:T(1024)S(1)} %get-tuple-element.534) | copy-start | bytes 9220
  248.4 182.9 %copy-start.130 = (f32[768]{0:T(1024)}, f32[768]{0:T(1024)S(1)}, u32[]{:S(2)}) copy-start(f32[768]{0:T(1024)S(1)} %get-tuple-element.536) | copy-start | bytes 9220
  342.0 9.9 copy-start.1
  346.1 1.9 collective-permute-start
  377.4 41.8 %collective-permute-start.1 = (f32[128,768]{1,0:T(8,128)}, f32[128,768]{1,0:T(8,128)}, u32[]{:S(2)}, u32[]{:S(2)}) collective-permute-start(f32[128,768]{1,0:T(8,128)} %fusion.260), channel_id=1, source_target_pairs={{16,0},{0,16},{17,1},{1,17},{18,2},{2,18},{19,3},{3,19},{20,4},{4,... | collective-permute-start | bytes 1179656 | tf_op jit(solution)/shard_map/ppermute | solution.py:33
  441.7 418.8 %reduce-scatter.15.cloned.1.call-start = ((), (), s32[]{:S(2)}) async-start(), calls=%async_computation.14 | async-start | bytes 6684672 | tf_op jit(solution)/shard_map/reduce_scatter | solution.py:377
  648.4 12.4 copy-start
  648.4 12.4 copy-start.41
  648.4 20.3 slice-start.6
  648.4 20.3 slice-start.7
  668.7 10.5 copy-start.42
  684.4 12.4 copy-start
  684.4 12.4 copy-start.41
  684.4 20.3 slice-start.6
  684.4 20.3 slice-start.7
  704.7 10.5 copy-start.42
  719.1 141.4 %copy-start.44 = (f32[128,768]{1,0:T(8,128)S(1)}, f32[128,768]{1,0:T(8,128)}, u32[]{:S(2)}) copy-start(f32[128,768]{1,0:T(8,128)} %copy-done.43) | copy-start | bytes 1179652
  719.1 141.4 %copy-start.181 = (f32[768]{0:T(1024)S(1)}, f32[768]{0:T(1024)}, u32[]{:S(2)}) copy-start(f32[768]{0:T(1024)} %get-tuple-element.542) | copy-start | bytes 9220
  719.1 141.4 %copy-start.252 = (f32[128]{0:T(128)S(1)}, f32[128]{0:T(128)}, u32[]{:S(2)}) copy-start(f32[128]{0:T(128)} %copy-done.251) | copy-start | bytes 1540
  719.1 141.4 %copy-start.256 = (f32[128]{0:T(128)S(1)}, f32[128]{0:T(128)}, u32[]{:S(2)}) copy-start(f32[128]{0:T(128)} %copy-done.255) | copy-start | bytes 1540
  719.1 143.4 %copy-start.285 = (f32[128]{0:T(128)S(1)}, f32[128]{0:T(128)}, u32[]{:S(2)}) copy-start(f32[128]{0:T(128)} %copy-done.284) | copy-start | bytes 1540
  719.2 294.6 %all-gather.23.cloned.1.call-start = ((), (), s32[]{:S(2)}) async-start(), calls=%async_computation.19 | async-start | bytes 6684672 | tf_op jit(solution)/shard_map/all_gather | solution.py:402
  721.4 151.2 %copy-start.8 = (bf16[1,768,768]{2,1,0:T(8,128)(2,1)}, bf16[1,768,768]{2,1,0:T(8,128)(2,1)S(1)}, u32[]{:S(2)}) copy-start(bf16[1,768,768]{2,1,0:T(8,128)(2,1)S(1)} %copy.264) | copy-start | bytes 3538948
  882.0 1.8 collective-permute-start.2
  900.7 1.8 collective-permute-start.3
  920.3 218.1 %reduce-scatter.29.cloned.1.call-start = ((), (), s32[]{:S(2)}) async-start(), calls=%async_computation.23 | async-start | bytes 417792
  921.8 342.6 %reduce-scatter.25.cloned.1.call-start = ((), (), s32[]{:S(2)}) async-start(), calls=%async_computation.21 | async-start | bytes 417792
  924.4 465.3 %reduce-scatter.27.cloned.1.call-start = ((), (), s32[]{:S(2)}) async-start(), calls=%async_computation.22 | async-start | bytes 417792
  925.4 597.2 %reduce-scatter.19.cloned.1.call-start = ((), (), s32[]{:S(2)}) async-start(), calls=%async_computation.16 | async-start | bytes 2506752 | tf_op jit(solution)/shard_map/reduce_scatter | solution.py:410
  928.6 749.5 %reduce-scatter.17.cloned.1.call-start = ((), (), s32[]{:S(2)}) async-start(), calls=%async_computation.15 | async-start | bytes 7520256 | tf_op jit(solution)/shard_map/reduce_scatter | solution.py:409
  938.4 915.6 %reduce-scatter.21.cloned.1.call-start = ((), (), s32[]{:S(2)}) async-start(), calls=%async_computation.17 | async-start | bytes 10027008 | tf_op jit(solution)/shard_map/reduce_scatter | solution.py:411
  947.6 1083.4 %reduce-scatter.23.cloned.1.call-start = ((), (), s32[]{:S(2)}) async-start(), calls=%async_computation.18 | async-start | bytes 10027008 | tf_op jit(solution)/shard_map/reduce_scatter | solution.py:412
  958.3 1115.7 %all-reduce.5.cloned.1.call-start = ((), (), s32[]{:S(2)}) async-start(), calls=%async_computation.20 | async-start | bytes 19316736 | tf_op jit(solution)/shard_map/psum | solution.py:417
  1037.2 1340.6 %all-reduce.7.cloned.1.call-start = ((), (), s32[]{:S(2)}) async-start(), calls=%async_computation.24 | async-start | bytes 14155776 | tf_op jit(solution)/shard_map/psum | solution.py:440
  1394.2 639.3 %copy-start.174 = (f32[128,48]{0,1:T(8,128)}, f32[128,48]{0,1:T(8,128)S(1)}, u32[]{:S(2)}) copy-start(f32[128,48]{0,1:T(8,128)S(1)} %get-tuple-element.595) | copy-start | bytes 73732
  2034.1 90.0 %copy-start.113 = (f32[768,192]{0,1:T(8,128)S(1)}, f32[768,192]{0,1:T(8,128)}, u32[]{:S(2)}) copy-start(f32[768,192]{0,1:T(8,128)} %reduce-scatter.21.cloned.1.call-done) | copy-start | bytes 1769476
  2034.1 90.0 %copy-start.114 = (f32[768,192]{0,1:T(8,128)S(1)}, f32[768,192]{0,1:T(8,128)}, u32[]{:S(2)}) copy-start(f32[768,192]{0,1:T(8,128)} %reduce-scatter.23.cloned.1.call-done) | copy-start | bytes 1769476
  2034.1 90.0 %copy-start.159 = (f32[1,768,192]{1,2,0:T(8,128)S(1)}, f32[1,768,192]{1,2,0:T(8,128)}, u32[]{:S(2)}) copy-start(f32[1,768,192]{1,2,0:T(8,128)} %param.45) | copy-start | bytes 1769476
  2034.1 90.0 %copy-start.160 = (f32[1,768,192]{1,2,0:T(8,128)S(1)}, f32[1,768,192]{1,2,0:T(8,128)}, u32[]{:S(2)}) copy-start(f32[1,768,192]{1,2,0:T(8,128)} %param.44) | copy-start | bytes 1769476
  (284 other events, 960.4 us)
Sparse Core Ops, SparseCore 0:
  11.4 92.2 all-gather.12
  107.0 69.4 all-gather.14
  179.9 79.7 all-gather.16
  262.9 79.0 all-gather.18
  441.8 64.0 all-gather.20
  719.2 141.2 reduce-scatter.14
  920.4 93.3 all-gather.22
  1018.4 119.8 reduce-scatter.28
  1143.7 120.6 reduce-scatter.24
  1268.9 120.6 reduce-scatter.26
  1395.9 126.6 reduce-scatter.18
  1527.8 150.2 reduce-scatter.16
  1684.4 169.6 reduce-scatter.20
  1861.1 169.8 reduce-scatter.22
  2033.9 40.1 all-reduce.4
  2150.4 227.3 all-reduce.6
where the time goes:
time: 2880 us; the launch traced here: 2870 us
  waiting for transfers between devices  1520 us (53%)
  matrix products  664 us (23%)
  blocking collectives  415 us (14%)
  other arithmetic  133 us (5%)
  local copies, waits for them, and re-layouts  105 us (4%)
  between operations  29.5 us (1%)
    dot_general x80, matrix products, precise_mul(): return jnp.matmul(left_mat, right_mat, precision=PRECISE)  470 us
    unnamed x19, waiting for transfers between devices  350 us
    psum x1, waiting for transfers between devices, shards(): summed = lax.psum(gram_halves(new_moms, half_width), 'fsdp')  196 us
    reduce_scatter x1, waiting for transfers between devices, shards(): lax.psum_scatter(totals[3], 'fsdp', scatter_dimension=1, tiled=True)  174 us
    reduce_scatter x1, waiting for transfers between devices, shards(): lax.psum_scatter(totals[2], 'fsdp', scatter_dimension=1, tiled=True)  173 us
    reduce_scatter x1, waiting for transfers between devices, shards(): lax.psum_scatter(totals[0], 'fsdp', scatter_dimension=1, tiled=True)  154 us
    reduce_scatter x1, waiting for transfers between devices, shards(): lax.psum_scatter(grad_blocks.reshape(token_rows, -1), 'fsdp', scatter_dim...  139 us
    reduce_scatter x1, waiting for transfers between devices, shards(): lax.psum_scatter(totals[1], 'fsdp', scatter_dimension=1, tiled=True)  127 us
  transfers between devices with their start and end apart: 21, of which 16 were waited for; matrix products, arithmetic and copies ran while one was open for 6% of the time, Pallas kernels for 0%

commit v1 on v0

v1 whole, which is shorter than its diff:
```python
import functools
import math

import jax
import jax.numpy as jnp
from jax import lax
from jax.experimental import pallas as pl
from jax.experimental.pallas import tpu as pltpu
from jax.sharding import Mesh
from jax.sharding import PartitionSpec as P

HD = 64
STEP = 10


LN_EPS = 1e-05
NEG_FILL = -1e30
Z_WEIGHT = 0.01
CLIP_NORM = 0.02
MOMENTUM = 0.5
MUON_RATE = 0.7
MUON_DECAY = 0.01
ADAM_ONE = 0.9
ADAM_TWO = 0.95
ADAM_EPS = 1e-08
ADAM_DECAY = 0.1
RATE_EMBED = 0.12
RATE_POS = 0.1
RATE_VEC = 0.2
NEWTON_COEFS = (3.4445, -4.775, 2.0315)
FSDP = ("za", "yb", "yc", "xd")
SPOTS = ("za", "yb")
GROUP = ("section", "yc", "xd")
NOTE = 8
UPPER = ((0, 0), (0, 1), (0, 2), (1, 1), (1, 2), (2, 2))
MOMENT_SCALE = 2.0**21
VMEM_BYTES = 56 * 1024 * 1024


def swapped(block, axis):
    size = lax.axis_size(axis)
    return lax.ppermute(block, axis, [(i, size - 1 - i) for i in range(size)])


def spread_small(block):
    count = lax.axis_size(FSDP)
    copies = jnp.broadcast_to(block[None], (count,) + block.shape)
    return lax.all_to_all(copies, FSDP, 0, 0, tiled=True)


def span():
    return (lax.axis_size("za"), lax.axis_size(("yb", "yc")), lax.axis_size("xd"))


def route(level, distance):
    za, yb, xd = span()
    pairs = []
    for section in range(2):
        for place in range(za * yb * xd):
            a, b, c = place // (yb * xd), place // xd % yb, place % xd
            if level == 2:
                a = (a + distance) % za
            elif section == level:
                b = (b + distance) % yb
            else:
                c = (c + distance) % xd
            start = section * za * yb * xd
            pairs.append((start + place, start + (a * yb + b) * xd + c))
    return pairs


def moved(block, level, distance=1):
    return lax.ppermute(block, ("section",) + FSDP, route(level, distance))


def pick(block, axis, index):
    return lax.dynamic_index_in_dim(block, index, axis, keepdims=False)


def after(value, *others):
    return lax.optimization_barrier((value,) + others)[0]


def column_near(block):
    return jnp.stack([block] + [moved(block, 2, -k) for k in range(1, span()[0])])


def plane_near(column):
    return jnp.stack([column] + [moved(column, 1, -k) for k in range(1, span()[2])])


def planes_near(plane):
    return [plane] + [moved(plane, 0, -k) for k in range(1, span()[1])]


def gathered_near(block):
    return planes_near(plane_near(column_near(block)))


def owners_near(section):
    za, yb, xd = span()
    a, b, c = lax.axis_index("za"), lax.axis_index(("yb", "yc")), lax.axis_index("xd")
    places = jnp.arange(za * yb * xd, dtype=jnp.int32)
    far, near, high = places // (xd * za), places // za % xd, places % za
    high = (a + high) % za
    row = jnp.where(section == 0, (b + far) % yb, (b + near) % yb)
    col = jnp.where(section == 0, (c + near) % xd, (c + far) % xd)
    return (high * yb + row) * xd + col


def places_near(section):
    za, yb, xd = span()
    a, b, c = lax.axis_index("za"), lax.axis_index(("yb", "yc")), lax.axis_index("xd")
    owners = jnp.arange(za * yb * xd, dtype=jnp.int32)
    high = (owners // (yb * xd) - a) % za
    row, col = (owners // xd % yb - b) % yb, (owners % xd - c) % xd
    far, near = jnp.where(section == 0, row, col), jnp.where(section == 0, col, row)
    return (far * xd + near) * za + high


def assemble_kernel(widths, each, spot_ref, *refs):
    sources, outs = refs[: -len(widths)], refs[-len(widths) :]
    for number, source in enumerate(sources):

        @pl.when(pl.program_id(0) // each == number)
        def _(source=source):
            start = 0
            for out, width in zip(outs, widths):
                out[...] = source[0, start : start + width, :]
                start += width


def assembled(own, other, widths):
    section = lax.axis_index("section")
    count = lax.axis_size(FSDP)
    rows, half = own[0].shape[-2:]
    pieces = [piece.reshape(-1, rows, half) for piece in own + other]
    if any(width % 16 for width in widths):
        sides = []
        for side, parts in ((section, pieces[: len(own)]), (1 - section, pieces[len(own) :])):
            sides.append(jnp.take(jnp.concatenate(parts), places_near(side), axis=0))
        first_side = section == 0
        left = jnp.where(first_side, sides[0], sides[1])
        right = jnp.where(first_side, sides[1], sides[0])
        whole = jnp.concatenate([left, right], -1)
        starts = [sum(widths[:n]) for n in range(5)]
        return [whole[:, starts[n] : starts[n + 1]].reshape(-1, 2 * half) for n in range(4)]
    sides = jnp.stack([section, 1 - section]).astype(jnp.int32)
    spots = jnp.concatenate(
        [owners_near(section), owners_near(1 - section), jnp.repeat(sides, count)]
    ).astype(jnp.int32)
    each = pieces[0].shape[0]

    def source_at(number):
        return lambda step, spot: (jnp.clip(step - number * each, 0, each - 1), 0, 0)

    return pl.pallas_call(
        functools.partial(assemble_kernel, tuple(widths), each),
        grid_spec=pltpu.PrefetchScalarGridSpec(
            num_scalar_prefetch=1,
            grid=(2 * count,),
            in_specs=[
                pl.BlockSpec((1, rows, half), source_at(number)) for number in range(len(pieces))
            ],
            out_specs=[
                pl.BlockSpec((width, half), lambda step, spot: (spot[step], spot[2 * count + step]))
                for width in widths
            ],
        ),
        out_shape=[
            jax.ShapeDtypeStruct((count * width, 2 * half), jnp.bfloat16) for width in widths
        ],
        compiler_params=pltpu.CompilerParams(vmem_limit_bytes=VMEM_BYTES),
        cost_estimate=pl.CostEstimate(
            flops=0, bytes_accessed=8 * count * rows * half, transcendentals=0
        ),
    )(spots, *pieces)


def exponent_for(bound):
    return jnp.floor(14.5 - jnp.log2(jnp.maximum(bound, 1e-30)))


def coded(values, exponent):
    rows = lax.broadcasted_iota(jnp.int32, values.shape, values.ndim - 2)
    noted = rows >= values.shape[-2] - NOTE
    return jnp.where(noted, exponent, values * jnp.exp2(exponent)).astype(jnp.float16)


def exponent_in(block):
    return block[(0,) * (block.ndim - 2) + (block.shape[-2] - 1, 0)].astype(jnp.float32)


def added(kept, came):
    first, second = exponent_in(kept), exponent_in(came)
    total = kept.astype(jnp.float32) * jnp.exp2(-first) + came.astype(jnp.float32) * jnp.exp2(
        -second
    )
    return coded(total, jnp.minimum(first, second) - 1.0)


def planes_cut(block):
    first_side = lax.axis_index("section") == 0
    sizes = span()
    block = block.reshape(sizes + block.shape[1:])
    b, c = lax.axis_index(("yb", "yc")), lax.axis_index("xd")
    parts = []
    for distance in range(sizes[1]):
        row, col = (b + distance) % sizes[1], (c + distance) % sizes[2]
        parts.append(jnp.where(first_side, pick(block, 1, row), pick(block, 2, col)))
    return parts


def planes_reduced(parts, add):
    total = parts[0]
    for distance in range(1, len(parts)):
        total = add(total, moved(parts[distance], 0, distance))
    return total


def plane_reduced(plane, add):
    first_side = lax.axis_index("section") == 0
    inner = jnp.where(first_side, lax.axis_index("xd"), lax.axis_index(("yb", "yc")))
    total = pick(plane, 1, inner)
    for distance in range(1, span()[2]):
        sent = pick(plane, 1, (inner + distance) % span()[2])
        total = add(total, moved(sent, 1, distance))
    return total


def column_parts(column):
    a = lax.axis_index("za")
    parts = [pick(column, 0, a)]
    for distance in range(1, span()[0]):
        parts.append(moved(pick(column, 0, (a + distance) % span()[0]), 2, distance))
    return parts


def decoded(block):
    return block[..., :-NOTE, :].astype(jnp.float32) * jnp.exp2(-exponent_in(block))


def row_sums(block):
    plane = planes_reduced(planes_cut(block), lax.add)
    return sum(part.astype(jnp.float32) for part in column_parts(plane_reduced(plane, lax.add)))


def parted_weights(grads, exponent):
    own = [grad.reshape(lax.axis_size(FSDP), -1, grad.shape[-1]) for grad in grads]
    note = jnp.broadcast_to(exponent.astype(jnp.float16), (own[0].shape[0], NOTE, own[0].shape[2]))
    return planes_cut(jnp.concatenate(own + [note], 1))


def summed_weights(layer_parts, *before):
    first_side = lax.axis_index("section") == 0
    plane_late = planes_reduced(layer_parts[1], added)
    column_late = plane_reduced(plane_late, added)
    parts_early = [after(part, column_late) for part in layer_parts[0]]
    plane_early = planes_reduced(parts_early, added)
    parts_late = column_parts(column_late)
    column_early = plane_reduced(plane_early, added)
    parts_early = column_parts(column_early)
    parts_early[0] = after(parts_early[0], *before)
    halves = [sum(decoded(part) for part in parts) for parts in (parts_early, parts_late)]
    kept = jnp.where(first_side, halves[0], halves[1])
    came = swapped(jnp.where(first_side, halves[1], halves[0]), "section")
    return jnp.where(
        first_side, jnp.concatenate([kept, came], 1), jnp.concatenate([came, kept], 1)
    )


def gram_summed(gram):
    tile = gram.shape[0] // 3
    blocks = [gram[i * tile : (i + 1) * tile, j * tile : (j + 1) * tile] for i, j in UPPER]
    near, far = jnp.stack(blocks[:3]), jnp.stack(blocks[3:])
    if lax.axis_size(GROUP) != 4:
        return lax.psum(jnp.concatenate([near, far]), GROUP)
    first_side = lax.axis_index("section") == 0
    kept, gone = jnp.where(first_side, near, far), jnp.where(first_side, far, near)
    kept = kept + swapped(gone, "section")
    kept = kept + swapped(kept, "xd")
    came = swapped(kept, "section")
    return jnp.where(first_side, jnp.concatenate([kept, came]), jnp.concatenate([came, kept]))


def layer_norm(values, gain_row, bias_row):
    average = jnp.mean(values, -1, keepdims=True)
    centered = values - average
    variance = jnp.mean(centered * centered, -1, keepdims=True)
    return centered * lax.rsqrt(variance + LN_EPS) * gain_row + bias_row


def split_vectors(vectors):
    rows = [vectors[number : number + 1] for number in range(12)]
    return (*rows[:7], jnp.concatenate(rows[7:11], 1), rows[11])


def contract_rows(left_mat, right_mat):
    return lax.dot_general(
        left_mat, right_mat, (((0,), (0,)), ((), ())), preferred_element_type=jnp.float32
    )


def contract_cols(left_mat, right_mat):
    return lax.dot_general(
        left_mat, right_mat, (((1,), (1,)), ((), ())), preferred_element_type=jnp.float32
    )


def plain_dot(left_mat, right_mat):
    return jnp.dot(left_mat, right_mat, preferred_element_type=jnp.float32)


def with_other(*values):
    joined = jnp.concatenate(values, 1)
    return jnp.concatenate([joined, swapped(joined, "section")], 0)


def own_half(values):
    half = values.shape[1] // 2
    return lax.dynamic_slice_in_dim(values, lax.axis_index("section") * half, half, 1)


def other_half(values):
    half = values.shape[1] // 2
    return lax.dynamic_slice_in_dim(values, (1 - lax.axis_index("section")) * half, half, 1)


def widest_column(values):
    return jnp.max(jnp.sum(jnp.square(values.astype(jnp.float32)), 0))


def gelu_tanh(values):
    return jax.nn.gelu(values, approximate=True)


def layer_forward(inputs, weights):
    qkv_t, proj_t, fc_t, down_t, vectors = weights
    g_one, b_one, q_bias, v_bias, p_bias, g_two, b_two, f_bias, d_bias = split_vectors(vectors)
    seq_len, model_width = inputs.shape
    head_count = model_width // HD
    factor = HD ** (-0.5)
    normed_a = layer_norm(inputs, g_one, b_one).astype(jnp.bfloat16)
    bias_qkv = jnp.concatenate([q_bias, jnp.zeros_like(q_bias), v_bias], 1)
    qkv_rows = (contract_cols(normed_a, qkv_t) + bias_qkv).astype(jnp.bfloat16)
    queries = qkv_rows[:, :model_width].reshape(seq_len, head_count, HD)
    keys_all = qkv_rows[:, model_width : 2 * model_width].reshape(seq_len, head_count, HD)
    values_all = qkv_rows[:, 2 * model_width :].reshape(seq_len, head_count, HD)
    scores = (
        jnp.einsum("qhd,khd->hqk", queries, keys_all, preferred_element_type=jnp.float32) * factor
    )
    causal = lax.broadcasted_iota(jnp.int32, (seq_len, seq_len), 0) >= lax.broadcasted_iota(
        jnp.int32, (seq_len, seq_len), 1
    )
    attn_probs = jax.nn.softmax(jnp.where(causal, scores, NEG_FILL), axis=-1)
    probs_low = attn_probs.astype(jnp.bfloat16)
    attended = jnp.einsum("hqk,khd->qhd", probs_low, values_all, preferred_element_type=jnp.float32)
    attended = attended.reshape(seq_len, model_width).astype(jnp.bfloat16)
    after_attn = inputs + contract_cols(attended, proj_t) + p_bias
    normed_b = layer_norm(after_attn, g_two, b_two).astype(jnp.bfloat16)
    hidden_pre = contract_cols(normed_b, fc_t) + f_bias
    hidden_low = gelu_tanh(hidden_pre).astype(jnp.bfloat16)
    outputs = after_attn + plain_dot(hidden_low, down_t) + d_bias
    saved = (
        inputs,
        normed_a,
        queries,
        keys_all,
        values_all,
        attn_probs,
        probs_low,
        attended,
        after_attn,
        normed_b,
        hidden_pre,
        with_other(hidden_low, normed_a, attended, normed_b),
    )
    return (outputs, saved)


def layer_backward(saved, grad_out, weights):
    qkv_t, proj_t, fc_t, down_t, vectors = weights
    g_one, b_one, q_bias, v_bias, p_bias, g_two, b_two, f_bias, d_bias = split_vectors(vectors)
    (
        inputs,
        normed_a,
        queries,
        keys_all,
        values_all,
        attn_probs,
        probs_low,
        attended,
        after_attn,
        normed_b,
        hidden_pre,
        early,
    ) = saved
    seq_len, model_width = inputs.shape
    factor = HD ** (-0.5)
    grad_mlp = grad_out.astype(jnp.bfloat16)
    d_dbias = jnp.sum(grad_mlp, 0, keepdims=True, dtype=jnp.float32)
    grad_hidden = contract_cols(grad_mlp, down_t)
    grad_pre = jax.vjp(gelu_tanh, hidden_pre)[1](grad_hidden)[0].astype(jnp.bfloat16)
    d_fbias = jnp.sum(grad_pre, 0, keepdims=True, dtype=jnp.float32)
    grad_nb = plain_dot(grad_pre, fc_t)
    ln_two = jax.vjp(layer_norm, after_attn, g_two, b_two)[1](grad_nb)
    grad_mid = grad_out + ln_two[0]
    grad_attn = grad_mid.astype(jnp.bfloat16)
    d_pbias = jnp.sum(grad_attn, 0, keepdims=True, dtype=jnp.float32)
    grad_att = plain_dot(grad_attn, proj_t).reshape(queries.shape).astype(jnp.bfloat16)
    grad_probs = jnp.einsum(
        "qhd,khd->hqk", grad_att, values_all, preferred_element_type=jnp.float32
    )
    grad_vals = jnp.einsum("hqk,qhd->khd", probs_low, grad_att, preferred_element_type=jnp.float32)
    grad_scores = attn_probs * (grad_probs - jnp.sum(grad_probs * attn_probs, -1, keepdims=True))
    grad_scores = grad_scores.astype(jnp.bfloat16)
    grad_q = (
        jnp.einsum("hqk,khd->qhd", grad_scores, keys_all, preferred_element_type=jnp.float32)
        * factor
    )
    grad_k = (
        jnp.einsum("hqk,qhd->khd", grad_scores, queries, preferred_element_type=jnp.float32)
        * factor
    )
    grad_qkv = jnp.concatenate(
        [
            grad_q.reshape(seq_len, model_width),
            grad_k.reshape(seq_len, model_width),
            grad_vals.reshape(seq_len, model_width),
        ],
        -1,
    ).astype(jnp.bfloat16)
    qkv_sums = jnp.sum(grad_qkv, 0, keepdims=True, dtype=jnp.float32)
    late = with_other(grad_qkv, grad_attn, grad_pre, grad_mlp)
    wide = hidden_pre.shape[1]

    def taken(block, start, width):
        return block[:, start : start + width]

    products = (
        (taken(late, 0, 3 * model_width), taken(early, wide, model_width)),
        (taken(late, 3 * model_width, model_width), taken(early, wide + model_width, model_width)),
        (taken(late, 4 * model_width, wide), taken(early, wide + 2 * model_width, model_width)),
        (taken(early, 0, wide), taken(late, 4 * model_width + wide, model_width)),
    )
    bounds = [widest_column(block) for block in (early, late)]
    exponent = exponent_for(jnp.sqrt(bounds[0]) * jnp.sqrt(bounds[1]))
    scale = jnp.exp2(exponent)
    d_qkv, d_proj, d_fc, d_down = (
        (contract_rows(left, own_half(right)) * scale).astype(jnp.float16)
        for left, right in products
    )
    grad_na = plain_dot(grad_qkv, qkv_t)
    ln_one = jax.vjp(layer_norm, inputs, g_one, b_one)[1](grad_na)
    grad_in = grad_mid + ln_one[0]
    d_vectors = [
        ln_one[1],
        ln_one[2],
        qkv_sums[:, :model_width],
        qkv_sums[:, 2 * model_width :],
        d_pbias,
        ln_two[1],
        ln_two[2],
        *(d_fbias[:, n * model_width : (n + 1) * model_width] for n in range(4)),
        d_dbias,
    ]
    return (grad_in, (d_qkv, d_proj, d_fc, d_down), d_vectors, exponent)


def adam_step(weights_in, gradient, first_mom, second_mom, step_rate):
    first_new = ADAM_ONE * first_mom + (1.0 - ADAM_ONE) * gradient
    second_new = ADAM_TWO * second_mom + (1.0 - ADAM_TWO) * gradient * gradient
    first_hat = first_new / (1.0 - ADAM_ONE**STEP)
    second_hat = second_new / (1.0 - ADAM_TWO**STEP)
    weights_new = weights_in - step_rate * (
        first_hat / (jnp.sqrt(second_hat) + ADAM_EPS) + ADAM_DECAY * weights_in
    )
    return (weights_new, first_new, second_new)


def halves_of(values):
    high = values.astype(jnp.bfloat16)
    return (high, (values - high.astype(jnp.float32)).astype(jnp.bfloat16))


def newton_kernel(gram_ref, out_ref, pair_a, pair_b, gram_now, poly, product):
    tile = gram_ref.shape[1]
    count = 3
    width = count * tile
    a, b, c = NEWTON_COEFS
    rows = lax.broadcasted_iota(jnp.int32, (width, width), 0)
    cols = lax.broadcasted_iota(jnp.int32, (width, width), 1)
    diagonal = rows == cols

    def store_pair(pair, values):
        for part in range(3):
            pair[part] = values.astype(jnp.bfloat16)
            values = values - pair[part].astype(jnp.float32)

    def multiply(left, right, write, terms=2):
        for i in range(count):
            row_at = slice(i * tile, (i + 1) * tile)
            for j in range(i, count):
                col_at = slice(j * tile, (j + 1) * tile)
                block = jnp.zeros((tile, tile), jnp.float32)
                for part in reversed(range(terms)):
                    for other in reversed(range(terms - part)):
                        block += plain_dot(left[part, row_at, :], right[other, :, col_at])
                write(row_at, col_at, block)
                if i != j:
                    write(col_at, row_at, block.T)

    def into(ref):
        def write(row_at, col_at, block):
            ref[row_at, col_at] = block

        return write

    for number, (i, j) in enumerate(UPPER):
        row_at, col_at = slice(i * tile, (i + 1) * tile), slice(j * tile, (j + 1) * tile)
        gram_now[row_at, col_at] = gram_ref[number]
        if i != j:
            gram_now[col_at, row_at] = gram_ref[number].T
    full = gram_now[...]
    trace = jnp.sum(jnp.where(diagonal, full, 0.0))
    inverse = 1.0 / (jnp.sqrt(jnp.full((1, 1), trace, jnp.float32)) + 1e-07)
    gram_now[...] = full * (inverse * inverse)
    for iteration in range(5):
        store_pair(pair_a, gram_now[...])
        multiply(pair_a, pair_a, into(poly))
        poly[...] = jnp.where(diagonal, a, 0.0) + b * gram_now[...] + c * poly[...]
        store_pair(pair_b, poly[...])
        if iteration < 4:
            terms = 3 if iteration < 2 else 2
            multiply(pair_a, pair_b, into(gram_now), terms)
            store_pair(pair_a, gram_now[...])
            multiply(pair_a, pair_b, into(gram_now), terms)
        if iteration == 0:
            product[...] = poly[...]
        else:
            store_pair(pair_a, product[...])
            multiply(pair_a, pair_b, into(product))
    out_ref[...] = product[...] * inverse


def newton_product(gram_blocks):
    width = 3 * gram_blocks.shape[1]
    square = (width, width)
    return pl.pallas_call(
        newton_kernel,
        out_shape=jax.ShapeDtypeStruct(square, jnp.float32),
        in_specs=[pl.BlockSpec(memory_space=pltpu.VMEM)],
        out_specs=pl.BlockSpec(memory_space=pltpu.VMEM),
        scratch_shapes=[
            pltpu.VMEM((3,) + square, jnp.bfloat16),
            pltpu.VMEM((3,) + square, jnp.bfloat16),
            pltpu.VMEM(square, jnp.float32),
            pltpu.VMEM(square, jnp.float32),
            pltpu.VMEM(square, jnp.float32),
        ],
        compiler_params=pltpu.CompilerParams(vmem_limit_bytes=48 * 1024 * 1024),
        cost_estimate=pl.CostEstimate(
            flops=17 * 4 * width**3, bytes_accessed=8 * width * width, transcendentals=0
        ),
    )(gram_blocks)


def head_forward_kernel(
    shard_rows, spot_ref, one_ref, two_ref, table_ref, target_ref, exp_ref, stat_ref, row_ref
):
    rows = jnp.concatenate([one_ref[0], two_ref[0]], 0)
    row_ref[...] = rows
    logits = contract_cols(rows, table_ref[...])
    cols = lax.broadcasted_iota(jnp.int32, logits.shape, 1)
    logits = jnp.where(cols < shard_rows, logits, NEG_FILL)
    highest = jnp.max(logits, -1, keepdims=True)
    exps = jnp.exp(logits - highest)
    total = jnp.sum(exps, -1, keepdims=True)
    target = jnp.sum(jnp.where(cols == target_ref[...], logits, 0.0), -1, keepdims=True)
    exp_ref[...] = exps.astype(jnp.bfloat16)
    lanes = lax.broadcasted_iota(jnp.int32, stat_ref.shape, 1)
    stat_ref[...] = jnp.where(lanes == 0, highest, jnp.where(lanes == 1, total, target))


def head_forward(blocks, places, table, targets, shard_rows):
    number, tokens, width = blocks.shape
    count = number * tokens
    vocab = table.shape[0]
    step = 2 * tokens
    return pl.pallas_call(
        functools.partial(head_forward_kernel, shard_rows),
        grid_spec=pltpu.PrefetchScalarGridSpec(
            num_scalar_prefetch=1,
            grid=(number // 2,),
            in_specs=[
                pl.BlockSpec((1, tokens, width), lambda i, spot: (spot[2 * i], 0, 0)),
                pl.BlockSpec((1, tokens, width), lambda i, spot: (spot[2 * i + 1], 0, 0)),
                pl.BlockSpec((vocab, width), lambda i, spot: (0, 0)),
                pl.BlockSpec((step, 1), lambda i, spot: (i, 0)),
            ],
            out_specs=[
                pl.BlockSpec((step, vocab), lambda i, spot: (i, 0)),
                pl.BlockSpec((step, 128), lambda i, spot: (i, 0)),
                pl.BlockSpec((step, width), lambda i, spot: (i, 0)),
            ],
        ),
        out_shape=[
            jax.ShapeDtypeStruct((count, vocab), jnp.bfloat16),
            jax.ShapeDtypeStruct((count, 128), jnp.float32),
            jax.ShapeDtypeStruct((count, width), jnp.bfloat16),
        ],
        compiler_params=pltpu.CompilerParams(vmem_limit_bytes=VMEM_BYTES),
        cost_estimate=pl.CostEstimate(
            flops=2 * count * vocab * width,
            bytes_accessed=2 * (vocab * width + count * (width + vocab)),
            transcendentals=count * vocab,
        ),
    )(places, blocks, blocks, table, targets)


def head_pull_kernel(exp_ref, target_ref, table_ref, soft_ref, hard_ref):
    exps = exp_ref[...]
    cols = lax.broadcasted_iota(jnp.int32, exps.shape, 1)
    chosen = jnp.where(cols == target_ref[...], 1.0, 0.0).astype(jnp.bfloat16)
    soft_ref[...] = plain_dot(exps, table_ref[...])
    hard_ref[...] = plain_dot(chosen, table_ref[...]).astype(jnp.bfloat16)


def head_pull(exps, targets, table):
    count, vocab = exps.shape
    width = table.shape[1]
    step = min(256, count)
    return pl.pallas_call(
        head_pull_kernel,
        grid=(count // step,),
        out_shape=[
            jax.ShapeDtypeStruct((count, width), jnp.float32),
            jax.ShapeDtypeStruct((count, width), jnp.bfloat16),
        ],
        in_specs=[
            pl.BlockSpec((step, vocab), lambda i: (i, 0)),
            pl.BlockSpec((step, 1), lambda i: (i, 0)),
            pl.BlockSpec((vocab, width), lambda i: (0, 0)),
        ],
        out_specs=[
            pl.BlockSpec((step, width), lambda i: (i, 0)),
            pl.BlockSpec((step, width), lambda i: (i, 0)),
        ],
        compiler_params=pltpu.CompilerParams(vmem_limit_bytes=VMEM_BYTES),
        cost_estimate=pl.CostEstimate(
            flops=4 * count * vocab * width,
            bytes_accessed=2 * (vocab * width + count * (3 * width + vocab)),
            transcendentals=0,
        ),
    )(exps, targets, table)


def head_table_kernel(exp_ref, token_ref, target_ref, row_ref, grad_ref):
    exps = exp_ref[...].astype(jnp.float32)
    cols = lax.broadcasted_iota(jnp.int32, exps.shape, 1)
    at_target = jnp.where(cols == target_ref[...], token_ref[:, 1:2], 0.0)
    grad_logit = (exps * token_ref[:, 0:1] - at_target).astype(jnp.bfloat16)

    @pl.when(pl.program_id(0) == 0)
    def _():
        grad_ref[...] = jnp.zeros_like(grad_ref)

    grad_ref[...] += contract_rows(grad_logit, row_ref[...])


def head_table(exps, token_scales, targets, rows):
    count, vocab = exps.shape
    width = rows.shape[1]
    step = min(256, count)
    return pl.pallas_call(
        head_table_kernel,
        grid=(count // step,),
        out_shape=jax.ShapeDtypeStruct((vocab, width), jnp.float32),
        in_specs=[
            pl.BlockSpec((step, vocab), lambda i: (i, 0)),
            pl.BlockSpec((step, 2), lambda i: (i, 0)),
            pl.BlockSpec((step, 1), lambda i: (i, 0)),
            pl.BlockSpec((step, width), lambda i: (i, 0)),
        ],
        out_specs=pl.BlockSpec((vocab, width), lambda i: (0, 0)),
        compiler_params=pltpu.CompilerParams(vmem_limit_bytes=VMEM_BYTES),
        cost_estimate=pl.CostEstimate(
            flops=2 * count * vocab * width,
            bytes_accessed=2 * (2 * vocab * width + count * (width + vocab)),
            transcendentals=0,
        ),
    )(exps, token_scales, targets, rows)


def row_scatter_kernel(id_ref, part_ref, total_ref, out_ref):
    @pl.when(pl.program_id(0) == 0)
    def _():
        out_ref[...] = total_ref[...]

    spots = lax.broadcasted_iota(jnp.int32, (out_ref.shape[0], id_ref.shape[1]), 0)
    chosen = jnp.where(spots == id_ref[...], 1.0, 0.0).astype(jnp.bfloat16)
    out_ref[...] += plain_dot(chosen, part_ref[...])


def rows_scattered(total, ids, parts):
    vocab, width = total.shape
    count = parts.shape[0]
    step = min(256, count)
    return pl.pallas_call(
        row_scatter_kernel,
        grid=(count // step,),
        out_shape=jax.ShapeDtypeStruct(total.shape, total.dtype),
        in_specs=[
            pl.BlockSpec((1, step), lambda i: (0, i)),
            pl.BlockSpec((step, width), lambda i: (i, 0)),
            pl.BlockSpec((vocab, width), lambda i: (0, 0)),
        ],
        out_specs=pl.BlockSpec((vocab, width), lambda i: (0, 0)),
        compiler_params=pltpu.CompilerParams(vmem_limit_bytes=VMEM_BYTES),
        cost_estimate=pl.CostEstimate(
            flops=2 * count * vocab * width,
            bytes_accessed=8 * vocab * width + 2 * count * width,
            transcendentals=0,
        ),
    )(ids.reshape(1, count), parts, total)


def shards(
    token_ids,
    target_ids,
    true_counts,
    embed_table,
    embed_m,
    embed_v,
    pos_table,
    pos_m,
    pos_v,
    w_qkv,
    w_proj,
    w_fc,
    w_down,
    mom_qkv,
    mom_proj,
    mom_fc,
    mom_down,
    layer_vecs,
    vecs_m,
    vecs_v,
    final_norm,
    norm_m,
    norm_v,
):
    section_index = lax.axis_index("section")
    section_count = lax.axis_size("section")
    fsdp_count = lax.axis_size(FSDP)
    shard_rows, model_width = embed_table.shape
    vocab_start = lax.axis_index(FSDP) * shard_rows
    vocab_rows = -(-shard_rows // 128) * 128
    table_rows = jnp.pad(embed_table.astype(jnp.bfloat16), ((0, vocab_rows - shard_rows), (0, 0)))
    masters_t = [w[0].T for w in (w_qkv, w_proj, w_fc, w_down)]
    moments_t = [m[0].T for m in (mom_qkv, mom_proj, mom_fc, mom_down)]
    widths = [w.shape[0] for w in masters_t]
    starts = [sum(widths[:number]) for number in range(5)]
    layer_rows, place_rows = layer_vecs.shape[1], pos_table.shape[0]
    norm_at = section_count * layer_rows
    places_at = norm_at + final_norm.shape[0]
    small_rows = -(-(places_at + place_rows) // 16) * 16

    def padded_rows(parts):
        missing = small_rows - sum(part.shape[0] for part in parts)
        return jnp.concatenate(parts + [jnp.zeros((missing, parts[0].shape[1]), parts[0].dtype)], 0)

    vecs_both = lax.all_gather(layer_vecs[0].astype(jnp.bfloat16), "section", axis=0, tiled=True)
    token_row = jnp.concatenate([token_ids[0], target_ids[0]], 1)
    token_row = jnp.concatenate([token_row // 256, token_row % 256], 1)
    lanes = layer_vecs.shape[2]
    token_rows = -(-token_row.shape[1] // lanes)
    token_row = jnp.pad(token_row, ((0, 0), (0, token_rows * lanes - token_row.shape[1])))
    token_row = token_row.reshape(token_rows, lanes).astype(jnp.bfloat16)
    small = padded_rows([vecs_both, final_norm.astype(jnp.bfloat16), pos_table.astype(jnp.bfloat16)])
    small = spread_small(jnp.concatenate([small, token_row], 0))
    ids_parts = small[:, small_rows:].astype(jnp.int32).reshape(fsdp_count, -1)
    seq_len = token_ids.shape[2]
    ids_targets = 256 * ids_parts[:, : 2 * seq_len] + ids_parts[:, 2 * seq_len : 4 * seq_len]
    ids_all, targets_all = ids_targets[:, :seq_len], ids_targets[:, seq_len:]
    seq_count = ids_all.shape[0]
    small = jnp.moveaxis(small[:, :small_rows], 0, 1).reshape(small_rows, model_width)
    small = small.astype(jnp.float32)
    head_norm = small[norm_at:places_at]
    positions = small[places_at : places_at + place_rows]
    pack = jnp.concatenate(masters_t, 0).astype(jnp.bfloat16)
    first_side = section_index == 0
    kept_half = own_half(pack)
    came_half = swapped(other_half(pack), "section")
    blocks = [jnp.where(section_index == layer, kept_half, came_half) for layer in range(2)]
    column_early = column_near(blocks[0])
    column_late = column_near(after(blocks[1], column_early))
    planes = [planes_near(plane_near(column_early))]
    planes.append(planes_near(plane_near(after(column_late, planes[0][-1]))))
    layer_sets = []
    for layer, own in enumerate(planes):
        other = [swapped(piece, "section") for piece in own]
        layer_sets.append(
            list(assembled(own, other, widths))
            + [small[layer * layer_rows : (layer + 1) * layer_rows]]
        )

    local_ids = ids_all - vocab_start
    inside = (local_ids >= 0) & (local_ids < shard_rows)
    safe_ids = jnp.clip(local_ids, 0, shard_rows - 1)
    contrib = jnp.where(
        inside[..., None], jnp.take(table_rows, safe_ids, axis=0), jnp.zeros((), jnp.bfloat16)
    )
    rows_in = row_sums(contrib)

    current = rows_in + positions
    kept = []
    for weights in layer_sets:
        current, saved = layer_forward(current, weights)
        kept.append(saved)
    final_rows = current
    normed_low = layer_norm(final_rows, head_norm[0:1], head_norm[1:2]).astype(jnp.bfloat16)
    blocks = jnp.concatenate(gathered_near(normed_low), 0).reshape((fsdp_count,) + normed_low.shape)
    counts_row = jnp.take(true_counts, section_index, axis=0)
    counted = lax.broadcasted_iota(jnp.int32, (seq_count, seq_len), 1) < counts_row[:, None]
    counted = counted.astype(jnp.float32).reshape(-1)
    token_total = jnp.sum(true_counts).astype(jnp.float32)
    local_targets = targets_all.reshape(-1) - vocab_start
    targets_col = jnp.where(local_targets < shard_rows, local_targets, -1)[:, None]
    exps, stats, rows_all = head_forward(
        blocks, places_near(section_index), table_rows, targets_col, shard_rows
    )
    stats = stats[:, :3].T
    block_max = stats[0]
    stats = spread_small(stats)
    soft_pull, hard_pull = head_pull(exps, targets_col, table_rows)
    highest = jnp.max(stats[:, 0], 0)
    merged_sum = jnp.sum(stats[:, 1] * jnp.exp(stats[:, 0] - highest), 0)
    partition = highest + jnp.log(merged_sum)
    target_all = jnp.sum(stats[:, 2], 0)
    loss_part = jnp.sum(counted * (partition - target_all + Z_WEIGHT * partition * partition))
    token_weight = counted / token_total
    pull = token_weight * (1.0 + 2.0 * Z_WEIGHT * partition) * jnp.exp(block_max - partition)
    token_scales = jnp.stack([pull, token_weight], 1)
    grad_rows = pull[:, None] * soft_pull - token_weight[:, None] * hard_pull.astype(jnp.float32)
    grad_parts = lax.all_to_all(
        grad_rows.astype(jnp.bfloat16).reshape(fsdp_count, -1, model_width), FSDP, 0, 0, tiled=True
    )
    table_grad = head_table(exps, token_scales, targets_col, rows_all)
    grad_normed = jnp.sum(grad_parts, 0, dtype=jnp.float32)
    grad_now, d_fgain, d_fbias = jax.vjp(layer_norm, final_rows, head_norm[0:1], head_norm[1:2])[1](
        grad_normed
    )
    layer_parts, vecs_parts = [], []
    for layer in reversed(range(section_count)):
        grad_now, grads, d_vectors, exponent = layer_backward(
            kept[layer], grad_now, layer_sets[layer]
        )
        layer_parts.insert(0, parted_weights(grads, exponent))
        if layer:
            grad_now = after(grad_now, layer_parts[0][-1])
        vecs_parts = d_vectors + vecs_parts
    emb_all = lax.all_gather(grad_now.astype(jnp.bfloat16), FSDP, axis=0, tiled=True)
    table_grad = rows_scattered(table_grad, local_ids.reshape(-1), emb_all)
    small_grad = lax.optimization_barrier(padded_rows(vecs_parts + [d_fgain, d_fbias, grad_now]))
    small_grad = jnp.moveaxis(small_grad.reshape(small_rows, fsdp_count, -1), 1, 0)
    small_grad = jnp.sum(lax.all_to_all(small_grad, FSDP, 0, 0, tiled=True), 0)
    table_grad = (table_grad + swapped(table_grad, "section"))[:shard_rows]
    table_squares = jnp.sum(table_grad * table_grad)
    flushed = summed_weights(layer_parts, table_squares)
    loss_row = jnp.broadcast_to(loss_part, (1, small_grad.shape[1]))
    small_grad = jnp.concatenate([small_grad, loss_row], 0)
    small_grad = small_grad + swapped(small_grad, "section")
    loss_sum = small_grad[-1, 0]
    vecs_grad = lax.dynamic_slice_in_dim(small_grad, section_index * layer_rows, layer_rows, 0)
    norm_grad = small_grad[norm_at:places_at]
    pos_grad = small_grad[places_at : places_at + place_rows]
    weight_grad = flushed
    own_squares = jnp.sum(weight_grad * weight_grad) + jnp.sum(vecs_grad * vecs_grad)
    shared_squares = table_squares + jnp.sum(pos_grad * pos_grad) + jnp.sum(norm_grad * norm_grad)
    device_squares = own_squares + jnp.where(section_index == 0, shared_squares, 0.0)
    square_sum = lax.psum(
        jnp.sum(spread_small(jnp.full((8, 128), device_squares)), 0)[0, 0], "section"
    )
    clip_norm = jnp.sqrt(square_sum)
    factor = jnp.minimum(1.0, CLIP_NORM / (clip_norm + 1e-06))

    new_moms = [
        MOMENTUM * moments_t[n] + factor * weight_grad[starts[n] : starts[n + 1]] for n in range(4)
    ]
    widest = max(widths)
    padded = jnp.stack([jnp.pad(mom, ((0, widest - mom.shape[0]), (0, 0))) for mom in new_moms])
    padded = (padded * MOMENT_SCALE).astype(jnp.float16)
    padded = padded.reshape(4, 2, widest // 2, model_width)
    sent = lax.all_to_all(padded, "section", 1, 1, tiled=True)
    sent = sent.reshape(4 * section_count, widest // 2, model_width)
    held = lax.all_to_all(sent, SPOTS, 0, 0, tiled=True).reshape(-1, model_width)
    held = held.astype(jnp.float32) * (1.0 / MOMENT_SCALE)
    high, lower = halves_of(held)
    crossed = contract_rows(high, lower)
    gram = contract_rows(high, high) + (crossed + crossed.T) + contract_rows(lower, lower)
    product = newton_product(gram_summed(gram))
    turned = jnp.matmul(held, product, precision=lax.Precision.HIGH).astype(jnp.float16)
    turned = turned.reshape(4 * section_count, widest // 2, model_width)
    back = lax.all_to_all(turned, SPOTS, 0, 0, tiled=True)
    back = back.reshape(4, section_count, widest // 2, model_width)
    back = lax.all_to_all(back, "section", 1, 1, tiled=True).reshape(4, widest, model_width)
    back = back.astype(jnp.float32)

    embed_new, embed_m_new, embed_v_new = adam_step(
        embed_table, factor * table_grad, embed_m, embed_v, RATE_EMBED
    )
    pos_new, pos_m_new, pos_v_new = adam_step(pos_table, factor * pos_grad, pos_m, pos_v, RATE_POS)
    norm_new, norm_m_new, norm_v_new = adam_step(
        final_norm, factor * norm_grad, norm_m, norm_v, RATE_VEC
    )
    vecs_new, vecs_m_new, vecs_v_new = adam_step(
        layer_vecs, factor * vecs_grad[None], vecs_m, vecs_v, RATE_VEC
    )
    results = []
    for number in range(4):
        column_factor = math.sqrt(widths[number] * fsdp_count / model_width)
        new_master = masters_t[number] - MUON_RATE * (
            column_factor * back[number, : widths[number]] + MUON_DECAY * masters_t[number]
        )
        new_master = new_master.T[None]
        results.append((new_master, new_master.astype(jnp.bfloat16), new_moms[number].T[None]))
    return (
        loss_sum,
        clip_norm,
        embed_new,
        embed_new.astype(jnp.bfloat16),
        embed_m_new,
        embed_v_new,
        pos_new,
        pos_m_new,
        pos_v_new,
        *results[0],
        *results[1],
        *results[2],
        *results[3],
        vecs_new,
        vecs_m_new,
        vecs_v_new,
        norm_new,
        norm_m_new,
        norm_v_new,
    )


def inner_mesh(mesh):
    section_count, fsdp_count = mesh.devices.shape
    parts = {16: (4, 2, 1, 2), 64: (4, 2, 2, 4)}.get(fsdp_count, (4, 2, fsdp_count // 8, 1))
    return Mesh(mesh.devices.reshape((section_count,) + parts), ("section",) + FSDP)


def solution(mesh):
    ids = P("section", FSDP, None)
    rows = P(FSDP, None)
    cols = P(None, FSDP)
    layer = P("section", None, FSDP)
    in_specs = (ids, ids, P()) + (rows,) * 3 + (cols,) * 3 + (layer,) * 11 + (cols,) * 3
    out_specs = (P(), P()) + (rows,) * 4 + (cols,) * 3 + (layer,) * 15 + (cols,) * 3
    return jax.shard_map(
        shards, mesh=inner_mesh(mesh), in_specs=in_specs, out_specs=out_specs, check_vma=False
    )
```

time: 2880 us -> 1110 us (0.39)
  waiting for transfers between devices: 1520 us -> 368 us
  matrix products: 664 us -> 66.2 us
  blocking collectives: 415 us -> 56.6 us
  Pallas kernels: 0 us -> 182 us
  starting transfers between devices: 5.61 us -> 113 us
  other arithmetic: 133 us -> 163 us
    reduce_scatter x5 -> x0, waiting for transfers between devices: 768 us -> none  [the longest x1 174 us: shards(): lax.psum_scatter(totals[3], 'fsdp', scatter_dimension=1, tiled=True)]
    dot_general x94 -> x9, matrix products: 526 us -> 13 us  [the longest x8 8.89 us: plain_dot(): return jnp.dot(left_mat, right_mat, preferred_element_type=jnp.float32)]
    all_gather x8 -> x1, blocking collectives: 370 us -> 1.81 us  [shards(): lax.all_gather(layer_vecs[0].astype(jnp.bfloat16), 'section', axis=0, til...]
    unnamed x19 -> x1, waiting for transfers between devices: 350 us -> 0.02 us
    ppermute x4 -> x45, waiting for transfers between devices: 5.14 us -> 278 us  [the longest x30 260 us: moved(): return lax.ppermute(block, ('section',) + FSDP, route(level, distance))]
    psum x2 -> x0, waiting for transfers between devices: 236 us -> none  [the longest x1 196 us: shards(): summed = lax.psum(gram_halves(new_moms, half_width), 'fsdp')]
    pallas_call x0 -> x7, Pallas kernels: none -> 182 us  [the longest x2 46.4 us: assembled(): pl.pallas_call(functools.partial(assemble_kernel, tuple(widths), each), g...]
    all_gather x6 -> x1, waiting for transfers between devices: 159 us -> 14.2 us  [shards(): lax.all_gather(grad_now.astype(jnp.bfloat16), FSDP, axis=0, tiled=True)]
  transfers between devices with their start and end apart: 21 -> 51, of which waited for: 16 -> 28; matrix products, arithmetic and copies ran while one was open for 6% -> 25% of each run, Pallas kernels for 0% -> 7%
where the time goes in v1:
time: 1110 us; the launch traced here: 1100 us
  waiting for transfers between devices  368 us (33%)
  Pallas kernels  182 us (16%)
  other arithmetic  163 us (15%)
  local copies, waits for them, and re-layouts  117 us (11%)
  starting transfers between devices  113 us (10%)
  matrix products  66.2 us (6%)
  blocking collectives  56.6 us (5%)
  between operations  37.7 us (3%)
    ppermute x30, waiting for transfers between devices, moved(): return lax.ppermute(block, ('section',) + FSDP, route(level, distance))  260 us
    ppermute x30, starting transfers between devices, moved(): return lax.ppermute(block, ('section',) + FSDP, route(level, distance))  72.2 us
    all_to_all x1, waiting for transfers between devices, shards(): lax.all_to_all(grad_rows.astype(jnp.bfloat16).reshape(fsdp_count, -1, mod...  54 us
    pallas_call x2, Pallas kernels, assembled(): pl.pallas_call(functools.partial(assemble_kernel, tuple(widths), each), g...  46.4 us
    pallas_call x1, Pallas kernels, newton_product(): pl.pallas_call(newton_kernel, out_shape=jax.ShapeDtypeStruct(square, jnp....  40.4 us
    unnamed x357, local copies, waits for them, and re-layouts  35.4 us
    all_to_all x1, blocking collectives, shards(): lax.all_to_all(sent, SPOTS, 0, 0, tiled=True).reshape(-1, model_width)  31.9 us
    dot_general x8, matrix products, contract_cols(): lax.dot_general(left_mat, right_mat, (((1,), (1,)), ((), ())), preferred_...  30.5 us
  transfers between devices with their start and end apart: 51, of which 28 were waited for; matrix products, arithmetic and copies ran while one was open for 25% of the time, Pallas kernels for 7%

profile of v1, /device:TPU:0, one launch (start us, length us, event | category | flops | bytes accessed | tf_op | source)
XLA Modules:
  0.0 1103.6 jit_solution(14052051082841491518)
XLA Ops:
  20.4 9.2 collective-permute-done.8
  29.5 18.5 %collective-permute-done.7 = bf16[576,384]{1,0:T(8,128)(2,1)S(1)} collective-permute-done((bf16[576,384]{1,0:T(8,128)(2,1)S(1)}, bf16[576,384]{1,0:T(8,128)(2,1)S(1)}, u32[]{:S(2)}, u32[]{:S(2)}) %collective-permute-start.7) | collective-permute-done | bytes 442400 | tf_op jit(solution)/shard_map/ppermute | solution.py:73
  50.0 21.0 %collective-permute-done.9 = bf16[4,576,384]{2,1,0:T(8,128)(2,1)S(1)} collective-permute-done((bf16[4,576,384]{2,1,0:T(8,128)(2,1)S(1)}, bf16[4,576,384]{2,1,0:T(8,128)(2,1)S(1)}, u32[]{:S(2)}, u32[]{:S(2)}) %collective-permute-start.9) | collective-permute-done | bytes 1769504 | tf_op jit(solution)/shard_map/ppermute | solution.py:73
  77.9 13.3 %all-to-all-start = ((bf16[16,171,48]{1,2,0:T(8,128)(2,1)}), bf16[16,171,48]{1,2,0:T(8,128)(2,1)S(1)}, u32[]{:S(2)}, u32[]{:S(2)}) async-start(bf16[16,171,48]{1,2,0:T(8,128)(2,1)} %broadcast_in_dim.207), calls=%async_computation | async-start | bytes 786432 | tf_op jit(solution)/shard_map/all_to_all | solution.py:48
  98.1 21.1 %all-to-all-done = bf16[16,171,48]{1,2,0:T(8,128)(2,1)S(1)} async-done(((bf16[16,171,48]{1,2,0:T(8,128)(2,1)}), bf16[16,171,48]{1,2,0:T(8,128)(2,1)S(1)}, u32[]{:S(2)}, u32[]{:S(2)}) %all-to-all-start) | async-done | bytes 262688 | tf_op jit(solution)/shard_map/all_to_all | solution.py:48
  120.2 11.5 %gather_fusion = bf16[2048,768]{1,0:T(8,128)(2,1)S(1)} fusion(bf16[3200,768]{1,0:T(8,128)(2,1)} %pad.19.table_ref, s32[2048]{0:T(1024)S(1)} %bitcast_clamp_fusion), kind=kCustom, calls=%fused_computation | custom fusion | bytes 6299648 | tf_op jit(solution)/shard_map/jit(_take)/gather | solution.py:812
  131.7 10.0 collective-permute-start.15
  146.5 7.7 collective-permute-done.15
  154.2 16.3 %collective-permute-done.14 = bf16[576,384]{1,0:T(8,128)(2,1)S(1)} collective-permute-done((bf16[576,384]{1,0:T(8,128)(2,1)}, bf16[576,384]{1,0:T(8,128)(2,1)S(1)}, u32[]{:S(2)}, u32[]{:S(2)}) %collective-permute-start.14) | collective-permute-done | bytes 442400 | tf_op jit(solution)/shard_map/ppermute | solution.py:73
  176.5 33.2 %collective-permute-done.16 = bf16[4,576,384]{2,1,0:T(8,128)(2,1)} collective-permute-done((bf16[4,576,384]{2,1,0:T(8,128)(2,1)S(1)}, bf16[4,576,384]{2,1,0:T(8,128)(2,1)}, u32[]{:S(2)}, u32[]{:S(2)}) %collective-permute-start.16) | collective-permute-done | bytes 1769504 | tf_op jit(solution)/shard_map/ppermute | solution.py:73
  229.1 10.1 collective-permute-done.1
  240.5 13.0 %collective-permute-start.4 = (bf16[128,768]{1,0:T(8,128)(2,1)S(1)}, bf16[128,768]{1,0:T(8,128)(2,1)S(1)}, u32[]{:S(2)}, u32[]{:S(2)}) collective-permute-start(bf16[128,768]{1,0:T(8,128)(2,1)S(1)} %get-tuple-element.467), channel_id=1, source_target_pairs={{0,12},{1,13},{2,14},{3,15},{4,0},{5,1},{6,2},{7,3},{8,4},{9,5},{1... | collective-permute-start | bytes 589832 | tf_op jit(solution)/shard_map/ppermute | solution.py:73
  257.9 5.0 collective-permute-start.2
  267.1 23.1 %shard_map.430 = (bf16[2304,768]{1,0:T(8,128)(2,1)}, bf16[768,768]{1,0:T(8,128)(2,1)}, bf16[3072,768]{1,0:T(8,128)(2,1)}, bf16[3072,768]{1,0:T(8,128)(2,1)}) custom-call(s32[64]{0:T(128)} %pad_add_fusion.2.spot_ref, bf16[8,576,384]{2,1,0:T(8,128)(2,1)} %bitcast.33.refs_0_, bf16[8,576,384]{2,1,0:T(8,128)(2,1)} %bitcast.34.refs_1_, ...), custom_call_target="tpu_custom_call" | custom-call | bytes 28311552 | tf_op jit(solution)/shard_map/pallas_call | solution.py:157
  298.4 5.4 multiply_convert_fusion.5
  305.2 23.3 %shard_map.431 = (bf16[2304,768]{1,0:T(8,128)(2,1)}, bf16[768,768]{1,0:T(8,128)(2,1)}, bf16[3072,768]{1,0:T(8,128)(2,1)}, bf16[3072,768]{1,0:T(8,128)(2,1)}) custom-call(s32[64]{0:T(128)} %pad_add_fusion.2.spot_ref, bf16[8,576,384]{2,1,0:T(8,128)(2,1)} %bitcast.51.refs_0_, bf16[8,576,384]{2,1,0:T(8,128)(2,1)} %bitcast.52.refs_1_, ...), custom_call_target="tpu_custom_call" | custom-call | bytes 28311552 | tf_op jit(solution)/shard_map/pallas_call | solution.py:157
  336.8 5.4 multiply_convert_fusion.4
  348.5 4.7 collective-permute-done.22
  353.2 7.3 collective-permute-done.21
  362.2 10.6 collective-permute-done.23
  381.0 14.7 %collective-permute-done.24 = bf16[2,4,128,768]{3,2,1,0:T(8,128)(2,1)} collective-permute-done((bf16[2,4,128,768]{3,2,1,0:T(8,128)(2,1)}, bf16[2,4,128,768]{3,2,1,0:T(8,128)(2,1)}, u32[]{:S(2)}, u32[]{:S(2)}) %collective-permute-start.24) | collective-permute-done | bytes 1572896 | tf_op jit(solution)/shard_map/ppermute | solution.py:73
  399.1 22.1 %shard_map.432 = (bf16[2048,3200]{1,0:T(8,128)(2,1)}, f32[2048,128]{1,0:T(8,128)}, bf16[2048,768]{1,0:T(8,128)(2,1)}) custom-call(s32[16]{0:T(128)} %fusion.129.spot_ref, bf16[16,128,768]{2,1,0:T(8,128)(2,1)} %bitcast.483, bf16[16,128,768]{2,1,0:T(8,128)(2,1)} %bitcast.484, bf16[3200,768]{1,0:T(8,128)(2,1)} %pad.19.table_ref, ...), custom_call_target="tpu_custom_call" | custom-call | flops 10066329600 | bytes 21168128 | tf_op jit(solution)/shard_map/pallas_call | solution.py:590
  423.6 6.9 all-to-all-start.1
  430.6 26.8 %shard_map.433 = (f32[2048,768]{1,0:T(8,128)}, bf16[2048,768]{1,0:T(8,128)(2,1)}) custom-call(bf16[2048,3200]{1,0:T(8,128)(2,1)} %get-tuple-element.57.exp_ref, s32[2048,1]{1,0:T(8,128)} %compare_select_fusion.target_ref, bf16[3200,768]{1,0:T(8,128)(2,1)} %pad.19.table_ref), custom_call_target="tpu_custom_call" | custom-call | flops 20132659200 | bytes 27459584 | tf_op jit(solution)/shard_map/pallas_call | solution.py:633
  460.5 5.5 subtract_convert_fusion
  465.9 7.0 all-to-all-start.2
  478.2 54.0 %all-to-all-done.2 = bf16[16,128,768]{2,1,0:T(8,128)(2,1)} async-done(((bf16[16,128,768]{2,1,0:T(8,128)(2,1)}), bf16[16,128,768]{2,1,0:T(8,128)(2,1)}, u32[]{:S(2)}, u32[]{:S(2)}) %all-to-all-start.2) | async-done | bytes 3145760 | tf_op jit(solution)/shard_map/all_to_all | solution.py:846
  537.9 5.5 convert_reduce_fusion.2
  552.7 5.1 multiply_reduce_fusion.4
  585.0 5.0 convert_reduce_fusion.3
  603.0 8.4 multiply_reduce_fusion.3
  613.2 4.8 collective-permute-start.30
  627.8 26.1 %shard_map.434.total_ref = f32[3200,768]{1,0:T(8,128)} custom-call(bf16[2048,3200]{1,0:T(8,128)(2,1)} %get-tuple-element.57.exp_ref, f32[2048,2]{1,0:T(8,128)} %copy.669.token_ref, s32[2048,1]{1,0:T(8,128)} %compare_select_fusion.target_ref, bf16[2048,768]{1,0:T(8,128)(2,1)} %get-tuple-element.63.row_ref), custom_call_target="tpu_custom_call" | custom-call | flops 10066329600 | bytes 26083328 | tf_op jit(solution)/shard_map/pallas_call | solution.py:675
  672.2 14.2 %all-gather.3.cloned.1.call-done.part_ref = bf16[2048,768]{1,0:T(8,128)(2,1)} async-done(((bf16[128,768]{1,0:T(8,128)(2,1)}), bf16[2048,768]{1,0:T(8,128)(2,1)}) %all-gather.3.cloned.1.call-update) | async-done | bytes 3145744 | tf_op jit(solution)/shard_map/all_gather | solution.py:863
  686.4 20.3 %shard_map.435 = f32[3200,768]{1,0:T(8,128)} custom-call(s32[1,2048]{1,0:T(1,128)} %bitcast.554, bf16[2048,768]{1,0:T(8,128)(2,1)} %all-gather.3.cloned.1.call-done.part_ref, f32[3200,768]{1,0:T(8,128)} %shard_map.434.total_ref), custom_call_target="tpu_custom_call" | custom-call | flops 10066329600 | bytes 22806528 | tf_op jit(solution)/shard_map/pallas_call | solution.py:709
  721.8 6.3 bitcast_select_fusion.2
  729.3 5.3 collective-permute-done.31
  743.8 38.7 %collective-permute-done.32 = f16[4,2,584,384]{3,2,1,0:T(8,128)(2,1)S(1)} collective-permute-done((f16[4,2,584,384]{3,2,1,0:T(8,128)(2,1)S(1)}, f16[4,2,584,384]{3,2,1,0:T(8,128)(2,1)S(1)}, u32[]{:S(2)}, u32[]{:S(2)}) %collective-permute-start.32) | collective-permute-done | bytes 3588128 | tf_op jit(solution)/shard_map/ppermute | solution.py:73
  800.3 13.6 %collective-permute-done.33 = f16[4,584,384]{2,1,0:T(8,128)(2,1)S(1)} collective-permute-done((f16[4,584,384]{2,1,0:T(8,128)(2,1)S(1)}, f16[4,584,384]{2,1,0:T(8,128)(2,1)S(1)}, u32[]{:S(2)}, u32[]{:S(2)}) %collective-permute-start.33) | collective-permute-done | bytes 1794080 | tf_op jit(solution)/shard_map/ppermute | solution.py:73
  827.2 29.5 %collective-permute-done.39 = f16[584,384]{1,0:T(8,128)(2,1)S(1)} collective-permute-done((f16[584,384]{1,0:T(8,128)(2,1)}, f16[584,384]{1,0:T(8,128)(2,1)S(1)}, u32[]{:S(2)}, u32[]{:S(2)}) %collective-permute-start.39) | collective-permute-done | bytes 448544 | tf_op jit(solution)/shard_map/ppermute | solution.py:73
  860.0 5.7 all-to-all-start.3
  874.5 10.7 collective-permute-done.36
  888.9 9.6 multiply_reduce_fusion
  916.0 10.5 all_to_all.45
  938.8 31.9 %all_to_all.47 = f16[8,96,768]{2,1,0:T(8,128)(2,1)S(1)} all-to-all(f16[8,96,768]{2,1,0:T(8,128)(2,1)S(1)} %bitcast.470), channel_id=1, replica_groups=mesh['section'=2,'za'=4,'yb'=2,'yc'=1,'xd'=2] {'za','yb'}, dimensions={0} | all-to-all | bytes 2359296 | tf_op jit(solution)/shard_map/all_to_all | solution.py:897
  987.1 13.2 %collective-permute-done.43 = f32[3,256,256]{2,1,0:T(8,128)} collective-permute-done((f32[3,256,256]{2,1,0:T(8,128)S(1)}, f32[3,256,256]{2,1,0:T(8,128)}, u32[]{:S(2)}, u32[]{:S(2)}) %collective-permute-start.43) | collective-permute-done | bytes 786464 | tf_op jit(solution)/shard_map/ppermute | solution.py:42
  1008.4 40.4 %shard_map.436 = f32[768,768]{1,0:T(8,128)S(1)} custom-call(f32[6,256,256]{2,1,0:T(8,128)S(1)} %maximum_select_fusion.1.gram_ref), custom_call_target="tpu_custom_call" | custom-call | flops 30802968576 | bytes 4718592 | tf_op jit(solution)/shard_map/pallas_call | solution.py:549
  1056.4 29.0 %fusion.187 = (bf16[3144,768]{1,0:T(8,128)(2,1)}, f32[3144,768]{1,0:T(8,128)}, f32[3144,768]{1,0:T(8,128)}, f32[3144,768]{1,0:T(8,128)}) fusion(f32[3144,768]{1,0:T(8,128)} %param.26, f32[3200,768]{1,0:T(8,128)} %collective-permute-done.34, f32[3200,768]{1,0:T(8,128)} %shard_map.435, f32[]{:T(128)S(6)} %min.33, f32[3144,768]{1,0:T(8,128)} %param.27, ...), kind=kLoop, calls=%fused_computation.556 | loop fusion | flops 43462656 | bytes 82096128 | tf_op jit(solution)/shard_map/convert_element_type | solution.py:932
  (757 shorter events, 325.7 us)
Async XLA Ops:
  13.5 16.1 %collective-permute-start.8 = (bf16[576,384]{1,0:T(8,128)(2,1)S(1)}, bf16[576,384]{1,0:T(8,128)(2,1)S(1)}, u32[]{:S(2)}, u32[]{:S(2)}) collective-permute-start(bf16[576,384]{1,0:T(8,128)(2,1)S(1)} %get-tuple-element.463), channel_id=1, source_target_pairs={{0,4},{1,5},{2,6},{3,7},{4,8},{5,9},{6,10},{7,11},{8,12},{9,13},{1... | collective-permute-start | bytes 1327112 | tf_op jit(solution)/shard_map/ppermute | solution.py:73
  16.4 31.6 %collective-permute-start.7 = (bf16[576,384]{1,0:T(8,128)(2,1)S(1)}, bf16[576,384]{1,0:T(8,128)(2,1)S(1)}, u32[]{:S(2)}, u32[]{:S(2)}) collective-permute-start(bf16[576,384]{1,0:T(8,128)(2,1)S(1)} %get-tuple-element.463), channel_id=1, source_target_pairs={{0,8},{1,9},{2,10},{3,11},{4,12},{5,13},{6,14},{7,15},{8,0},{9,1},... | collective-permute-start | bytes 1327112 | tf_op jit(solution)/shard_map/ppermute | solution.py:73
  19.0 29.0 %collective-permute-start.6 = (bf16[576,384]{1,0:T(8,128)(2,1)S(1)}, bf16[576,384]{1,0:T(8,128)(2,1)S(1)}, u32[]{:S(2)}, u32[]{:S(2)}) collective-permute-start(bf16[576,384]{1,0:T(8,128)(2,1)S(1)} %get-tuple-element.463), channel_id=1, source_target_pairs={{0,12},{1,13},{2,14},{3,15},{4,0},{5,1},{6,2},{7,3},{8,4},{9,5},{1... | collective-permute-start | bytes 1327112 | tf_op jit(solution)/shard_map/ppermute | solution.py:73
  48.4 22.6 %collective-permute-start.9 = (bf16[4,576,384]{2,1,0:T(8,128)(2,1)S(1)}, bf16[4,576,384]{2,1,0:T(8,128)(2,1)S(1)}, u32[]{:S(2)}, u32[]{:S(2)}) collective-permute-start(bf16[4,576,384]{2,1,0:T(8,128)(2,1)S(1)} %get-tuple-element.461), channel_id=1, source_target_pairs={{0,1},{1,0},{2,3},{3,2},{4,5},{5,4},{6,7},{7,6},{8,9},{9,8},{10,11... | collective-permute-start | bytes 5308424 | tf_op jit(solution)/shard_map/ppermute | solution.py:73
  73.2 97.6 %collective-permute-start.10 = (bf16[2,4,576,384]{3,2,1,0:T(8,128)(2,1)}, bf16[2,4,576,384]{3,2,1,0:T(8,128)(2,1)}, u32[]{:S(2)}, u32[]{:S(2)}) collective-permute-start(bf16[2,4,576,384]{3,2,1,0:T(8,128)(2,1)} %pad_maximum_fusion.2), channel_id=1, source_target_pairs={{0,2},{1,3},{2,0},{3,1},{4,6},{5,7},{6,4},{7,5},{8,10},{9,11},{10,... | collective-permute-start | bytes 10616840 | tf_op jit(solution)/shard_map/ppermute | solution.py:73
  77.9 41.2 %all-to-all-start = ((bf16[16,171,48]{1,2,0:T(8,128)(2,1)}), bf16[16,171,48]{1,2,0:T(8,128)(2,1)S(1)}, u32[]{:S(2)}, u32[]{:S(2)}) async-start(bf16[16,171,48]{1,2,0:T(8,128)(2,1)} %broadcast_in_dim.207), calls=%async_computation | async-start | bytes 786432 | tf_op jit(solution)/shard_map/all_to_all | solution.py:48
  131.7 22.5 %collective-permute-start.15 = (bf16[576,384]{1,0:T(8,128)(2,1)}, bf16[576,384]{1,0:T(8,128)(2,1)S(1)}, u32[]{:S(2)}, u32[]{:S(2)}) collective-permute-start(bf16[576,384]{1,0:T(8,128)(2,1)} %get-tuple-element.50), channel_id=1, source_target_pairs={{0,4},{1,5},{2,6},{3,7},{4,8},{5,9},{6,10},{7,11},{8,12},{9,13},{1... | collective-permute-start | bytes 1327112 | tf_op jit(solution)/shard_map/ppermute | solution.py:73
  141.7 28.8 %collective-permute-start.14 = (bf16[576,384]{1,0:T(8,128)(2,1)}, bf16[576,384]{1,0:T(8,128)(2,1)S(1)}, u32[]{:S(2)}, u32[]{:S(2)}) collective-permute-start(bf16[576,384]{1,0:T(8,128)(2,1)} %get-tuple-element.50), channel_id=1, source_target_pairs={{0,8},{1,9},{2,10},{3,11},{4,12},{5,13},{6,14},{7,15},{8,0},{9,1},... | collective-permute-start | bytes 1327112 | tf_op jit(solution)/shard_map/ppermute | solution.py:73
  143.3 27.2 %collective-permute-start.13 = (bf16[576,384]{1,0:T(8,128)(2,1)}, bf16[576,384]{1,0:T(8,128)(2,1)S(1)}, u32[]{:S(2)}, u32[]{:S(2)}) collective-permute-start(bf16[576,384]{1,0:T(8,128)(2,1)} %get-tuple-element.50), channel_id=1, source_target_pairs={{0,12},{1,13},{2,14},{3,15},{4,0},{5,1},{6,2},{7,3},{8,4},{9,5},{1... | collective-permute-start | bytes 1327112 | tf_op jit(solution)/shard_map/ppermute | solution.py:73
  170.8 38.9 %collective-permute-start.16 = (bf16[4,576,384]{2,1,0:T(8,128)(2,1)S(1)}, bf16[4,576,384]{2,1,0:T(8,128)(2,1)}, u32[]{:S(2)}, u32[]{:S(2)}) collective-permute-start(bf16[4,576,384]{2,1,0:T(8,128)(2,1)S(1)} %pad_maximum_fusion.8), channel_id=1, source_target_pairs={{0,1},{1,0},{2,3},{3,2},{4,5},{5,4},{6,7},{7,6},{8,9},{9,8},{10,11... | collective-permute-start | bytes 5308424 | tf_op jit(solution)/shard_map/ppermute | solution.py:73
  175.3 39.6 %collective-permute-start = (bf16[4,2,128,768]{3,2,0,1:T(8,128)(2,1)}, bf16[4,2,128,768]{3,2,0,1:T(8,128)(2,1)}, u32[]{:S(2)}, u32[]{:S(2)}) collective-permute-start(bf16[4,2,128,768]{3,2,0,1:T(8,128)(2,1)} %bitcast_select_fusion.4), channel_id=1, source_target_pairs={{0,2},{1,3},{2,0},{3,1},{4,6},{5,7},{6,4},{7,5},{8,10},{9,11},{10,... | collective-permute-start | bytes 4718600 | tf_op jit(solution)/shard_map/ppermute | solution.py:73
  175.9 91.2 %collective-permute-start.11 = (bf16[2,4,576,384]{3,2,1,0:T(8,128)(2,1)}, bf16[2,4,576,384]{3,2,1,0:T(8,128)(2,1)}, u32[]{:S(2)}, u32[]{:S(2)}) collective-permute-start(bf16[2,4,576,384]{3,2,1,0:T(8,128)(2,1)} %pad_maximum_fusion.2), channel_id=1, source_target_pairs={{0,16},{16,0},{1,17},{17,1},{2,18},{18,2},{3,19},{19,3},{4,20},{20... | collective-permute-start | bytes 10616840 | tf_op jit(solution)/shard_map/ppermute | solution.py:42
  176.0 91.1 %collective-permute-start.12 = (bf16[2,4,576,384]{3,2,1,0:T(8,128)(2,1)}, bf16[2,4,576,384]{3,2,1,0:T(8,128)(2,1)}, u32[]{:S(2)}, u32[]{:S(2)}) collective-permute-start(bf16[2,4,576,384]{3,2,1,0:T(8,128)(2,1)} %collective-permute-done.10), channel_id=1, source_target_pairs={{0,16},{16,0},{1,17},{17,1},{2,18},{18,2},{3,19},{19,3},{4,20},{20... | collective-permute-start | bytes 10616840 | tf_op jit(solution)/shard_map/ppermute | solution.py:42
  213.4 76.9 %collective-permute-start.17 = (bf16[2,4,576,384]{3,2,1,0:T(8,128)(2,1)}, bf16[2,4,576,384]{3,2,1,0:T(8,128)(2,1)}, u32[]{:S(2)}, u32[]{:S(2)}) collective-permute-start(bf16[2,4,576,384]{3,2,1,0:T(8,128)(2,1)} %pad_maximum_fusion.3), channel_id=1, source_target_pairs={{0,2},{1,3},{2,0},{3,1},{4,6},{5,7},{6,4},{7,5},{8,10},{9,11},{10,... | collective-permute-start | bytes 10616840 | tf_op jit(solution)/shard_map/ppermute | solution.py:73
  218.4 20.8 %collective-permute-start.1 = (bf16[4,128,768]{2,1,0:T(8,128)(2,1)}, bf16[4,128,768]{2,1,0:T(8,128)(2,1)}, u32[]{:S(2)}, u32[]{:S(2)}) collective-permute-start(bf16[4,128,768]{2,1,0:T(8,128)(2,1)} %dynamic-slice_bitcast_fusion.4), channel_id=1, source_target_pairs={{0,1},{1,0},{2,3},{3,2},{4,5},{5,4},{6,7},{7,6},{8,9},{9,8},{10,11... | collective-permute-start | bytes 2359304 | tf_op jit(solution)/shard_map/ppermute | solution.py:73
  240.5 17.4 %collective-permute-start.4 = (bf16[128,768]{1,0:T(8,128)(2,1)S(1)}, bf16[128,768]{1,0:T(8,128)(2,1)S(1)}, u32[]{:S(2)}, u32[]{:S(2)}) collective-permute-start(bf16[128,768]{1,0:T(8,128)(2,1)S(1)} %get-tuple-element.467), channel_id=1, source_target_pairs={{0,12},{1,13},{2,14},{3,15},{4,0},{5,1},{6,2},{7,3},{8,4},{9,5},{1... | collective-permute-start | bytes 589832 | tf_op jit(solution)/shard_map/ppermute | solution.py:73
  253.5 10.8 collective-permute-start.3
  257.9 8.5 collective-permute-start.2
  267.0 38.2 %collective-permute-start.18 = (bf16[2,4,576,384]{3,2,1,0:T(8,128)(2,1)}, bf16[2,4,576,384]{3,2,1,0:T(8,128)(2,1)}, u32[]{:S(2)}, u32[]{:S(2)}) collective-permute-start(bf16[2,4,576,384]{3,2,1,0:T(8,128)(2,1)} %pad_maximum_fusion.3), channel_id=1, source_target_pairs={{0,16},{16,0},{1,17},{17,1},{2,18},{18,2},{3,19},{19,3},{4,20},{20... | collective-permute-start | bytes 10616840 | tf_op jit(solution)/shard_map/ppermute | solution.py:42
  290.3 14.9 %collective-permute-start.19 = (bf16[2,4,576,384]{3,2,1,0:T(8,128)(2,1)}, bf16[2,4,576,384]{3,2,1,0:T(8,128)(2,1)}, u32[]{:S(2)}, u32[]{:S(2)}) collective-permute-start(bf16[2,4,576,384]{3,2,1,0:T(8,128)(2,1)} %collective-permute-done.17), channel_id=1, source_target_pairs={{0,16},{16,0},{1,17},{17,1},{2,18},{18,2},{3,19},{19,3},{4,20},{20... | collective-permute-start | bytes 10616840 | tf_op jit(solution)/shard_map/ppermute | solution.py:42
  343.4 9.8 collective-permute-start.22
  345.7 14.8 %collective-permute-start.21 = (bf16[128,768]{1,0:T(8,128)(2,1)S(1)}, bf16[128,768]{1,0:T(8,128)(2,1)S(1)}, u32[]{:S(2)}, u32[]{:S(2)}) collective-permute-start(bf16[128,768]{1,0:T(8,128)(2,1)S(1)} %add_convert_fusion), channel_id=1, source_target_pairs={{0,8},{1,9},{2,10},{3,11},{4,12},{5,13},{6,14},{7,15},{8,0},{9,1},... | collective-permute-start | bytes 589832 | tf_op jit(solution)/shard_map/ppermute | solution.py:73
  346.0 14.5 %collective-permute-start.20 = (bf16[128,768]{1,0:T(8,128)(2,1)S(1)}, bf16[128,768]{1,0:T(8,128)(2,1)S(1)}, u32[]{:S(2)}, u32[]{:S(2)}) collective-permute-start(bf16[128,768]{1,0:T(8,128)(2,1)S(1)} %add_convert_fusion), channel_id=1, source_target_pairs={{0,12},{1,13},{2,14},{3,15},{4,0},{5,1},{6,2},{7,3},{8,4},{9,5},{1... | collective-permute-start | bytes 589832 | tf_op jit(solution)/shard_map/ppermute | solution.py:73
  360.7 12.1 %collective-permute-start.23 = (bf16[4,128,768]{2,1,0:T(8,128)(2,1)S(1)}, bf16[4,128,768]{2,1,0:T(8,128)(2,1)S(1)}, u32[]{:S(2)}, u32[]{:S(2)}) collective-permute-start(bf16[4,128,768]{2,1,0:T(8,128)(2,1)S(1)} %get-tuple-element.465), channel_id=1, source_target_pairs={{0,1},{1,0},{2,3},{3,2},{4,5},{5,4},{6,7},{7,6},{8,9},{9,8},{10,11... | collective-permute-start | bytes 2359304 | tf_op jit(solution)/shard_map/ppermute | solution.py:73
  374.9 20.7 %collective-permute-start.24 = (bf16[2,4,128,768]{3,2,1,0:T(8,128)(2,1)}, bf16[2,4,128,768]{3,2,1,0:T(8,128)(2,1)}, u32[]{:S(2)}, u32[]{:S(2)}) collective-permute-start(bf16[2,4,128,768]{3,2,1,0:T(8,128)(2,1)} %pad_maximum_fusion.9), channel_id=1, source_target_pairs={{0,2},{1,3},{2,0},{3,1},{4,6},{5,7},{6,4},{7,5},{8,10},{9,11},{10,... | collective-permute-start | bytes 4718600 | tf_op jit(solution)/shard_map/ppermute | solution.py:73
  423.6 34.1 %all-to-all-start.1 = ((f32[16,3,2048]{2,1,0:T(4,128)}), f32[16,3,2048]{2,1,0:T(4,128)}, u32[]{:S(2)}, u32[]{:S(2)}) async-start(f32[16,3,2048]{2,1,0:T(4,128)} %broadcast_in_dim.221), calls=%async_computation.1 | async-start | bytes 1048576 | tf_op jit(solution)/shard_map/all_to_all | solution.py:48
  465.9 66.3 %all-to-all-start.2 = ((bf16[16,128,768]{2,1,0:T(8,128)(2,1)}), bf16[16,128,768]{2,1,0:T(8,128)(2,1)}, u32[]{:S(2)}, u32[]{:S(2)}) async-start(bf16[16,128,768]{2,1,0:T(8,128)(2,1)} %bitcast.455), calls=%async_computation.2 | async-start | bytes 6291456 | tf_op jit(solution)/shard_map/all_to_all | solution.py:846
  473.0 213.4 %all-gather.3.cloned.1.call-start = ((), (), s32[]{:S(2)}) async-start(), calls=%async_computation.9 | async-start | bytes 3342336 | tf_op jit(solution)/shard_map/all_gather | solution.py:863
  475.4 127.5 %collective-permute-start.29 = (bf16[128,5376]{1,0:T(8,128)(2,1)}, bf16[128,5376]{1,0:T(8,128)(2,1)}, u32[]{:S(2)}, u32[]{:S(2)}) collective-permute-start(bf16[128,5376]{1,0:T(8,128)(2,1)} %pad_maximum_fusion.11), channel_id=1, source_target_pairs={{0,16},{16,0},{1,17},{17,1},{2,18},{18,2},{3,19},{19,3},{4,20},{20... | collective-permute-start | bytes 4128776 | tf_op jit(solution)/shard_map/ppermute | solution.py:42
  477.7 75.0 %collective-permute-start.26 = (bf16[128,5376]{1,0:T(8,128)(2,1)}, bf16[128,5376]{1,0:T(8,128)(2,1)}, u32[]{:S(2)}, u32[]{:S(2)}) collective-permute-start(bf16[128,5376]{1,0:T(8,128)(2,1)} %pad_maximum_fusion.10), channel_id=1, source_target_pairs={{0,16},{16,0},{1,17},{17,1},{2,18},{18,2},{3,19},{19,3},{4,20},{20... | collective-permute-start | bytes 4128776 | tf_op jit(solution)/shard_map/ppermute | solution.py:42
  552.6 13.9 %collective-permute-start.25 = (bf16[128,6912]{1,0:T(8,128)(2,1)S(1)}, bf16[128,6912]{1,0:T(8,128)(2,1)S(1)}, u32[]{:S(2)}, u32[]{:S(2)}) collective-permute-start(bf16[128,6912]{1,0:T(8,128)(2,1)S(1)} %constant_dynamic-update-slice_fusion), channel_id=1, source_target_pairs={{0,16},{16,0},{1,17},{17,1},{2,18},{18,2},{3,19},{19,3},{4,20},{20... | collective-permute-start | bytes 5308424 | tf_op jit(solution)/shard_map/ppermute | solution.py:42
  613.2 57.1 %collective-permute-start.30 = (f16[4,2,584,384]{3,2,1,0:T(8,128)(2,1)}, f16[4,2,584,384]{3,2,1,0:T(8,128)(2,1)}, u32[]{:S(2)}, u32[]{:S(2)}) collective-permute-start(f16[4,2,584,384]{3,2,1,0:T(8,128)(2,1)} %get-tuple-element.421), channel_id=1, source_target_pairs={{0,2},{1,3},{2,0},{3,1},{4,6},{5,7},{6,4},{7,5},{8,10},{9,11},{10,... | collective-permute-start | bytes 10764296 | tf_op jit(solution)/shard_map/ppermute | solution.py:73
  620.0 36.6 %collective-permute-start.28 = (bf16[128,6912]{1,0:T(8,128)(2,1)S(1)}, bf16[128,6912]{1,0:T(8,128)(2,1)S(1)}, u32[]{:S(2)}, u32[]{:S(2)}) collective-permute-start(bf16[128,6912]{1,0:T(8,128)(2,1)S(1)} %constant_dynamic-update-slice_fusion.6), channel_id=1, source_target_pairs={{0,16},{16,0},{1,17},{17,1},{2,18},{18,2},{3,19},{19,3},{4,20},{20... | collective-permute-start | bytes 5308424 | tf_op jit(solution)/shard_map/ppermute | solution.py:42
  706.7 182.2 %collective-permute-start.34 = (f32[3200,768]{1,0:T(8,128)}, f32[3200,768]{1,0:T(8,128)}, u32[]{:S(2)}, u32[]{:S(2)}) collective-permute-start(f32[3200,768]{1,0:T(8,128)} %shard_map.435), channel_id=1, source_target_pairs={{0,16},{16,0},{1,17},{17,1},{2,18},{18,2},{3,19},{19,3},{4,20},{20... | collective-permute-start | bytes 29491208 | tf_op jit(solution)/shard_map/ppermute | solution.py:42
  711.7 22.9 %collective-permute-start.31 = (f16[4,584,384]{2,1,0:T(8,128)(2,1)S(1)}, f16[4,584,384]{2,1,0:T(8,128)(2,1)S(1)}, u32[]{:S(2)}, u32[]{:S(2)}) collective-permute-start(f16[4,584,384]{2,1,0:T(8,128)(2,1)S(1)} %get-tuple-element.427), channel_id=1, source_target_pairs={{0,1},{1,0},{2,3},{3,2},{4,5},{5,4},{6,7},{7,6},{8,9},{9,8},{10,11... | collective-permute-start | bytes 5382152 | tf_op jit(solution)/shard_map/ppermute | solution.py:73
  740.3 42.1 %collective-permute-start.32 = (f16[4,2,584,384]{3,2,1,0:T(8,128)(2,1)S(1)}, f16[4,2,584,384]{3,2,1,0:T(8,128)(2,1)S(1)}, u32[]{:S(2)}, u32[]{:S(2)}) collective-permute-start(f16[4,2,584,384]{3,2,1,0:T(8,128)(2,1)S(1)} %copy-done.22), channel_id=1, source_target_pairs={{0,2},{1,3},{2,0},{3,1},{4,6},{5,7},{6,4},{7,5},{8,10},{9,11},{10,... | collective-permute-start | bytes 10764296 | tf_op jit(solution)/shard_map/ppermute | solution.py:73
  791.0 22.9 %collective-permute-start.33 = (f16[4,584,384]{2,1,0:T(8,128)(2,1)S(1)}, f16[4,584,384]{2,1,0:T(8,128)(2,1)S(1)}, u32[]{:S(2)}, u32[]{:S(2)}) collective-permute-start(f16[4,584,384]{2,1,0:T(8,128)(2,1)S(1)} %get-tuple-element.425), channel_id=1, source_target_pairs={{0,1},{1,0},{2,3},{3,2},{4,5},{5,4},{6,7},{7,6},{8,9},{9,8},{10,11... | collective-permute-start | bytes 5382152 | tf_op jit(solution)/shard_map/ppermute | solution.py:73
  795.0 27.7 %collective-permute-start.40 = (f16[584,384]{1,0:T(8,128)(2,1)}, f16[584,384]{1,0:T(8,128)(2,1)S(1)}, u32[]{:S(2)}, u32[]{:S(2)}) collective-permute-start(f16[584,384]{1,0:T(8,128)(2,1)} %get-tuple-element.451), channel_id=1, source_target_pairs={{0,12},{1,13},{2,14},{3,15},{4,0},{5,1},{6,2},{7,3},{8,4},{9,5},{1... | collective-permute-start | bytes 1345544 | tf_op jit(solution)/shard_map/ppermute | solution.py:73
  796.8 59.9 %collective-permute-start.39 = (f16[584,384]{1,0:T(8,128)(2,1)}, f16[584,384]{1,0:T(8,128)(2,1)S(1)}, u32[]{:S(2)}, u32[]{:S(2)}) collective-permute-start(f16[584,384]{1,0:T(8,128)(2,1)} %get-tuple-element.452), channel_id=1, source_target_pairs={{0,8},{1,9},{2,10},{3,11},{4,12},{5,13},{6,14},{7,15},{8,0},{9,1},... | collective-permute-start | bytes 1345544 | tf_op jit(solution)/shard_map/ppermute | solution.py:73
  797.8 72.9 %collective-permute-start.38 = (f16[584,384]{1,0:T(8,128)(2,1)}, f16[584,384]{1,0:T(8,128)(2,1)}, u32[]{:S(2)}, u32[]{:S(2)}) collective-permute-start(f16[584,384]{1,0:T(8,128)(2,1)} %get-tuple-element.453), channel_id=1, source_target_pairs={{0,4},{1,5},{2,6},{3,7},{4,8},{5,9},{6,10},{7,11},{8,12},{9,13},{1... | collective-permute-start | bytes 1345544 | tf_op jit(solution)/shard_map/ppermute | solution.py:73
  820.8 51.8 %collective-permute-start.37 = (f16[584,384]{1,0:T(8,128)(2,1)}, f16[584,384]{1,0:T(8,128)(2,1)}, u32[]{:S(2)}, u32[]{:S(2)}) collective-permute-start(f16[584,384]{1,0:T(8,128)(2,1)} %get-tuple-element.455), channel_id=1, source_target_pairs={{0,12},{1,13},{2,14},{3,15},{4,0},{5,1},{6,2},{7,3},{8,4},{9,5},{1... | collective-permute-start | bytes 1345544 | tf_op jit(solution)/shard_map/ppermute | solution.py:73
  822.7 62.4 %collective-permute-start.36 = (f16[584,384]{1,0:T(8,128)(2,1)}, f16[584,384]{1,0:T(8,128)(2,1)}, u32[]{:S(2)}, u32[]{:S(2)}) collective-permute-start(f16[584,384]{1,0:T(8,128)(2,1)} %get-tuple-element.456), channel_id=1, source_target_pairs={{0,8},{1,9},{2,10},{3,11},{4,12},{5,13},{6,14},{7,15},{8,0},{9,1},... | collective-permute-start | bytes 1345544 | tf_op jit(solution)/shard_map/ppermute | solution.py:73
  856.7 30.3 %collective-permute-start.35 = (f16[584,384]{1,0:T(8,128)(2,1)}, f16[584,384]{1,0:T(8,128)(2,1)}, u32[]{:S(2)}, u32[]{:S(2)}) collective-permute-start(f16[584,384]{1,0:T(8,128)(2,1)} %get-tuple-element.457), channel_id=1, source_target_pairs={{0,4},{1,5},{2,6},{3,7},{4,8},{5,9},{6,10},{7,11},{8,12},{9,13},{1... | collective-permute-start | bytes 1345544 | tf_op jit(solution)/shard_map/ppermute | solution.py:73
  860.0 42.8 %all-to-all-start.3 = ((f32[16,160,48]{1,2,0:T(8,128)}), f32[16,160,48]{1,2,0:T(8,128)S(1)}, u32[]{:S(2)}, u32[]{:S(2)}) async-start(f32[16,160,48]{1,2,0:T(8,128)} %bitcast.485), calls=%async_computation.3 | async-start | bytes 1572864 | tf_op jit(solution)/shard_map/all_to_all | solution.py:867
  902.8 9.2 collective-permute-start.41
  980.5 19.8 %collective-permute-start.43 = (f32[3,256,256]{2,1,0:T(8,128)S(1)}, f32[3,256,256]{2,1,0:T(8,128)}, u32[]{:S(2)}, u32[]{:S(2)}) collective-permute-start(f32[3,256,256]{2,1,0:T(8,128)S(1)} %select_add_fusion), channel_id=1, source_target_pairs={{0,1},{1,0},{2,3},{3,2},{4,5},{5,4},{6,7},{7,6},{8,9},{9,8},{10,11... | collective-permute-start | bytes 2359304 | tf_op jit(solution)/shard_map/ppermute | solution.py:42
  1001.8 6.4 collective-permute-start.44
  1052.8 33.0 %all-to-all-start.7 = ((f16[8,96,768]{2,1,0:T(8,128)(2,1)}), f16[8,96,768]{2,1,0:T(8,128)(2,1)S(1)}, u32[]{:S(2)}, u32[]{:S(2)}) async-start(f16[8,96,768]{2,1,0:T(8,128)(2,1)} %bitcast.177), calls=%async_computation.7 | async-start | bytes 2359296 | tf_op jit(solution)/shard_map/all_to_all | solution.py:905
  (168 other events, 1594.5 us)
Sparse Core Ops, SparseCore 0:
  601.8 84.5 all-gather.2

commit v2 on v1

--- a/solution.py
+++ b/solution.py
@@ -33,7 +33,6 @@
 GROUP = ("section", "yc", "xd")
 NOTE = 8
 UPPER = ((0, 0), (0, 1), (0, 2), (1, 1), (1, 2), (2, 2))
-MOMENT_SCALE = 2.0**21
 VMEM_BYTES = 56 * 1024 * 1024
 
 
@@ -77,8 +76,12 @@
     return lax.dynamic_index_in_dim(block, index, axis, keepdims=False)
 
 
+def nothing_of(*arrays):
+    return sum(jnp.sum(array[(slice(0, 1),) * array.ndim].astype(jnp.float32)) * 0.0 for array in arrays)
+
+
 def after(value, *others):
-    return lax.optimization_barrier((value,) + others)[0]
+    return value + nothing_of(*others).astype(value.dtype)
 
 
 def column_near(block):
@@ -95,17 +98,6 @@
 
 def gathered_near(block):
     return planes_near(plane_near(column_near(block)))
-
-
-def owners_near(section):
-    za, yb, xd = span()
-    a, b, c = lax.axis_index("za"), lax.axis_index(("yb", "yc")), lax.axis_index("xd")
-    places = jnp.arange(za * yb * xd, dtype=jnp.int32)
-    far, near, high = places // (xd * za), places // za % xd, places % za
-    high = (a + high) % za
-    row = jnp.where(section == 0, (b + far) % yb, (b + near) % yb)
-    col = jnp.where(section == 0, (c + near) % xd, (c + far) % xd)
-    return (high * yb + row) * xd + col
 
 
 def places_near(section):
@@ -118,16 +110,24 @@
     return (far * xd + near) * za + high
 
 
-def assemble_kernel(widths, each, spot_ref, *refs):
+def assemble_kernel(widths, count, spot_ref, *refs):
     sources, outs = refs[: -len(widths)], refs[-len(widths) :]
+    owner = pl.program_id(0)
+    each, half = sources[0].shape[0], sources[0].shape[2]
     for number, source in enumerate(sources):
-
-        @pl.when(pl.program_id(0) // each == number)
-        def _(source=source):
-            start = 0
-            for out, width in zip(outs, widths):
-                out[...] = source[0, start : start + width, :]
-                start += width
+        kind = number // (len(sources) // 2)
+        piece = number % (len(sources) // 2)
+        place = spot_ref[kind * count + owner]
+        for side in range(2):
+
+            @pl.when((place // each == piece) & (spot_ref[2 * count + kind] == side))
+            def _(source=source, place=place, side=side):
+                start = 0
+                for out, width in zip(outs, widths):
+                    out[:, side * half : (side + 1) * half] = source[
+                        place % each, start : start + width, :
+                    ]
+                    start += width
 
 
 def assembled(own, other, widths):
@@ -145,26 +145,16 @@
         whole = jnp.concatenate([left, right], -1)
         starts = [sum(widths[:n]) for n in range(5)]
         return [whole[:, starts[n] : starts[n + 1]].reshape(-1, 2 * half) for n in range(4)]
-    sides = jnp.stack([section, 1 - section]).astype(jnp.int32)
-    spots = jnp.concatenate(
-        [owners_near(section), owners_near(1 - section), jnp.repeat(sides, count)]
-    ).astype(jnp.int32)
-    each = pieces[0].shape[0]
-
-    def source_at(number):
-        return lambda step, spot: (jnp.clip(step - number * each, 0, each - 1), 0, 0)
-
+    sides = jnp.stack([section, 1 - section])
+    spots = jnp.concatenate([places_near(section), places_near(1 - section), sides])
     return pl.pallas_call(
-        functools.partial(assemble_kernel, tuple(widths), each),
+        functools.partial(assemble_kernel, tuple(widths), count),
         grid_spec=pltpu.PrefetchScalarGridSpec(
             num_scalar_prefetch=1,
-            grid=(2 * count,),
-            in_specs=[
-                pl.BlockSpec((1, rows, half), source_at(number)) for number in range(len(pieces))
-            ],
+            grid=(count,),
+            in_specs=[pl.BlockSpec(piece.shape, lambda step, spot: (0, 0, 0)) for piece in pieces],
             out_specs=[
-                pl.BlockSpec((width, half), lambda step, spot: (spot[step], spot[2 * count + step]))
-                for width in widths
+                pl.BlockSpec((width, 2 * half), lambda step, spot: (step, 0)) for width in widths
             ],
         ),
         out_shape=[
@@ -174,7 +164,7 @@
         cost_estimate=pl.CostEstimate(
             flops=0, bytes_accessed=8 * count * rows * half, transcendentals=0
         ),
-    )(spots, *pieces)
+    )(spots.astype(jnp.int32), *pieces)
 
 
 def exponent_for(bound):
@@ -240,9 +230,8 @@
     return block[..., :-NOTE, :].astype(jnp.float32) * jnp.exp2(-exponent_in(block))
 
 
-def row_sums(block):
-    plane = planes_reduced(planes_cut(block), lax.add)
-    return sum(part.astype(jnp.float32) for part in column_parts(plane_reduced(plane, lax.add)))
+def column_sums(column):
+    return sum(part.astype(jnp.float32) for part in column_parts(column))
 
 
 def parted_weights(grads, exponent):
@@ -251,17 +240,10 @@
     return planes_cut(jnp.concatenate(own + [note], 1))
 
 
-def summed_weights(layer_parts, *before):
+def summed_weights(parts_early, parts_late, *before):
     first_side = lax.axis_index("section") == 0
-    plane_late = planes_reduced(layer_parts[1], added)
-    column_late = plane_reduced(plane_late, added)
-    parts_early = [after(part, column_late) for part in layer_parts[0]]
-    plane_early = planes_reduced(parts_early, added)
-    parts_late = column_parts(column_late)
-    column_early = plane_reduced(plane_early, added)
-    parts_early = column_parts(column_early)
-    parts_early[0] = after(parts_early[0], *before)
     halves = [sum(decoded(part) for part in parts) for parts in (parts_early, parts_late)]
+    halves[0] = after(halves[0], *before)
     kept = jnp.where(first_side, halves[0], halves[1])
     came = swapped(jnp.where(first_side, halves[1], halves[0]), "section")
     return jnp.where(
@@ -326,8 +308,8 @@
     return lax.dynamic_slice_in_dim(values, (1 - lax.axis_index("section")) * half, half, 1)
 
 
-def widest_column(values):
-    return jnp.max(jnp.sum(jnp.square(values.astype(jnp.float32)), 0))
+def largest(values):
+    return jnp.max(jnp.abs(values)).astype(jnp.float32)
 
 
 def gelu_tanh(values):
@@ -378,7 +360,7 @@
     return (outputs, saved)
 
 
-def layer_backward(saved, grad_out, weights):
+def layer_backward(saved, grad_out, weights, nothing):
     qkv_t, proj_t, fc_t, down_t, vectors = weights
     g_one, b_one, q_bias, v_bias, p_bias, g_two, b_two, f_bias, d_bias = split_vectors(vectors)
     (
@@ -431,7 +413,7 @@
         -1,
     ).astype(jnp.bfloat16)
     qkv_sums = jnp.sum(grad_qkv, 0, keepdims=True, dtype=jnp.float32)
-    late = with_other(grad_qkv, grad_attn, grad_pre, grad_mlp)
+    late = with_other(grad_qkv + nothing, grad_attn, grad_pre, grad_mlp)
     wide = hidden_pre.shape[1]
 
     def taken(block, start, width):
@@ -443,8 +425,8 @@
         (taken(late, 4 * model_width, wide), taken(early, wide + 2 * model_width, model_width)),
         (taken(early, 0, wide), taken(late, 4 * model_width + wide, model_width)),
     )
-    bounds = [widest_column(block) for block in (early, late)]
-    exponent = exponent_for(jnp.sqrt(bounds[0]) * jnp.sqrt(bounds[1]))
+    bound = late.shape[0] * largest(early) * largest(late)
+    exponent = exponent_for(bound)
     scale = jnp.exp2(exponent)
     d_qkv, d_proj, d_fc, d_down = (
         (contract_rows(left, own_half(right)) * scale).astype(jnp.float16)
@@ -479,8 +461,8 @@
 
 
 def halves_of(values):
-    high = values.astype(jnp.bfloat16)
-    return (high, (values - high.astype(jnp.float32)).astype(jnp.bfloat16))
+    high = lax.reduce_precision(values, 8, 7)
+    return (high.astype(jnp.bfloat16), (values - high).astype(jnp.bfloat16))
 
 
 def newton_kernel(gram_ref, out_ref, pair_a, pair_b, gram_now, poly, product):
@@ -525,21 +507,34 @@
     trace = jnp.sum(jnp.where(diagonal, full, 0.0))
     inverse = 1.0 / (jnp.sqrt(jnp.full((1, 1), trace, jnp.float32)) + 1e-07)
     gram_now[...] = full * (inverse * inverse)
-    for iteration in range(5):
+
+    def step_poly():
         store_pair(pair_a, gram_now[...])
         multiply(pair_a, pair_a, into(poly))
         poly[...] = jnp.where(diagonal, a, 0.0) + b * gram_now[...] + c * poly[...]
         store_pair(pair_b, poly[...])
-        if iteration < 4:
-            terms = 3 if iteration < 2 else 2
-            multiply(pair_a, pair_b, into(gram_now), terms)
-            store_pair(pair_a, gram_now[...])
-            multiply(pair_a, pair_b, into(gram_now), terms)
-        if iteration == 0:
-            product[...] = poly[...]
-        else:
-            store_pair(pair_a, product[...])
-            multiply(pair_a, pair_b, into(product))
+
+    def step_gram(terms):
+        multiply(pair_a, pair_b, into(gram_now), terms)
+        store_pair(pair_a, gram_now[...])
+        multiply(pair_a, pair_b, into(gram_now), terms)
+
+    def step_product():
+        store_pair(pair_a, product[...])
+        multiply(pair_a, pair_b, into(product))
+
+    step_poly()
+    step_gram(3)
+    product[...] = poly[...]
+
+    @pl.loop(0, 3)
+    def _(iteration):
+        step_poly()
+        step_gram(2)
+        step_product()
+
+    step_poly()
+    step_product()
     out_ref[...] = product[...] * inverse
 
 
@@ -622,7 +617,7 @@
     exps = exp_ref[...]
     cols = lax.broadcasted_iota(jnp.int32, exps.shape, 1)
     chosen = jnp.where(cols == target_ref[...], 1.0, 0.0).astype(jnp.bfloat16)
-    soft_ref[...] = plain_dot(exps, table_ref[...])
+    soft_ref[...] = plain_dot(exps, table_ref[...]).astype(jnp.bfloat16)
     hard_ref[...] = plain_dot(chosen, table_ref[...]).astype(jnp.bfloat16)
 
 
@@ -634,7 +629,7 @@
         head_pull_kernel,
         grid=(count // step,),
         out_shape=[
-            jax.ShapeDtypeStruct((count, width), jnp.float32),
+            jax.ShapeDtypeStruct((count, width), jnp.bfloat16),
             jax.ShapeDtypeStruct((count, width), jnp.bfloat16),
         ],
         in_specs=[
@@ -710,6 +705,7 @@
         row_scatter_kernel,
         grid=(count // step,),
         out_shape=jax.ShapeDtypeStruct(total.shape, total.dtype),
+        input_output_aliases={2: 0},
         in_specs=[
             pl.BlockSpec((1, step), lambda i: (0, i)),
             pl.BlockSpec((step, width), lambda i: (i, 0)),
@@ -723,6 +719,32 @@
             transcendentals=0,
         ),
     )(ids.reshape(1, count), parts, total)
+
+
+def to_spots(matrices, code):
+    widest = max(matrix.shape[0] for matrix in matrices)
+    padded = jnp.stack([jnp.pad(m, ((0, widest - m.shape[0]), (0, 0))) for m in matrices])
+    padded = padded.reshape(4, 2, widest // 2, -1)
+    if code:
+        padded = jnp.pad(padded, ((0, 0), (0, 0), (0, NOTE), (0, 0)))
+        padded = coded(padded, exponent_for(jnp.max(jnp.abs(padded))))
+    sent = lax.all_to_all(padded, "section", 1, 1, tiled=True)
+    sent = sent.reshape((-1,) + sent.shape[2:])
+    return lax.all_to_all(sent, SPOTS, 0, 0, tiled=True), sent
+
+
+def at_spots(held, code):
+    if code:
+        exponents = held[:, -1:, :1].astype(jnp.float32)
+        held = held[:, :-NOTE].astype(jnp.float32) * jnp.exp2(-exponents)
+    return held.reshape(-1, held.shape[2])
+
+
+def from_spots(held):
+    back = lax.all_to_all(held.reshape(8, -1, held.shape[1]), SPOTS, 0, 0, tiled=True)
+    back = back.reshape((4, 2) + back.shape[1:])
+    back = lax.all_to_all(back, "section", 1, 1, tiled=True)
+    return back.reshape(4, -1, back.shape[3])
 
 
 def shards(
@@ -789,14 +811,22 @@
     head_norm = small[norm_at:places_at]
     positions = small[places_at : places_at + place_rows]
     pack = jnp.concatenate(masters_t, 0).astype(jnp.bfloat16)
+    local_ids = ids_all - vocab_start
+    inside = (local_ids >= 0) & (local_ids < shard_rows)
+    safe_ids = jnp.clip(local_ids, 0, shard_rows - 1)
+    contrib = jnp.where(
+        inside[..., None], jnp.take(table_rows, safe_ids, axis=0), jnp.zeros((), jnp.bfloat16)
+    )
     first_side = section_index == 0
     kept_half = own_half(pack)
     came_half = swapped(other_half(pack), "section")
     blocks = [jnp.where(section_index == layer, kept_half, came_half) for layer in range(2)]
-    column_early = column_near(blocks[0])
-    column_late = column_near(after(blocks[1], column_early))
+    column_early = after(column_near(blocks[0]), small)
+    column_late = column_near(after(lax.optimization_barrier(blocks[1]), contrib))
+    rows_plane = planes_reduced(planes_cut(contrib), lax.add)
     planes = [planes_near(plane_near(column_early))]
-    planes.append(planes_near(plane_near(after(column_late, planes[0][-1]))))
+    planes.append(planes_near(plane_near(after(column_late, rows_plane))))
+    rows_in = column_sums(plane_reduced(rows_plane, lax.add))
     layer_sets = []
     for layer, own in enumerate(planes):
         other = [swapped(piece, "section") for piece in own]
@@ -805,13 +835,6 @@
             + [small[layer * layer_rows : (layer + 1) * layer_rows]]
         )
 
-    local_ids = ids_all - vocab_start
-    inside = (local_ids >= 0) & (local_ids < shard_rows)
-    safe_ids = jnp.clip(local_ids, 0, shard_rows - 1)
-    contrib = jnp.where(
-        inside[..., None], jnp.take(table_rows, safe_ids, axis=0), jnp.zeros((), jnp.bfloat16)
-    )
-    rows_in = row_sums(contrib)
 
     current = rows_in + positions
     kept = []
@@ -826,14 +849,17 @@
     counted = counted.astype(jnp.float32).reshape(-1)
     token_total = jnp.sum(true_counts).astype(jnp.float32)
     local_targets = targets_all.reshape(-1) - vocab_start
-    targets_col = jnp.where(local_targets < shard_rows, local_targets, -1)[:, None]
+    targets_here = (local_targets >= 0) & (local_targets < shard_rows)
+    targets_col = jnp.where(targets_here, local_targets, -1)[:, None]
     exps, stats, rows_all = head_forward(
         blocks, places_near(section_index), table_rows, targets_col, shard_rows
     )
     stats = stats[:, :3].T
-    block_max = stats[0]
+    block_max, target_logit = stats[0], stats[2]
     stats = spread_small(stats)
     soft_pull, hard_pull = head_pull(exps, targets_col, table_rows)
+    moments_sent = [after(moment, blocks) for moment in moments_t]
+    held_moments = at_spots(to_spots(moments_sent, True)[0], True)
     highest = jnp.max(stats[:, 0], 0)
     merged_sum = jnp.sum(stats[:, 1] * jnp.exp(stats[:, 0] - highest), 0)
     partition = highest + jnp.log(merged_sum)
@@ -842,32 +868,52 @@
     token_weight = counted / token_total
     pull = token_weight * (1.0 + 2.0 * Z_WEIGHT * partition) * jnp.exp(block_max - partition)
     token_scales = jnp.stack([pull, token_weight], 1)
-    grad_rows = pull[:, None] * soft_pull - token_weight[:, None] * hard_pull.astype(jnp.float32)
+    z_pull = token_weight * (1.0 + 2.0 * Z_WEIGHT * partition)
+    at_target = z_pull * jnp.exp(target_all - partition) - token_weight
+    at_target = lax.reduce_precision(at_target, 8, 7)
+    in_soft = jnp.where(targets_here, jnp.exp(target_logit - block_max), 0.0)
+    hard_scale = at_target - pull * lax.reduce_precision(in_soft, 8, 7)
+    hard_scale = after(hard_scale, held_moments)
+    grad_rows = pull[:, None] * soft_pull.astype(jnp.float32) + hard_scale[:, None] * (
+        hard_pull.astype(jnp.float32)
+    )
     grad_parts = lax.all_to_all(
         grad_rows.astype(jnp.bfloat16).reshape(fsdp_count, -1, model_width), FSDP, 0, 0, tiled=True
     )
     table_grad = head_table(exps, token_scales, targets_col, rows_all)
+    grad_parts = after(grad_parts, table_grad)
     grad_normed = jnp.sum(grad_parts, 0, dtype=jnp.float32)
     grad_now, d_fgain, d_fbias = jax.vjp(layer_norm, final_rows, head_norm[0:1], head_norm[1:2])[1](
         grad_normed
     )
-    layer_parts, vecs_parts = [], []
+    planes_part, vecs_parts = [], []
+    nothing = jnp.zeros((), jnp.bfloat16)
     for layer in reversed(range(section_count)):
         grad_now, grads, d_vectors, exponent = layer_backward(
-            kept[layer], grad_now, layer_sets[layer]
+            kept[layer], grad_now, layer_sets[layer], nothing
         )
-        layer_parts.insert(0, parted_weights(grads, exponent))
+        parted = parted_weights(grads, exponent)
+        planes_part.insert(0, planes_reduced(parted, added))
         if layer:
-            grad_now = after(grad_now, layer_parts[0][-1])
+            grad_now = after(grad_now, parted[-1])
+            column_late = plane_reduced(planes_part[0], added)
+            parts_late = column_parts(column_late)
+            nothing = nothing_of(column_late).astype(jnp.bfloat16)
         vecs_parts = d_vectors + vecs_parts
     emb_all = lax.all_gather(grad_now.astype(jnp.bfloat16), FSDP, axis=0, tiled=True)
-    table_grad = rows_scattered(table_grad, local_ids.reshape(-1), emb_all)
+    late_ids = local_ids.reshape(-1) + nothing_of(planes_part[0], *parts_late).astype(
+        jnp.int32
+    )
+    table_grad = rows_scattered(table_grad, late_ids, emb_all)
     small_grad = lax.optimization_barrier(padded_rows(vecs_parts + [d_fgain, d_fbias, grad_now]))
     small_grad = jnp.moveaxis(small_grad.reshape(small_rows, fsdp_count, -1), 1, 0)
     small_grad = jnp.sum(lax.all_to_all(small_grad, FSDP, 0, 0, tiled=True), 0)
     table_grad = (table_grad + swapped(table_grad, "section"))[:shard_rows]
-    table_squares = jnp.sum(table_grad * table_grad)
-    flushed = summed_weights(layer_parts, table_squares)
+    own_rows = shard_rows // section_count
+    table_part = lax.dynamic_slice_in_dim(table_grad, section_index * own_rows, own_rows, 0)
+    table_squares = jnp.sum(table_part * table_part)
+    parts_early = column_parts(plane_reduced(planes_part[0], added))
+    flushed = summed_weights(parts_early, parts_late, table_squares, small_grad)
     loss_row = jnp.broadcast_to(loss_part, (1, small_grad.shape[1]))
     small_grad = jnp.concatenate([small_grad, loss_row], 0)
     small_grad = small_grad + swapped(small_grad, "section")
@@ -876,9 +922,13 @@
     norm_grad = small_grad[norm_at:places_at]
     pos_grad = small_grad[places_at : places_at + place_rows]
     weight_grad = flushed
+    held_grads, set_out = to_spots([weight_grad[starts[n] : starts[n + 1]] for n in range(4)], True)
+    held_grads = at_spots(held_grads, True)
     own_squares = jnp.sum(weight_grad * weight_grad) + jnp.sum(vecs_grad * vecs_grad)
-    shared_squares = table_squares + jnp.sum(pos_grad * pos_grad) + jnp.sum(norm_grad * norm_grad)
-    device_squares = own_squares + jnp.where(section_index == 0, shared_squares, 0.0)
+    shared_squares = jnp.sum(pos_grad * pos_grad) + jnp.sum(norm_grad * norm_grad)
+    device_squares = (
+        own_squares + table_squares + jnp.where(section_index == 0, shared_squares, 0.0)
+    )
     square_sum = lax.psum(
         jnp.sum(spread_small(jnp.full((8, 128), device_squares)), 0)[0, 0], "section"
     )
@@ -888,23 +938,14 @@
     new_moms = [
         MOMENTUM * moments_t[n] + factor * weight_grad[starts[n] : starts[n + 1]] for n in range(4)
     ]
-    widest = max(widths)
-    padded = jnp.stack([jnp.pad(mom, ((0, widest - mom.shape[0]), (0, 0))) for mom in new_moms])
-    padded = (padded * MOMENT_SCALE).astype(jnp.float16)
-    padded = padded.reshape(4, 2, widest // 2, model_width)
-    sent = lax.all_to_all(padded, "section", 1, 1, tiled=True)
-    sent = sent.reshape(4 * section_count, widest // 2, model_width)
-    held = lax.all_to_all(sent, SPOTS, 0, 0, tiled=True).reshape(-1, model_width)
-    held = held.astype(jnp.float32) * (1.0 / MOMENT_SCALE)
+    held = MOMENTUM * held_moments + factor * held_grads
     high, lower = halves_of(held)
-    crossed = contract_rows(high, lower)
-    gram = contract_rows(high, high) + (crossed + crossed.T) + contract_rows(lower, lower)
+    gram = contract_rows(
+        jnp.concatenate([lower, lower, high, high]), jnp.concatenate([lower, high, lower, high])
+    )
     product = newton_product(gram_summed(gram))
     turned = jnp.matmul(held, product, precision=lax.Precision.HIGH).astype(jnp.float16)
-    turned = turned.reshape(4 * section_count, widest // 2, model_width)
-    back = lax.all_to_all(turned, SPOTS, 0, 0, tiled=True)
-    back = back.reshape(4, section_count, widest // 2, model_width)
-    back = lax.all_to_all(back, "section", 1, 1, tiled=True).reshape(4, widest, model_width)
+    back = from_spots(turned)
     back = back.astype(jnp.float32)
 
     embed_new, embed_m_new, embed_v_new = adam_step(

time: 1110 us -> 1120 us (level)
  waiting for transfers between devices: 368 us -> 302 us
  starting transfers between devices: 113 us -> 154 us
  Pallas kernels: 182 us -> 162 us
  other arithmetic: 163 us -> 177 us
  local copies, waits for them, and re-layouts: 117 us -> 131 us
  between operations: 37.7 us -> 50.7 us
    ppermute x30, waiting for transfers between devices: 260 us -> 228 us  [moved(): return lax.ppermute(block, ('section',) + FSDP, route(level, distance))]
    ppermute x30, starting transfers between devices: 72.2 us -> 99.9 us  [moved(): return lax.ppermute(block, ('section',) + FSDP, route(level, distance))]
    all_to_all x1, waiting for transfers between devices: 54 us -> 29.6 us  [shards(): lax.all_to_all(grad_rows.astype(jnp.bfloat16).reshape(fsdp_count, -1, mod...]
    reduce_sum x7 -> x2, other arithmetic: 28.3 us -> 4.9 us  [the longest x1 4.28 us: shards(): table_squares = jnp.sum(table_part * table_part)]
    reduce_max x4 -> x7, other arithmetic: 5.41 us -> 26.5 us  [the longest x4 23.8 us: largest(): return jnp.max(jnp.abs(values)).astype(jnp.float32)]
    pallas_call x2, Pallas kernels: 46.4 us -> 28.9 us  [assembled(): pl.pallas_call(functools.partial(assemble_kernel, tuple(widths), count),...]
    all_to_all x1, starting transfers between devices: 5.68 us -> 21.6 us  [shards(): small_grad = jnp.sum(lax.all_to_all(small_grad, FSDP, 0, 0, tiled=True), 0)]
    add x6 -> x12, other arithmetic: 2.03 us -> 16.4 us  [the longest x1 11.7 us: shards(): table_grad = (table_grad + swapped(table_grad, 'section'))[:shard_rows]]
  transfers between devices with their start and end apart: 51 -> 52, of which waited for: 28 -> 29; matrix products, arithmetic and copies ran while one was open for 25% -> 23% of each run, Pallas kernels for 7% -> 6%
where the time goes in v2:
time: 1120 us; the launch traced here: 1110 us
  waiting for transfers between devices  302 us (27%)
  other arithmetic  177 us (16%)
  Pallas kernels  162 us (14%)
  starting transfers between devices  154 us (14%)
  local copies, waits for them, and re-layouts  131 us (12%)
  matrix products  66.8 us (6%)
  blocking collectives  66.2 us (6%)
  between operations  50.7 us (5%)
    ppermute x30, waiting for transfers between devices, moved(): return lax.ppermute(block, ('section',) + FSDP, route(level, distance))  228 us
    ppermute x30, starting transfers between devices, moved(): return lax.ppermute(block, ('section',) + FSDP, route(level, distance))  99.9 us
    pallas_call x1, Pallas kernels, newton_product(): pl.pallas_call(newton_kernel, out_shape=jax.ShapeDtypeStruct(square, jnp....  38.1 us
    unnamed x440, local copies, waits for them, and re-layouts  33.9 us
    all_to_all x1, blocking collectives, to_spots(): return (lax.all_to_all(sent, SPOTS, 0, 0, tiled=True), sent)  33.6 us
    all_to_all x1, waiting for transfers between devices, shards(): lax.all_to_all(grad_rows.astype(jnp.bfloat16).reshape(fsdp_count, -1, mod...  29.6 us
    pallas_call x2, Pallas kernels, assembled(): pl.pallas_call(functools.partial(assemble_kernel, tuple(widths), count),...  28.9 us
    pallas_call x1, Pallas kernels, head_pull(): pl.pallas_call(head_pull_kernel, grid=(count // step,), out_shape=[jax.Sh...  26.8 us
  transfers between devices with their start and end apart: 52, of which 29 were waited for; matrix products, arithmetic and copies ran while one was open for 23% of the time, Pallas kernels for 6%

profile of v2, /device:TPU:0, one launch (start us, length us, event | category | flops | bytes accessed | tf_op | source)
XLA Modules:
  0.0 1110.3 jit_solution(6178871125158775184)
XLA Ops:
  14.4 8.1 all-to-all-start
  37.4 7.1 collective-permute-done.8
  44.6 18.8 %collective-permute-done.7 = bf16[576,384]{1,0:T(8,128)(2,1)S(1)} collective-permute-done((bf16[576,384]{1,0:T(8,128)(2,1)S(1)}, bf16[576,384]{1,0:T(8,128)(2,1)S(1)}, u32[]{:S(2)}, u32[]{:S(2)}) %collective-permute-start.7) | collective-permute-done | bytes 442400 | tf_op jit(solution)/shard_map/ppermute | solution.py:72
  67.2 13.1 %gather_fusion = bf16[2048,768]{1,0:T(8,128)(2,1)} fusion(bf16[3200,768]{1,0:T(8,128)(2,1)} %pad.32.table_ref, s32[2048]{0:T(1024)S(1)} %bitcast_clamp_fusion), kind=kCustom, calls=%fused_computation | custom fusion | bytes 6299648 | tf_op jit(solution)/shard_map/jit(_take)/gather | solution.py:818
  85.0 6.7 collective-permute-done.9
  100.4 9.5 collective-permute-start.15
  113.9 8.6 collective-permute-done.15
  122.6 12.8 %collective-permute-done.14 = bf16[576,384]{1,0:T(8,128)(2,1)S(1)} collective-permute-done((bf16[576,384]{1,0:T(8,128)(2,1)S(1)}, bf16[576,384]{1,0:T(8,128)(2,1)S(1)}, u32[]{:S(2)}, u32[]{:S(2)}) %collective-permute-start.14) | collective-permute-done | bytes 442400 | tf_op jit(solution)/shard_map/ppermute | solution.py:72
  136.4 25.8 %collective-permute-done.16 = bf16[4,576,384]{2,1,0:T(8,128)(2,1)S(1)} collective-permute-done((bf16[4,576,384]{2,1,0:T(8,128)(2,1)S(1)}, bf16[4,576,384]{2,1,0:T(8,128)(2,1)S(1)}, u32[]{:S(2)}, u32[]{:S(2)}) %collective-permute-start.16) | collective-permute-done | bytes 1769504 | tf_op jit(solution)/shard_map/ppermute | solution.py:72
  177.2 10.8 collective-permute-done.1
  189.3 10.8 collective-permute-start.4
  200.5 4.9 collective-permute-done.4
  205.4 10.1 collective-permute-start.2
  219.8 14.4 %shard_map.430 = (bf16[2304,768]{1,0:T(8,128)(2,1)}, bf16[768,768]{1,0:T(8,128)(2,1)}, bf16[3072,768]{1,0:T(8,128)(2,1)}, bf16[3072,768]{1,0:T(8,128)(2,1)}) custom-call(s32[34]{0:T(128)} %pad_add_fusion.1.spot_ref, bf16[8,576,384]{2,1,0:T(8,128)(2,1)} %bitcast.38.refs_0_, bf16[8,576,384]{2,1,0:T(8,128)(2,1)} %bitcast.39.refs_1_, ...), custom_call_target="tpu_custom_call" | custom-call | bytes 28311552 | tf_op jit(solution)/shard_map/pallas_call | solution.py:150
  241.1 5.4 multiply_convert_fusion.5
  247.9 14.5 %shard_map.431 = (bf16[2304,768]{1,0:T(8,128)(2,1)}, bf16[768,768]{1,0:T(8,128)(2,1)}, bf16[3072,768]{1,0:T(8,128)(2,1)}, bf16[3072,768]{1,0:T(8,128)(2,1)}) custom-call(s32[34]{0:T(128)} %pad_add_fusion.1.spot_ref, bf16[8,576,384]{2,1,0:T(8,128)(2,1)} %bitcast.62.refs_0_, bf16[8,576,384]{2,1,0:T(8,128)(2,1)} %bitcast.63.refs_1_, ...), custom_call_target="tpu_custom_call" | custom-call | bytes 28311552 | tf_op jit(solution)/shard_map/pallas_call | solution.py:150
  269.3 5.4 multiply_convert_fusion.4
  287.4 8.2 collective-permute-done.21
  297.3 10.5 collective-permute-done.23
  316.0 14.8 %collective-permute-done.24 = bf16[2,4,128,768]{3,2,1,0:T(8,128)(2,1)} collective-permute-done((bf16[2,4,128,768]{3,2,1,0:T(8,128)(2,1)}, bf16[2,4,128,768]{3,2,1,0:T(8,128)(2,1)}, u32[]{:S(2)}, u32[]{:S(2)}) %collective-permute-start.24) | collective-permute-done | bytes 1572896 | tf_op jit(solution)/shard_map/ppermute | solution.py:72
  334.1 22.1 %shard_map.432 = (bf16[2048,3200]{1,0:T(8,128)(2,1)}, f32[2048,128]{1,0:T(8,128)}, bf16[2048,768]{1,0:T(8,128)(2,1)}) custom-call(s32[16]{0:T(128)} %copy-done.180, bf16[16,128,768]{2,1,0:T(8,128)(2,1)} %bitcast.581, bf16[16,128,768]{2,1,0:T(8,128)(2,1)} %bitcast.582, bf16[3200,768]{1,0:T(8,128)(2,1)} %pad.32.table_ref, s32[2048,1]{1,0:T(8,128)} %and_select_fusion.target_ref), custom_call_target="tpu_custom_call" | custom-call | flops 10066329600 | bytes 21168128 | tf_op jit(solution)/shard_map/pallas_call | solution.py:585
  365.4 5.6 all_to_all.55
  371.9 8.6 all-to-all-start.1
  385.4 10.5 all-to-all-done.1
  400.2 26.8 %shard_map.433 = (bf16[2048,768]{1,0:T(8,128)(2,1)}, bf16[2048,768]{1,0:T(8,128)(2,1)}) custom-call(bf16[2048,3200]{1,0:T(8,128)(2,1)} %get-tuple-element.49.exp_ref, s32[2048,1]{1,0:T(8,128)} %and_select_fusion.target_ref, bf16[3200,768]{1,0:T(8,128)(2,1)} %pad.32.table_ref), custom_call_target="tpu_custom_call" | custom-call | flops 20132659200 | bytes 27459584 | tf_op jit(solution)/shard_map/pallas_call | solution.py:628
  446.8 26.1 %shard_map.434.total_ref = f32[3200,768]{1,0:T(8,128)} custom-call(bf16[2048,3200]{1,0:T(8,128)(2,1)} %get-tuple-element.49.exp_ref, f32[2048,2]{1,0:T(8,128)} %copy.670.token_ref, s32[2048,1]{1,0:T(8,128)} %and_select_fusion.target_ref, bf16[2048,768]{1,0:T(8,128)(2,1)} %get-tuple-element.52.row_ref), custom_call_target="tpu_custom_call" | custom-call | flops 10066329600 | bytes 26083328 | tf_op jit(solution)/shard_map/pallas_call | solution.py:670
  474.8 29.6 %all-to-all-done.4 = bf16[16,128,768]{2,1,0:T(8,128)(2,1)} async-done(((bf16[16,128,768]{2,1,0:T(8,128)(2,1)}), bf16[16,128,768]{2,1,0:T(8,128)(2,1)}, u32[]{:S(2)}, u32[]{:S(2)}) %all-to-all-start.4) | async-done | bytes 3145760 | tf_op jit(solution)/shard_map/all_to_all | solution.py:880
  509.7 5.0 convert_reduce_fusion.2
  525.6 4.9 abs_reduce_fusion.2
  549.9 5.1 bitcast_select_fusion.3
  571.0 28.9 %collective-permute-done.28 = f16[4,2,584,384]{3,2,0,1:T(8,128)(2,1)S(1)} collective-permute-done((f16[4,2,584,384]{3,2,0,1:T(8,128)(2,1)}, f16[4,2,584,384]{3,2,0,1:T(8,128)(2,1)S(1)}, u32[]{:S(2)}, u32[]{:S(2)}) %collective-permute-start.28) | collective-permute-done | bytes 3588128 | tf_op jit(solution)/shard_map/ppermute | solution.py:72
  626.2 6.3 collective-permute-done.29
  640.7 10.0 abs_reduce_fusion.1
  658.7 7.7 abs_reduce_fusion
  688.4 8.1 collective-permute-start.37
  700.1 13.2 %collective-permute-done.37 = f16[584,384]{1,0:T(8,128)(2,1)S(1)} collective-permute-done((f16[584,384]{1,0:T(8,128)(2,1)S(1)}, f16[584,384]{1,0:T(8,128)(2,1)S(1)}, u32[]{:S(2)}, u32[]{:S(2)}) %collective-permute-start.37) | collective-permute-done | bytes 448544 | tf_op jit(solution)/shard_map/ppermute | solution.py:72
  714.5 17.3 %collective-permute-done.38 = f16[584,384]{1,0:T(8,128)(2,1)S(1)} collective-permute-done((f16[584,384]{1,0:T(8,128)(2,1)S(1)}, f16[584,384]{1,0:T(8,128)(2,1)S(1)}, u32[]{:S(2)}, u32[]{:S(2)}) %collective-permute-start.38) | collective-permute-done | bytes 448544 | tf_op jit(solution)/shard_map/ppermute | solution.py:72
  749.7 8.8 all-gather.3.cloned.1.call-done.part_ref
  758.5 20.3 %shard_map.435 = f32[3200,768]{1,0:T(8,128)} custom-call(s32[1,2048]{1,0:T(1,128)} %bitcast.659, bf16[2048,768]{1,0:T(8,128)(2,1)} %all-gather.3.cloned.1.call-done.part_ref, f32[3200,768]{1,0:T(8,128)} %shard_map.434.total_ref), custom_call_target="tpu_custom_call", output_to_operand_aliasing={{}: (2, {})} | custom-call | flops 10066329600 | bytes 22806528 | tf_op jit(solution)/shard_map/pallas_call | solution.py:704
  786.5 21.6 %all-to-all-start.5 = ((f32[16,160,48]{1,2,0:T(8,128)}), f32[16,160,48]{1,2,0:T(8,128)S(1)}, u32[]{:S(2)}, u32[]{:S(2)}) async-start(f32[16,160,48]{1,2,0:T(8,128)} %bitcast.583), calls=%async_computation.5 | async-start | bytes 1572864 | tf_op jit(solution)/shard_map/all_to_all | solution.py:910
  817.8 21.8 %collective-permute-start.36 = (f16[584,384]{1,0:T(8,128)(2,1)}, f16[584,384]{1,0:T(8,128)(2,1)}, u32[]{:S(2)}, u32[]{:S(2)}) collective-permute-start(f16[584,384]{1,0:T(8,128)(2,1)} %get-tuple-element.448), channel_id=1, source_target_pairs={{0,12},{1,13},{2,14},{3,15},{4,0},{5,1},{6,2},{7,3},{8,4},{9,5},{1... | collective-permute-start | bytes 1345544 | tf_op jit(solution)/shard_map/ppermute | solution.py:72
  852.6 23.3 %collective-permute-done.35 = f16[584,384]{1,0:T(8,128)(2,1)} collective-permute-done((f16[584,384]{1,0:T(8,128)(2,1)}, f16[584,384]{1,0:T(8,128)(2,1)}, u32[]{:S(2)}, u32[]{:S(2)}) %collective-permute-start.35) | collective-permute-done | bytes 448544 | tf_op jit(solution)/shard_map/ppermute | solution.py:72
  879.5 11.7 %slice_add_fusion = f32[3144,768]{1,0:T(8,128)} fusion(f32[3200,768]{1,0:T(8,128)} %collective-permute-done.40, f32[3200,768]{1,0:T(8,128)} %shard_map.435), kind=kLoop, calls=%fused_computation.5 | loop fusion | flops 2414592 | bytes 28975104 | tf_op jit(solution)/shard_map/add | solution.py:911
  912.2 12.6 %all_to_all.56 = f32[16,8,128]{2,1,0:T(8,128)S(1)} all-to-all(f32[16,8,128]{2,1,0:T(8,128)S(1)} %broadcast_in_dim_broadcast_in_dim_broadcast_in_dim.3), channel_id=1, replica_groups=mesh['section'=2,'za'=4,'yb'=2,'yc'=1,'xd'=2] {'za','yb','yc','xd'}, dimensions={0} | all-to-all | bytes 131072 | tf_op jit(solution)/shard_map/all_to_all | solution.py:47
  939.7 33.6 %all_to_all.58 = f16[8,104,768]{2,1,0:T(8,128)(2,1)S(1)} all-to-all(f16[8,104,768]{2,1,0:T(8,128)(2,1)S(1)} %bitcast.558), channel_id=1, replica_groups=mesh['section'=2,'za'=4,'yb'=2,'yc'=1,'xd'=2] {'za','yb'}, dimensions={0} | all-to-all | bytes 2555904 | tf_op jit(solution)/shard_map/all_to_all | solution.py:733
  989.3 15.6 %collective-permute-done.43 = f32[3,256,256]{2,1,0:T(8,128)} collective-permute-done((f32[3,256,256]{2,1,0:T(8,128)}, f32[3,256,256]{2,1,0:T(8,128)}, u32[]{:S(2)}, u32[]{:S(2)}) %collective-permute-start.43) | collective-permute-done | bytes 786464 | tf_op jit(solution)/shard_map/ppermute | solution.py:41
  1017.0 38.1 %shard_map.436 = f32[768,768]{1,0:T(8,128)S(1)} custom-call(f32[6,256,256]{2,1,0:T(8,128)S(1)} %maximum_select_fusion.1.gram_ref), custom_call_target="tpu_custom_call" | custom-call | flops 30802968576 | bytes 4718592 | tf_op jit(solution)/shard_map/pallas_call | solution.py:544
  1062.8 26.1 %fusion.172 = (bf16[3144,768]{1,0:T(8,128)(2,1)}, f32[3144,768]{1,0:T(8,128)}, f32[3144,768]{1,0:T(8,128)}, f32[3144,768]{1,0:T(8,128)}) fusion(f32[3144,768]{1,0:T(8,128)} %param.26, f32[3144,768]{1,0:T(8,128)} %slice_add_fusion, f32[]{:T(128)S(6)} %min.33, f32[3144,768]{1,0:T(8,128)} %param.27, f32[3144,768]{1,0:T(8,128)} %param.28), kind=kLoop, calls=%fused_computation.543 | loop fusion | flops 41048064 | bytes 72437760 | tf_op jit(solution)/shard_map/convert_element_type | solution.py:973
  (873 shorter events, 369.9 us)
Async XLA Ops:
  10.7 18.6 %collective-permute-start.5 = (bf16[576,384]{1,0:T(8,128)(2,1)S(1)}, bf16[576,384]{1,0:T(8,128)(2,1)S(1)}, u32[]{:S(2)}, u32[]{:S(2)}) collective-permute-start(bf16[576,384]{1,0:T(8,128)(2,1)S(1)} %constant_dynamic-slice_fusion.10), channel_id=1, source_target_pairs={{0,16},{16,0},{1,17},{17,1},{2,18},{18,2},{3,19},{19,3},{4,20},{20... | collective-permute-start | bytes 1327112 | tf_op jit(solution)/shard_map/ppermute | solution.py:41
  14.4 21.1 %all-to-all-start = ((bf16[16,171,48]{1,2,0:T(8,128)(2,1)}), bf16[16,171,48]{1,2,0:T(8,128)(2,1)S(1)}, u32[]{:S(2)}, u32[]{:S(2)}) async-start(bf16[16,171,48]{1,2,0:T(8,128)(2,1)} %broadcast_in_dim.220), calls=%async_computation | async-start | bytes 786432 | tf_op jit(solution)/shard_map/all_to_all | solution.py:47
  29.5 15.0 %collective-permute-start.8 = (bf16[576,384]{1,0:T(8,128)(2,1)S(1)}, bf16[576,384]{1,0:T(8,128)(2,1)S(1)}, u32[]{:S(2)}, u32[]{:S(2)}) collective-permute-start(bf16[576,384]{1,0:T(8,128)(2,1)S(1)} %get-tuple-element.463), channel_id=1, source_target_pairs={{0,4},{1,5},{2,6},{3,7},{4,8},{5,9},{6,10},{7,11},{8,12},{9,13},{1... | collective-permute-start | bytes 1327112 | tf_op jit(solution)/shard_map/ppermute | solution.py:72
  31.5 31.9 %collective-permute-start.7 = (bf16[576,384]{1,0:T(8,128)(2,1)S(1)}, bf16[576,384]{1,0:T(8,128)(2,1)S(1)}, u32[]{:S(2)}, u32[]{:S(2)}) collective-permute-start(bf16[576,384]{1,0:T(8,128)(2,1)S(1)} %get-tuple-element.463), channel_id=1, source_target_pairs={{0,8},{1,9},{2,10},{3,11},{4,12},{5,13},{6,14},{7,15},{8,0},{9,1},... | collective-permute-start | bytes 1327112 | tf_op jit(solution)/shard_map/ppermute | solution.py:72
  33.8 29.5 %collective-permute-start.6 = (bf16[576,384]{1,0:T(8,128)(2,1)S(1)}, bf16[576,384]{1,0:T(8,128)(2,1)S(1)}, u32[]{:S(2)}, u32[]{:S(2)}) collective-permute-start(bf16[576,384]{1,0:T(8,128)(2,1)S(1)} %get-tuple-element.463), channel_id=1, source_target_pairs={{0,12},{1,13},{2,14},{3,15},{4,0},{5,1},{6,2},{7,3},{8,4},{9,5},{1... | collective-permute-start | bytes 1327112 | tf_op jit(solution)/shard_map/ppermute | solution.py:72
  65.8 26.0 %collective-permute-start.9 = (bf16[4,576,384]{2,1,0:T(8,128)(2,1)}, bf16[4,576,384]{2,1,0:T(8,128)(2,1)S(1)}, u32[]{:S(2)}, u32[]{:S(2)}) collective-permute-start(bf16[4,576,384]{2,1,0:T(8,128)(2,1)} %maximum_add_fusion.1), channel_id=1, source_target_pairs={{0,1},{1,0},{2,3},{3,2},{4,5},{5,4},{6,7},{7,6},{8,9},{9,8},{10,11... | collective-permute-start | bytes 5308424 | tf_op jit(solution)/shard_map/ppermute | solution.py:72
  83.2 29.4 %collective-permute-start = (bf16[4,2,128,768]{3,2,0,1:T(8,128)(2,1)S(1)}, bf16[4,2,128,768]{3,2,0,1:T(8,128)(2,1)S(1)}, u32[]{:S(2)}, u32[]{:S(2)}) collective-permute-start(bf16[4,2,128,768]{3,2,0,1:T(8,128)(2,1)S(1)} %bitcast_select_fusion.4), channel_id=1, source_target_pairs={{0,2},{1,3},{2,0},{3,1},{4,6},{5,7},{6,4},{7,5},{8,10},{9,11},{10,... | collective-permute-start | bytes 4718600 | tf_op jit(solution)/shard_map/ppermute | solution.py:72
  93.9 71.8 %collective-permute-start.10 = (bf16[2,4,576,384]{3,2,1,0:T(8,128)(2,1)}, bf16[2,4,576,384]{3,2,1,0:T(8,128)(2,1)}, u32[]{:S(2)}, u32[]{:S(2)}) collective-permute-start(bf16[2,4,576,384]{3,2,1,0:T(8,128)(2,1)} %pad_maximum_fusion.7), channel_id=1, source_target_pairs={{0,2},{1,3},{2,0},{3,1},{4,6},{5,7},{6,4},{7,5},{8,10},{9,11},{10,... | collective-permute-start | bytes 10616840 | tf_op jit(solution)/shard_map/ppermute | solution.py:72
  100.4 22.2 %collective-permute-start.15 = (bf16[576,384]{1,0:T(8,128)(2,1)S(1)}, bf16[576,384]{1,0:T(8,128)(2,1)S(1)}, u32[]{:S(2)}, u32[]{:S(2)}) collective-permute-start(bf16[576,384]{1,0:T(8,128)(2,1)S(1)} %broadcast_add_fusion.3), channel_id=1, source_target_pairs={{0,4},{1,5},{2,6},{3,7},{4,8},{5,9},{6,10},{7,11},{8,12},{9,13},{1... | collective-permute-start | bytes 1327112 | tf_op jit(solution)/shard_map/ppermute | solution.py:72
  109.9 25.5 %collective-permute-start.14 = (bf16[576,384]{1,0:T(8,128)(2,1)S(1)}, bf16[576,384]{1,0:T(8,128)(2,1)S(1)}, u32[]{:S(2)}, u32[]{:S(2)}) collective-permute-start(bf16[576,384]{1,0:T(8,128)(2,1)S(1)} %broadcast_add_fusion.3), channel_id=1, source_target_pairs={{0,8},{1,9},{2,10},{3,11},{4,12},{5,13},{6,14},{7,15},{8,0},{9,1},... | collective-permute-start | bytes 1327112 | tf_op jit(solution)/shard_map/ppermute | solution.py:72
  112.0 23.4 %collective-permute-start.13 = (bf16[576,384]{1,0:T(8,128)(2,1)S(1)}, bf16[576,384]{1,0:T(8,128)(2,1)S(1)}, u32[]{:S(2)}, u32[]{:S(2)}) collective-permute-start(bf16[576,384]{1,0:T(8,128)(2,1)S(1)} %broadcast_add_fusion.3), channel_id=1, source_target_pairs={{0,12},{1,13},{2,14},{3,15},{4,0},{5,1},{6,2},{7,3},{8,4},{9,5},{1... | collective-permute-start | bytes 1327112 | tf_op jit(solution)/shard_map/ppermute | solution.py:72
  135.7 26.5 %collective-permute-start.16 = (bf16[4,576,384]{2,1,0:T(8,128)(2,1)S(1)}, bf16[4,576,384]{2,1,0:T(8,128)(2,1)S(1)}, u32[]{:S(2)}, u32[]{:S(2)}) collective-permute-start(bf16[4,576,384]{2,1,0:T(8,128)(2,1)S(1)} %maximum_add_fusion.3), channel_id=1, source_target_pairs={{0,1},{1,0},{2,3},{3,2},{4,5},{5,4},{6,7},{7,6},{8,9},{9,8},{10,11... | collective-permute-start | bytes 5308424 | tf_op jit(solution)/shard_map/ppermute | solution.py:72
  164.4 54.9 %collective-permute-start.17 = (bf16[2,4,576,384]{3,2,1,0:T(8,128)(2,1)}, bf16[2,4,576,384]{3,2,1,0:T(8,128)(2,1)}, u32[]{:S(2)}, u32[]{:S(2)}) collective-permute-start(bf16[2,4,576,384]{3,2,1,0:T(8,128)(2,1)} %pad_maximum_fusion.8), channel_id=1, source_target_pairs={{0,2},{1,3},{2,0},{3,1},{4,6},{5,7},{6,4},{7,5},{8,10},{9,11},{10,... | collective-permute-start | bytes 10616840 | tf_op jit(solution)/shard_map/ppermute | solution.py:72
  165.7 54.1 %collective-permute-start.11 = (bf16[2,4,576,384]{3,2,1,0:T(8,128)(2,1)}, bf16[2,4,576,384]{3,2,1,0:T(8,128)(2,1)}, u32[]{:S(2)}, u32[]{:S(2)}) collective-permute-start(bf16[2,4,576,384]{3,2,1,0:T(8,128)(2,1)} %pad_maximum_fusion.7), channel_id=1, source_target_pairs={{0,16},{16,0},{1,17},{17,1},{2,18},{18,2},{3,19},{19,3},{4,20},{20... | collective-permute-start | bytes 10616840 | tf_op jit(solution)/shard_map/ppermute | solution.py:41
  165.7 54.1 %collective-permute-start.12 = (bf16[2,4,576,384]{3,2,1,0:T(8,128)(2,1)}, bf16[2,4,576,384]{3,2,1,0:T(8,128)(2,1)}, u32[]{:S(2)}, u32[]{:S(2)}) collective-permute-start(bf16[2,4,576,384]{3,2,1,0:T(8,128)(2,1)} %collective-permute-done.10), channel_id=1, source_target_pairs={{0,16},{16,0},{1,17},{17,1},{2,18},{18,2},{3,19},{19,3},{4,20},{20... | collective-permute-start | bytes 10616840 | tf_op jit(solution)/shard_map/ppermute | solution.py:41
  167.2 20.8 %collective-permute-start.1 = (bf16[4,128,768]{2,1,0:T(8,128)(2,1)}, bf16[4,128,768]{2,1,0:T(8,128)(2,1)}, u32[]{:S(2)}, u32[]{:S(2)}) collective-permute-start(bf16[4,128,768]{2,1,0:T(8,128)(2,1)} %dynamic-slice_bitcast_fusion.4), channel_id=1, source_target_pairs={{0,1},{1,0},{2,3},{3,2},{4,5},{5,4},{6,7},{7,6},{8,9},{9,8},{10,11... | collective-permute-start | bytes 2359304 | tf_op jit(solution)/shard_map/ppermute | solution.py:72
  189.3 16.1 %collective-permute-start.4 = (bf16[128,768]{1,0:T(8,128)(2,1)S(1)}, bf16[128,768]{1,0:T(8,128)(2,1)S(1)}, u32[]{:S(2)}, u32[]{:S(2)}) collective-permute-start(bf16[128,768]{1,0:T(8,128)(2,1)S(1)} %get-tuple-element.467), channel_id=1, source_target_pairs={{0,12},{1,13},{2,14},{3,15},{4,0},{5,1},{6,2},{7,3},{8,4},{9,5},{1... | collective-permute-start | bytes 589832 | tf_op jit(solution)/shard_map/ppermute | solution.py:72
  200.0 17.0 %collective-permute-start.3 = (bf16[128,768]{1,0:T(8,128)(2,1)S(1)}, bf16[128,768]{1,0:T(8,128)(2,1)S(1)}, u32[]{:S(2)}, u32[]{:S(2)}) collective-permute-start(bf16[128,768]{1,0:T(8,128)(2,1)S(1)} %get-tuple-element.468), channel_id=1, source_target_pairs={{0,8},{1,9},{2,10},{3,11},{4,12},{5,13},{6,14},{7,15},{8,0},{9,1},... | collective-permute-start | bytes 589832 | tf_op jit(solution)/shard_map/ppermute | solution.py:72
  205.4 13.2 %collective-permute-start.2 = (bf16[128,768]{1,0:T(8,128)(2,1)S(1)}, bf16[128,768]{1,0:T(8,128)(2,1)S(1)}, u32[]{:S(2)}, u32[]{:S(2)}) collective-permute-start(bf16[128,768]{1,0:T(8,128)(2,1)S(1)} %get-tuple-element.466), channel_id=1, source_target_pairs={{0,4},{1,5},{2,6},{3,7},{4,8},{5,9},{6,10},{7,11},{8,12},{9,13},{1... | collective-permute-start | bytes 589832 | tf_op jit(solution)/shard_map/ppermute | solution.py:72
  219.2 28.7 %collective-permute-start.18 = (bf16[2,4,576,384]{3,2,1,0:T(8,128)(2,1)}, bf16[2,4,576,384]{3,2,1,0:T(8,128)(2,1)}, u32[]{:S(2)}, u32[]{:S(2)}) collective-permute-start(bf16[2,4,576,384]{3,2,1,0:T(8,128)(2,1)} %pad_maximum_fusion.8), channel_id=1, source_target_pairs={{0,16},{16,0},{1,17},{17,1},{2,18},{18,2},{3,19},{19,3},{4,20},{20... | collective-permute-start | bytes 10616840 | tf_op jit(solution)/shard_map/ppermute | solution.py:41
  219.3 28.6 %collective-permute-start.19 = (bf16[2,4,576,384]{3,2,1,0:T(8,128)(2,1)}, bf16[2,4,576,384]{3,2,1,0:T(8,128)(2,1)}, u32[]{:S(2)}, u32[]{:S(2)}) collective-permute-start(bf16[2,4,576,384]{3,2,1,0:T(8,128)(2,1)} %collective-permute-done.17), channel_id=1, source_target_pairs={{0,16},{16,0},{1,17},{17,1},{2,18},{18,2},{3,19},{19,3},{4,20},{20... | collective-permute-start | bytes 10616840 | tf_op jit(solution)/shard_map/ppermute | solution.py:41
  276.1 11.3 %collective-permute-start.22 = (bf16[128,768]{1,0:T(8,128)(2,1)S(1)}, bf16[128,768]{1,0:T(8,128)(2,1)S(1)}, u32[]{:S(2)}, u32[]{:S(2)}) collective-permute-start(bf16[128,768]{1,0:T(8,128)(2,1)S(1)} %add_convert_fusion.1), channel_id=1, source_target_pairs={{0,4},{1,5},{2,6},{3,7},{4,8},{5,9},{6,10},{7,11},{8,12},{9,13},{1... | collective-permute-start | bytes 589832 | tf_op jit(solution)/shard_map/ppermute | solution.py:72
  280.5 15.1 %collective-permute-start.21 = (bf16[128,768]{1,0:T(8,128)(2,1)S(1)}, bf16[128,768]{1,0:T(8,128)(2,1)S(1)}, u32[]{:S(2)}, u32[]{:S(2)}) collective-permute-start(bf16[128,768]{1,0:T(8,128)(2,1)S(1)} %add_convert_fusion.1), channel_id=1, source_target_pairs={{0,8},{1,9},{2,10},{3,11},{4,12},{5,13},{6,14},{7,15},{8,0},{9,1},... | collective-permute-start | bytes 589832 | tf_op jit(solution)/shard_map/ppermute | solution.py:72
  282.1 13.5 %collective-permute-start.20 = (bf16[128,768]{1,0:T(8,128)(2,1)S(1)}, bf16[128,768]{1,0:T(8,128)(2,1)S(1)}, u32[]{:S(2)}, u32[]{:S(2)}) collective-permute-start(bf16[128,768]{1,0:T(8,128)(2,1)S(1)} %add_convert_fusion.1), channel_id=1, source_target_pairs={{0,12},{1,13},{2,14},{3,15},{4,0},{5,1},{6,2},{7,3},{8,4},{9,5},{1... | collective-permute-start | bytes 589832 | tf_op jit(solution)/shard_map/ppermute | solution.py:72
  295.8 12.1 %collective-permute-start.23 = (bf16[4,128,768]{2,1,0:T(8,128)(2,1)S(1)}, bf16[4,128,768]{2,1,0:T(8,128)(2,1)S(1)}, u32[]{:S(2)}, u32[]{:S(2)}) collective-permute-start(bf16[4,128,768]{2,1,0:T(8,128)(2,1)S(1)} %get-tuple-element.465), channel_id=1, source_target_pairs={{0,1},{1,0},{2,3},{3,2},{4,5},{5,4},{6,7},{7,6},{8,9},{9,8},{10,11... | collective-permute-start | bytes 2359304 | tf_op jit(solution)/shard_map/ppermute | solution.py:72
  310.0 20.8 %collective-permute-start.24 = (bf16[2,4,128,768]{3,2,1,0:T(8,128)(2,1)}, bf16[2,4,128,768]{3,2,1,0:T(8,128)(2,1)}, u32[]{:S(2)}, u32[]{:S(2)}) collective-permute-start(bf16[2,4,128,768]{3,2,1,0:T(8,128)(2,1)} %pad_maximum_fusion.14), channel_id=1, source_target_pairs={{0,2},{1,3},{2,0},{3,1},{4,6},{5,7},{6,4},{7,5},{8,10},{9,11},{10,... | collective-permute-start | bytes 4718600 | tf_op jit(solution)/shard_map/ppermute | solution.py:72
  371.9 24.0 %all-to-all-start.1 = ((f32[16,3,2048]{2,1,0:T(4,128)}), f32[16,3,2048]{2,1,0:T(4,128)S(1)}, u32[]{:S(2)}, u32[]{:S(2)}) async-start(f32[16,3,2048]{2,1,0:T(4,128)} %broadcast_in_dim.237), calls=%async_computation.1 | async-start | bytes 1048576 | tf_op jit(solution)/shard_map/all_to_all | solution.py:47
  395.9 34.0 %all-to-all-start.3 = ((f16[8,104,768]{2,1,0:T(8,128)(2,1)}), f16[8,104,768]{2,1,0:T(8,128)(2,1)}, u32[]{:S(2)}, u32[]{:S(2)}) async-start(f16[8,104,768]{2,1,0:T(8,128)(2,1)} %bitcast.557), calls=%async_computation.3 | async-start | bytes 2555904 | tf_op jit(solution)/shard_map/all_to_all | solution.py:733
  439.1 65.3 %all-to-all-start.4 = ((bf16[16,128,768]{2,1,0:T(8,128)(2,1)}), bf16[16,128,768]{2,1,0:T(8,128)(2,1)}, u32[]{:S(2)}, u32[]{:S(2)}) async-start(bf16[16,128,768]{2,1,0:T(8,128)(2,1)} %bitcast.537), calls=%async_computation.4 | async-start | bytes 6291456 | tf_op jit(solution)/shard_map/all_to_all | solution.py:880
  443.7 314.8 %all-gather.3.cloned.1.call-start = ((), (), s32[]{:S(2)}) async-start(), calls=%async_computation.11 | async-start | bytes 3342336 | tf_op jit(solution)/shard_map/all_gather | solution.py:903
  445.4 80.2 %collective-permute-start.26 = (bf16[128,5376]{1,0:T(8,128)(2,1)}, bf16[128,5376]{1,0:T(8,128)(2,1)}, u32[]{:S(2)}, u32[]{:S(2)}) collective-permute-start(bf16[128,5376]{1,0:T(8,128)(2,1)} %pad_maximum_fusion.15), channel_id=1, source_target_pairs={{0,16},{16,0},{1,17},{17,1},{2,18},{18,2},{3,19},{19,3},{4,20},{20... | collective-permute-start | bytes 4128776 | tf_op jit(solution)/shard_map/ppermute | solution.py:41
  523.2 11.0 collective-permute-start.25
  555.0 44.9 %collective-permute-start.28 = (f16[4,2,584,384]{3,2,0,1:T(8,128)(2,1)}, f16[4,2,584,384]{3,2,0,1:T(8,128)(2,1)S(1)}, u32[]{:S(2)}, u32[]{:S(2)}) collective-permute-start(f16[4,2,584,384]{3,2,0,1:T(8,128)(2,1)} %bitcast_select_fusion.3), channel_id=1, source_target_pairs={{0,2},{1,3},{2,0},{3,1},{4,6},{5,7},{6,4},{7,5},{8,10},{9,11},{10,... | collective-permute-start | bytes 10764296 | tf_op jit(solution)/shard_map/ppermute | solution.py:72
  560.9 79.7 %collective-permute-start.31 = (bf16[128,5376]{1,0:T(8,128)(2,1)}, bf16[128,5376]{1,0:T(8,128)(2,1)}, u32[]{:S(2)}, u32[]{:S(2)}) collective-permute-start(bf16[128,5376]{1,0:T(8,128)(2,1)} %pad_maximum_fusion.16), channel_id=1, source_target_pairs={{0,16},{16,0},{1,17},{17,1},{2,18},{18,2},{3,19},{19,3},{4,20},{20... | collective-permute-start | bytes 4128776 | tf_op jit(solution)/shard_map/ppermute | solution.py:41
  609.5 23.1 %collective-permute-start.29 = (f16[4,584,384]{2,1,0:T(8,128)(2,1)}, f16[4,584,384]{2,1,0:T(8,128)(2,1)}, u32[]{:S(2)}, u32[]{:S(2)}) collective-permute-start(f16[4,584,384]{2,1,0:T(8,128)(2,1)} %get-tuple-element.424), channel_id=1, source_target_pairs={{0,1},{1,0},{2,3},{3,2},{4,5},{5,4},{6,7},{7,6},{8,9},{9,8},{10,11... | collective-permute-start | bytes 5382152 | tf_op jit(solution)/shard_map/ppermute | solution.py:72
  640.5 18.1 %collective-permute-start.30 = (bf16[128,6912]{1,0:T(8,128)(2,1)}, bf16[128,6912]{1,0:T(8,128)(2,1)}, u32[]{:S(2)}, u32[]{:S(2)}) collective-permute-start(bf16[128,6912]{1,0:T(8,128)(2,1)} %pad_maximum_fusion.13), channel_id=1, source_target_pairs={{0,16},{16,0},{1,17},{17,1},{2,18},{18,2},{3,19},{19,3},{4,20},{20... | collective-permute-start | bytes 5308424 | tf_op jit(solution)/shard_map/ppermute | solution.py:41
  685.9 52.5 %collective-permute-start.32 = (f16[4,2,584,384]{3,2,0,1:T(8,128)(2,1)S(1)}, f16[4,2,584,384]{3,2,0,1:T(8,128)(2,1)S(1)}, u32[]{:S(2)}, u32[]{:S(2)}) collective-permute-start(f16[4,2,584,384]{3,2,0,1:T(8,128)(2,1)S(1)} %bitcast_select_fusion), channel_id=1, source_target_pairs={{0,2},{1,3},{2,0},{3,1},{4,6},{5,7},{6,4},{7,5},{8,10},{9,11},{10,... | collective-permute-start | bytes 10764296 | tf_op jit(solution)/shard_map/ppermute | solution.py:72
  688.4 24.9 %collective-permute-start.37 = (f16[584,384]{1,0:T(8,128)(2,1)S(1)}, f16[584,384]{1,0:T(8,128)(2,1)S(1)}, u32[]{:S(2)}, u32[]{:S(2)}) collective-permute-start(f16[584,384]{1,0:T(8,128)(2,1)S(1)} %get-tuple-element.454), channel_id=1, source_target_pairs={{0,4},{1,5},{2,6},{3,7},{4,8},{5,9},{6,10},{7,11},{8,12},{9,13},{1... | collective-permute-start | bytes 1345544 | tf_op jit(solution)/shard_map/ppermute | solution.py:72
  696.5 35.3 %collective-permute-start.38 = (f16[584,384]{1,0:T(8,128)(2,1)S(1)}, f16[584,384]{1,0:T(8,128)(2,1)S(1)}, u32[]{:S(2)}, u32[]{:S(2)}) collective-permute-start(f16[584,384]{1,0:T(8,128)(2,1)S(1)} %get-tuple-element.453), channel_id=1, source_target_pairs={{0,8},{1,9},{2,10},{3,11},{4,12},{5,13},{6,14},{7,15},{8,0},{9,1},... | collective-permute-start | bytes 1345544 | tf_op jit(solution)/shard_map/ppermute | solution.py:72
  697.4 35.6 %collective-permute-start.39 = (f16[584,384]{1,0:T(8,128)(2,1)S(1)}, f16[584,384]{1,0:T(8,128)(2,1)S(1)}, u32[]{:S(2)}, u32[]{:S(2)}) collective-permute-start(f16[584,384]{1,0:T(8,128)(2,1)S(1)} %get-tuple-element.452), channel_id=1, source_target_pairs={{0,12},{1,13},{2,14},{3,15},{4,0},{5,1},{6,2},{7,3},{8,4},{9,5},{1... | collective-permute-start | bytes 1345544 | tf_op jit(solution)/shard_map/ppermute | solution.py:72
  779.0 100.5 %collective-permute-start.40 = (f32[3200,768]{1,0:T(8,128)}, f32[3200,768]{1,0:T(8,128)}, u32[]{:S(2)}, u32[]{:S(2)}) collective-permute-start(f32[3200,768]{1,0:T(8,128)} %shard_map.435), channel_id=1, source_target_pairs={{0,16},{16,0},{1,17},{17,1},{2,18},{18,2},{3,19},{19,3},{4,20},{20... | collective-permute-start | bytes 29491208 | tf_op jit(solution)/shard_map/ppermute | solution.py:41
  781.8 28.2 %collective-permute-start.33 = (f16[4,584,384]{2,1,0:T(8,128)(2,1)}, f16[4,584,384]{2,1,0:T(8,128)(2,1)}, u32[]{:S(2)}, u32[]{:S(2)}) collective-permute-start(f16[4,584,384]{2,1,0:T(8,128)(2,1)} %get-tuple-element.422), channel_id=1, source_target_pairs={{0,1},{1,0},{2,3},{3,2},{4,5},{5,4},{6,7},{7,6},{8,9},{9,8},{10,11... | collective-permute-start | bytes 5382152 | tf_op jit(solution)/shard_map/ppermute | solution.py:72
  786.5 53.7 %all-to-all-start.5 = ((f32[16,160,48]{1,2,0:T(8,128)}), f32[16,160,48]{1,2,0:T(8,128)S(1)}, u32[]{:S(2)}, u32[]{:S(2)}) async-start(f32[16,160,48]{1,2,0:T(8,128)} %bitcast.583), calls=%async_computation.5 | async-start | bytes 1572864 | tf_op jit(solution)/shard_map/all_to_all | solution.py:910
  817.8 32.9 %collective-permute-start.36 = (f16[584,384]{1,0:T(8,128)(2,1)}, f16[584,384]{1,0:T(8,128)(2,1)}, u32[]{:S(2)}, u32[]{:S(2)}) collective-permute-start(f16[584,384]{1,0:T(8,128)(2,1)} %get-tuple-element.448), channel_id=1, source_target_pairs={{0,12},{1,13},{2,14},{3,15},{4,0},{5,1},{6,2},{7,3},{8,4},{9,5},{1... | collective-permute-start | bytes 1345544 | tf_op jit(solution)/shard_map/ppermute | solution.py:72
  839.6 36.2 %collective-permute-start.35 = (f16[584,384]{1,0:T(8,128)(2,1)}, f16[584,384]{1,0:T(8,128)(2,1)}, u32[]{:S(2)}, u32[]{:S(2)}) collective-permute-start(f16[584,384]{1,0:T(8,128)(2,1)} %get-tuple-element.449), channel_id=1, source_target_pairs={{0,8},{1,9},{2,10},{3,11},{4,12},{5,13},{6,14},{7,15},{8,0},{9,1},... | collective-permute-start | bytes 1345544 | tf_op jit(solution)/shard_map/ppermute | solution.py:72
  839.6 38.1 %collective-permute-start.34 = (f16[584,384]{1,0:T(8,128)(2,1)}, f16[584,384]{1,0:T(8,128)(2,1)}, u32[]{:S(2)}, u32[]{:S(2)}) collective-permute-start(f16[584,384]{1,0:T(8,128)(2,1)} %get-tuple-element.450), channel_id=1, source_target_pairs={{0,4},{1,5},{2,6},{3,7},{4,8},{5,9},{6,10},{7,11},{8,12},{9,13},{1... | collective-permute-start | bytes 1345544 | tf_op jit(solution)/shard_map/ppermute | solution.py:72
  984.9 20.0 %collective-permute-start.43 = (f32[3,256,256]{2,1,0:T(8,128)}, f32[3,256,256]{2,1,0:T(8,128)}, u32[]{:S(2)}, u32[]{:S(2)}) collective-permute-start(f32[3,256,256]{2,1,0:T(8,128)} %select_add_fusion), channel_id=1, source_target_pairs={{0,1},{1,0},{2,3},{3,2},{4,5},{5,4},{6,7},{7,6},{8,9},{9,8},{10,11... | collective-permute-start | bytes 2359304 | tf_op jit(solution)/shard_map/ppermute | solution.py:41
  1059.2 33.0 %all-to-all-start.9 = ((f16[8,96,768]{2,1,0:T(8,128)(2,1)}), f16[8,96,768]{2,1,0:T(8,128)(2,1)S(1)}, u32[]{:S(2)}, u32[]{:S(2)}) async-start(f16[8,96,768]{2,1,0:T(8,128)(2,1)} %bitcast.206), calls=%async_computation.9 | async-start | bytes 2359296 | tf_op jit(solution)/shard_map/all_to_all | solution.py:744
  (212 other events, 2610.8 us)
Sparse Core Ops, SparseCore 0:
  658.8 99.7 all-gather.2

commit v3 on v2

--- a/solution.py
+++ b/solution.py
@@ -901,19 +901,20 @@
             nothing = nothing_of(column_late).astype(jnp.bfloat16)
         vecs_parts = d_vectors + vecs_parts
     emb_all = lax.all_gather(grad_now.astype(jnp.bfloat16), FSDP, axis=0, tiled=True)
-    late_ids = local_ids.reshape(-1) + nothing_of(planes_part[0], *parts_late).astype(
-        jnp.int32
-    )
-    table_grad = rows_scattered(table_grad, late_ids, emb_all)
     small_grad = lax.optimization_barrier(padded_rows(vecs_parts + [d_fgain, d_fbias, grad_now]))
     small_grad = jnp.moveaxis(small_grad.reshape(small_rows, fsdp_count, -1), 1, 0)
     small_grad = jnp.sum(lax.all_to_all(small_grad, FSDP, 0, 0, tiled=True), 0)
+    column_early = plane_reduced(planes_part[0], added)
+    parts_early = column_parts(column_early)
+    late_ids = local_ids.reshape(-1) + nothing_of(column_early, small_grad, *parts_late).astype(
+        jnp.int32
+    )
+    table_grad = rows_scattered(table_grad, late_ids, emb_all)
     table_grad = (table_grad + swapped(table_grad, "section"))[:shard_rows]
     own_rows = shard_rows // section_count
     table_part = lax.dynamic_slice_in_dim(table_grad, section_index * own_rows, own_rows, 0)
     table_squares = jnp.sum(table_part * table_part)
-    parts_early = column_parts(plane_reduced(planes_part[0], added))
-    flushed = summed_weights(parts_early, parts_late, table_squares, small_grad)
+    flushed = summed_weights(parts_early, parts_late, table_squares)
     loss_row = jnp.broadcast_to(loss_part, (1, small_grad.shape[1]))
     small_grad = jnp.concatenate([small_grad, loss_row], 0)
     small_grad = small_grad + swapped(small_grad, "section")

time: 1120 us -> 1140 us (1.018)
  waiting for transfers between devices: 302 us -> 342 us
  starting transfers between devices: 154 us -> 129 us
    ppermute x30, waiting for transfers between devices: 228 us -> 257 us  [moved(): return lax.ppermute(block, ('section',) + FSDP, route(level, distance))]
    all_to_all x1, waiting for transfers between devices: 0.01 us -> 20 us  [shards(): small_grad = jnp.sum(lax.all_to_all(small_grad, FSDP, 0, 0, tiled=True), 0)]
    ppermute x30, starting transfers between devices: 99.9 us -> 84.6 us  [moved(): return lax.ppermute(block, ('section',) + FSDP, route(level, distance))]
    unnamed x440 -> x422, local copies, waits for them, and re-layouts: 33.9 us -> 30.9 us
  transfers between devices with their start and end apart: 52 -> 52, of which waited for: 29 -> 30; matrix products, arithmetic and copies ran while one was open for 23% -> 20% of each run, Pallas kernels for 6% -> 6%
where the time goes in v3:
time: 1140 us; the launch traced here: 1130 us
  waiting for transfers between devices  342 us (30%)
  other arithmetic  182 us (16%)
  Pallas kernels  162 us (14%)
  local copies, waits for them, and re-layouts  132 us (12%)
  starting transfers between devices  129 us (11%)
  matrix products  65.7 us (6%)
  blocking collectives  64.7 us (6%)
  between operations  50.6 us (4%)
    ppermute x30, waiting for transfers between devices, moved(): return lax.ppermute(block, ('section',) + FSDP, route(level, distance))  257 us
    ppermute x30, starting transfers between devices, moved(): return lax.ppermute(block, ('section',) + FSDP, route(level, distance))  84.6 us
    pallas_call x1, Pallas kernels, newton_product(): pl.pallas_call(newton_kernel, out_shape=jax.ShapeDtypeStruct(square, jnp....  38.1 us
    all_to_all x1, blocking collectives, to_spots(): return (lax.all_to_all(sent, SPOTS, 0, 0, tiled=True), sent)  33.6 us
    unnamed x422, local copies, waits for them, and re-layouts  30.9 us
    all_to_all x1, waiting for transfers between devices, shards(): lax.all_to_all(grad_rows.astype(jnp.bfloat16).reshape(fsdp_count, -1, mod...  29.6 us
    pallas_call x2, Pallas kernels, assembled(): pl.pallas_call(functools.partial(assemble_kernel, tuple(widths), count),...  28.9 us
    dot_general x8, matrix products, contract_cols(): lax.dot_general(left_mat, right_mat, (((1,), (1,)), ((), ())), preferred_...  27.1 us
  transfers between devices with their start and end apart: 52, of which 30 were waited for; matrix products, arithmetic and copies ran while one was open for 20% of the time, Pallas kernels for 6%

profile of v3, /device:TPU:0, one launch (start us, length us, event | category | flops | bytes accessed | tf_op | source)
XLA Modules:
  0.0 1128.1 jit_solution(12894589853368716414)
XLA Ops:
  14.4 8.1 all-to-all-start
  37.4 7.1 collective-permute-done.8
  44.6 18.8 %collective-permute-done.7 = bf16[576,384]{1,0:T(8,128)(2,1)S(1)} collective-permute-done((bf16[576,384]{1,0:T(8,128)(2,1)S(1)}, bf16[576,384]{1,0:T(8,128)(2,1)S(1)}, u32[]{:S(2)}, u32[]{:S(2)}) %collective-permute-start.7) | collective-permute-done | bytes 442400 | tf_op jit(solution)/shard_map/ppermute | solution.py:72
  67.2 13.1 %gather_fusion = bf16[2048,768]{1,0:T(8,128)(2,1)} fusion(bf16[3200,768]{1,0:T(8,128)(2,1)} %pad.32.table_ref, s32[2048]{0:T(1024)S(1)} %bitcast_clamp_fusion), kind=kCustom, calls=%fused_computation | custom fusion | bytes 6299648 | tf_op jit(solution)/shard_map/jit(_take)/gather | solution.py:818
  85.0 6.7 collective-permute-done.9
  100.4 9.5 collective-permute-start.15
  113.9 8.6 collective-permute-done.15
  122.6 12.8 %collective-permute-done.14 = bf16[576,384]{1,0:T(8,128)(2,1)S(1)} collective-permute-done((bf16[576,384]{1,0:T(8,128)(2,1)S(1)}, bf16[576,384]{1,0:T(8,128)(2,1)S(1)}, u32[]{:S(2)}, u32[]{:S(2)}) %collective-permute-start.14) | collective-permute-done | bytes 442400 | tf_op jit(solution)/shard_map/ppermute | solution.py:72
  136.4 25.8 %collective-permute-done.16 = bf16[4,576,384]{2,1,0:T(8,128)(2,1)S(1)} collective-permute-done((bf16[4,576,384]{2,1,0:T(8,128)(2,1)S(1)}, bf16[4,576,384]{2,1,0:T(8,128)(2,1)S(1)}, u32[]{:S(2)}, u32[]{:S(2)}) %collective-permute-start.16) | collective-permute-done | bytes 1769504 | tf_op jit(solution)/shard_map/ppermute | solution.py:72
  177.2 10.8 collective-permute-done.1
  189.3 10.8 collective-permute-start.4
  200.5 4.9 collective-permute-done.4
  205.4 10.1 collective-permute-start.2
  219.8 14.4 %shard_map.430 = (bf16[2304,768]{1,0:T(8,128)(2,1)}, bf16[768,768]{1,0:T(8,128)(2,1)}, bf16[3072,768]{1,0:T(8,128)(2,1)}, bf16[3072,768]{1,0:T(8,128)(2,1)}) custom-call(s32[34]{0:T(128)} %pad_add_fusion.1.spot_ref, bf16[8,576,384]{2,1,0:T(8,128)(2,1)} %bitcast.38.refs_0_, bf16[8,576,384]{2,1,0:T(8,128)(2,1)} %bitcast.39.refs_1_, ...), custom_call_target="tpu_custom_call" | custom-call | bytes 28311552 | tf_op jit(solution)/shard_map/pallas_call | solution.py:150
  241.2 5.4 multiply_convert_fusion.5
  247.9 14.5 %shard_map.431 = (bf16[2304,768]{1,0:T(8,128)(2,1)}, bf16[768,768]{1,0:T(8,128)(2,1)}, bf16[3072,768]{1,0:T(8,128)(2,1)}, bf16[3072,768]{1,0:T(8,128)(2,1)}) custom-call(s32[34]{0:T(128)} %pad_add_fusion.1.spot_ref, bf16[8,576,384]{2,1,0:T(8,128)(2,1)} %bitcast.62.refs_0_, bf16[8,576,384]{2,1,0:T(8,128)(2,1)} %bitcast.63.refs_1_, ...), custom_call_target="tpu_custom_call" | custom-call | bytes 28311552 | tf_op jit(solution)/shard_map/pallas_call | solution.py:150
  269.4 5.4 multiply_convert_fusion.4
  287.5 8.2 collective-permute-done.21
  297.3 10.6 collective-permute-done.23
  316.1 14.8 %collective-permute-done.24 = bf16[2,4,128,768]{3,2,1,0:T(8,128)(2,1)} collective-permute-done((bf16[2,4,128,768]{3,2,1,0:T(8,128)(2,1)}, bf16[2,4,128,768]{3,2,1,0:T(8,128)(2,1)}, u32[]{:S(2)}, u32[]{:S(2)}) %collective-permute-start.24) | collective-permute-done | bytes 1572896 | tf_op jit(solution)/shard_map/ppermute | solution.py:72
  334.2 22.1 %shard_map.432 = (bf16[2048,3200]{1,0:T(8,128)(2,1)}, f32[2048,128]{1,0:T(8,128)}, bf16[2048,768]{1,0:T(8,128)(2,1)}) custom-call(s32[16]{0:T(128)} %copy-done.172, bf16[16,128,768]{2,1,0:T(8,128)(2,1)} %bitcast.581, bf16[16,128,768]{2,1,0:T(8,128)(2,1)} %bitcast.582, bf16[3200,768]{1,0:T(8,128)(2,1)} %pad.32.table_ref, s32[2048,1]{1,0:T(8,128)} %and_select_fusion.target_ref), custom_call_target="tpu_custom_call" | custom-call | flops 10066329600 | bytes 21168128 | tf_op jit(solution)/shard_map/pallas_call | solution.py:585
  365.5 5.6 all_to_all.55
  372.0 8.6 all-to-all-start.1
  385.4 10.5 all-to-all-done.1
  400.2 26.8 %shard_map.433 = (bf16[2048,768]{1,0:T(8,128)(2,1)}, bf16[2048,768]{1,0:T(8,128)(2,1)}) custom-call(bf16[2048,3200]{1,0:T(8,128)(2,1)} %get-tuple-element.49.exp_ref, s32[2048,1]{1,0:T(8,128)} %and_select_fusion.target_ref, bf16[3200,768]{1,0:T(8,128)(2,1)} %pad.32.table_ref), custom_call_target="tpu_custom_call" | custom-call | flops 20132659200 | bytes 27459584 | tf_op jit(solution)/shard_map/pallas_call | solution.py:628
  446.9 26.1 %shard_map.434.total_ref = f32[3200,768]{1,0:T(8,128)} custom-call(bf16[2048,3200]{1,0:T(8,128)(2,1)} %get-tuple-element.49.exp_ref, f32[2048,2]{1,0:T(8,128)} %copy.670.token_ref, s32[2048,1]{1,0:T(8,128)} %and_select_fusion.target_ref, bf16[2048,768]{1,0:T(8,128)(2,1)} %get-tuple-element.52.row_ref), custom_call_target="tpu_custom_call" | custom-call | flops 10066329600 | bytes 26083328 | tf_op jit(solution)/shard_map/pallas_call | solution.py:670
  474.9 29.6 %all-to-all-done.4 = bf16[16,128,768]{2,1,0:T(8,128)(2,1)} async-done(((bf16[16,128,768]{2,1,0:T(8,128)(2,1)}), bf16[16,128,768]{2,1,0:T(8,128)(2,1)}, u32[]{:S(2)}, u32[]{:S(2)}) %all-to-all-start.4) | async-done | bytes 3145760 | tf_op jit(solution)/shard_map/all_to_all | solution.py:880
  509.8 5.0 convert_reduce_fusion.2
  525.7 4.9 abs_reduce_fusion.2
  550.0 5.1 bitcast_select_fusion.3
  573.3 26.7 %collective-permute-done.28 = f16[4,2,584,384]{3,2,0,1:T(8,128)(2,1)S(1)} collective-permute-done((f16[4,2,584,384]{3,2,0,1:T(8,128)(2,1)}, f16[4,2,584,384]{3,2,0,1:T(8,128)(2,1)S(1)}, u32[]{:S(2)}, u32[]{:S(2)}) %collective-permute-start.28) | collective-permute-done | bytes 3588128 | tf_op jit(solution)/shard_map/ppermute | solution.py:72
  640.6 10.0 abs_reduce_fusion.1
  653.7 9.3 abs_reduce_fusion
  696.4 34.4 %collective-permute-done.32 = f16[4,2,584,384]{3,2,0,1:T(8,128)(2,1)} collective-permute-done((f16[4,2,584,384]{3,2,0,1:T(8,128)(2,1)}, f16[4,2,584,384]{3,2,0,1:T(8,128)(2,1)}, u32[]{:S(2)}, u32[]{:S(2)}) %collective-permute-start.32) | collective-permute-done | bytes 3588128 | tf_op jit(solution)/shard_map/ppermute | solution.py:72
  742.6 11.5 %all-to-all-start.5 = ((f32[16,160,48]{1,2,0:T(8,128)}), f32[16,160,48]{1,2,0:T(8,128)S(1)}, u32[]{:S(2)}, u32[]{:S(2)}) async-start(f32[16,160,48]{1,2,0:T(8,128)} %bitcast.132), calls=%async_computation.5 | async-start | bytes 1572864 | tf_op jit(solution)/shard_map/all_to_all | solution.py:906
  761.3 20.0 %all-to-all-done.5 = f32[16,160,48]{1,2,0:T(8,128)S(1)} async-done(((f32[16,160,48]{1,2,0:T(8,128)}), f32[16,160,48]{1,2,0:T(8,128)S(1)}, u32[]{:S(2)}, u32[]{:S(2)}) %all-to-all-start.5) | async-done | bytes 491552 | tf_op jit(solution)/shard_map/all_to_all | solution.py:906
  788.6 21.1 %collective-permute-done.38 = f16[584,384]{1,0:T(8,128)(2,1)S(1)} collective-permute-done((f16[584,384]{1,0:T(8,128)(2,1)}, f16[584,384]{1,0:T(8,128)(2,1)S(1)}, u32[]{:S(2)}, u32[]{:S(2)}) %collective-permute-start.38) | collective-permute-done | bytes 448544 | tf_op jit(solution)/shard_map/ppermute | solution.py:72
  822.7 20.3 %shard_map.435 = f32[3200,768]{1,0:T(8,128)} custom-call(s32[1,2048]{1,0:T(1,128)} %bitcast.658, bf16[2048,768]{1,0:T(8,128)(2,1)} %all-gather.3.cloned.1.call-done.part_ref, f32[3200,768]{1,0:T(8,128)} %shard_map.434.total_ref), custom_call_target="tpu_custom_call", output_to_operand_aliasing={{}: (2, {})} | custom-call | flops 10066329600 | bytes 22806528 | tf_op jit(solution)/shard_map/pallas_call | solution.py:704
  845.0 11.6 %collective-permute-start.36 = (f16[584,384]{1,0:T(8,128)(2,1)}, f16[584,384]{1,0:T(8,128)(2,1)S(1)}, u32[]{:S(2)}, u32[]{:S(2)}) collective-permute-start(f16[584,384]{1,0:T(8,128)(2,1)} %get-tuple-element.448), channel_id=1, source_target_pairs={{0,12},{1,13},{2,14},{3,15},{4,0},{5,1},{6,2},{7,3},{8,4},{9,5},{1... | collective-permute-start | bytes 1345544 | tf_op jit(solution)/shard_map/ppermute | solution.py:72
  861.8 5.8 collective-permute-done.36
  868.8 26.2 %collective-permute-done.35 = f16[584,384]{1,0:T(8,128)(2,1)} collective-permute-done((f16[584,384]{1,0:T(8,128)(2,1)}, f16[584,384]{1,0:T(8,128)(2,1)}, u32[]{:S(2)}, u32[]{:S(2)}) %collective-permute-start.35) | collective-permute-done | bytes 448544 | tf_op jit(solution)/shard_map/ppermute | solution.py:72
  898.8 11.7 %slice_add_fusion = f32[3144,768]{1,0:T(8,128)} fusion(f32[3200,768]{1,0:T(8,128)} %collective-permute-done.40, f32[3200,768]{1,0:T(8,128)} %shard_map.435), kind=kLoop, calls=%fused_computation.5 | loop fusion | flops 2414592 | bytes 28975104 | tf_op jit(solution)/shard_map/add | solution.py:913
  931.4 11.2 all_to_all.56
  952.4 4.7 all_to_all.57
  957.4 33.6 %all_to_all.58 = f16[8,104,768]{2,1,0:T(8,128)(2,1)S(1)} all-to-all(f16[8,104,768]{2,1,0:T(8,128)(2,1)S(1)} %bitcast.558), channel_id=1, replica_groups=mesh['section'=2,'za'=4,'yb'=2,'yc'=1,'xd'=2] {'za','yb'}, dimensions={0} | all-to-all | bytes 2555904 | tf_op jit(solution)/shard_map/all_to_all | solution.py:733
  1007.0 15.6 %collective-permute-done.43 = f32[3,256,256]{2,1,0:T(8,128)} collective-permute-done((f32[3,256,256]{2,1,0:T(8,128)}, f32[3,256,256]{2,1,0:T(8,128)}, u32[]{:S(2)}, u32[]{:S(2)}) %collective-permute-start.43) | collective-permute-done | bytes 786464 | tf_op jit(solution)/shard_map/ppermute | solution.py:41
  1034.8 38.1 %shard_map.436 = f32[768,768]{1,0:T(8,128)S(1)} custom-call(f32[6,256,256]{2,1,0:T(8,128)S(1)} %maximum_select_fusion.1.gram_ref), custom_call_target="tpu_custom_call" | custom-call | flops 30802968576 | bytes 4718592 | tf_op jit(solution)/shard_map/pallas_call | solution.py:544
  1080.6 26.1 %fusion.172 = (bf16[3144,768]{1,0:T(8,128)(2,1)}, f32[3144,768]{1,0:T(8,128)}, f32[3144,768]{1,0:T(8,128)}, f32[3144,768]{1,0:T(8,128)}) fusion(f32[3144,768]{1,0:T(8,128)} %param.26, f32[3144,768]{1,0:T(8,128)} %slice_add_fusion, f32[]{:T(128)S(6)} %min.33, f32[3144,768]{1,0:T(8,128)} %param.27, f32[3144,768]{1,0:T(8,128)} %param.28), kind=kLoop, calls=%fused_computation.543 | loop fusion | flops 41048064 | bytes 72437760 | tf_op jit(solution)/shard_map/convert_element_type | solution.py:974
  (855 shorter events, 375.1 us)
Async XLA Ops:
  10.7 18.6 %collective-permute-start.5 = (bf16[576,384]{1,0:T(8,128)(2,1)S(1)}, bf16[576,384]{1,0:T(8,128)(2,1)S(1)}, u32[]{:S(2)}, u32[]{:S(2)}) collective-permute-start(bf16[576,384]{1,0:T(8,128)(2,1)S(1)} %constant_dynamic-slice_fusion.10), channel_id=1, source_target_pairs={{0,16},{16,0},{1,17},{17,1},{2,18},{18,2},{3,19},{19,3},{4,20},{20... | collective-permute-start | bytes 1327112 | tf_op jit(solution)/shard_map/ppermute | solution.py:41
  14.4 21.1 %all-to-all-start = ((bf16[16,171,48]{1,2,0:T(8,128)(2,1)}), bf16[16,171,48]{1,2,0:T(8,128)(2,1)S(1)}, u32[]{:S(2)}, u32[]{:S(2)}) async-start(bf16[16,171,48]{1,2,0:T(8,128)(2,1)} %broadcast_in_dim.220), calls=%async_computation | async-start | bytes 786432 | tf_op jit(solution)/shard_map/all_to_all | solution.py:47
  29.5 15.0 %collective-permute-start.8 = (bf16[576,384]{1,0:T(8,128)(2,1)S(1)}, bf16[576,384]{1,0:T(8,128)(2,1)S(1)}, u32[]{:S(2)}, u32[]{:S(2)}) collective-permute-start(bf16[576,384]{1,0:T(8,128)(2,1)S(1)} %get-tuple-element.463), channel_id=1, source_target_pairs={{0,4},{1,5},{2,6},{3,7},{4,8},{5,9},{6,10},{7,11},{8,12},{9,13},{1... | collective-permute-start | bytes 1327112 | tf_op jit(solution)/shard_map/ppermute | solution.py:72
  31.5 31.9 %collective-permute-start.7 = (bf16[576,384]{1,0:T(8,128)(2,1)S(1)}, bf16[576,384]{1,0:T(8,128)(2,1)S(1)}, u32[]{:S(2)}, u32[]{:S(2)}) collective-permute-start(bf16[576,384]{1,0:T(8,128)(2,1)S(1)} %get-tuple-element.463), channel_id=1, source_target_pairs={{0,8},{1,9},{2,10},{3,11},{4,12},{5,13},{6,14},{7,15},{8,0},{9,1},... | collective-permute-start | bytes 1327112 | tf_op jit(solution)/shard_map/ppermute | solution.py:72
  33.8 29.5 %collective-permute-start.6 = (bf16[576,384]{1,0:T(8,128)(2,1)S(1)}, bf16[576,384]{1,0:T(8,128)(2,1)S(1)}, u32[]{:S(2)}, u32[]{:S(2)}) collective-permute-start(bf16[576,384]{1,0:T(8,128)(2,1)S(1)} %get-tuple-element.463), channel_id=1, source_target_pairs={{0,12},{1,13},{2,14},{3,15},{4,0},{5,1},{6,2},{7,3},{8,4},{9,5},{1... | collective-permute-start | bytes 1327112 | tf_op jit(solution)/shard_map/ppermute | solution.py:72
  65.8 26.0 %collective-permute-start.9 = (bf16[4,576,384]{2,1,0:T(8,128)(2,1)}, bf16[4,576,384]{2,1,0:T(8,128)(2,1)S(1)}, u32[]{:S(2)}, u32[]{:S(2)}) collective-permute-start(bf16[4,576,384]{2,1,0:T(8,128)(2,1)} %maximum_add_fusion.1), channel_id=1, source_target_pairs={{0,1},{1,0},{2,3},{3,2},{4,5},{5,4},{6,7},{7,6},{8,9},{9,8},{10,11... | collective-permute-start | bytes 5308424 | tf_op jit(solution)/shard_map/ppermute | solution.py:72
  83.2 29.4 %collective-permute-start = (bf16[4,2,128,768]{3,2,0,1:T(8,128)(2,1)S(1)}, bf16[4,2,128,768]{3,2,0,1:T(8,128)(2,1)S(1)}, u32[]{:S(2)}, u32[]{:S(2)}) collective-permute-start(bf16[4,2,128,768]{3,2,0,1:T(8,128)(2,1)S(1)} %bitcast_select_fusion.4), channel_id=1, source_target_pairs={{0,2},{1,3},{2,0},{3,1},{4,6},{5,7},{6,4},{7,5},{8,10},{9,11},{10,... | collective-permute-start | bytes 4718600 | tf_op jit(solution)/shard_map/ppermute | solution.py:72
  93.9 71.8 %collective-permute-start.10 = (bf16[2,4,576,384]{3,2,1,0:T(8,128)(2,1)}, bf16[2,4,576,384]{3,2,1,0:T(8,128)(2,1)}, u32[]{:S(2)}, u32[]{:S(2)}) collective-permute-start(bf16[2,4,576,384]{3,2,1,0:T(8,128)(2,1)} %pad_maximum_fusion.7), channel_id=1, source_target_pairs={{0,2},{1,3},{2,0},{3,1},{4,6},{5,7},{6,4},{7,5},{8,10},{9,11},{10,... | collective-permute-start | bytes 10616840 | tf_op jit(solution)/shard_map/ppermute | solution.py:72
  100.4 22.2 %collective-permute-start.15 = (bf16[576,384]{1,0:T(8,128)(2,1)S(1)}, bf16[576,384]{1,0:T(8,128)(2,1)S(1)}, u32[]{:S(2)}, u32[]{:S(2)}) collective-permute-start(bf16[576,384]{1,0:T(8,128)(2,1)S(1)} %broadcast_add_fusion.3), channel_id=1, source_target_pairs={{0,4},{1,5},{2,6},{3,7},{4,8},{5,9},{6,10},{7,11},{8,12},{9,13},{1... | collective-permute-start | bytes 1327112 | tf_op jit(solution)/shard_map/ppermute | solution.py:72
  109.9 25.5 %collective-permute-start.14 = (bf16[576,384]{1,0:T(8,128)(2,1)S(1)}, bf16[576,384]{1,0:T(8,128)(2,1)S(1)}, u32[]{:S(2)}, u32[]{:S(2)}) collective-permute-start(bf16[576,384]{1,0:T(8,128)(2,1)S(1)} %broadcast_add_fusion.3), channel_id=1, source_target_pairs={{0,8},{1,9},{2,10},{3,11},{4,12},{5,13},{6,14},{7,15},{8,0},{9,1},... | collective-permute-start | bytes 1327112 | tf_op jit(solution)/shard_map/ppermute | solution.py:72
  112.0 23.4 %collective-permute-start.13 = (bf16[576,384]{1,0:T(8,128)(2,1)S(1)}, bf16[576,384]{1,0:T(8,128)(2,1)S(1)}, u32[]{:S(2)}, u32[]{:S(2)}) collective-permute-start(bf16[576,384]{1,0:T(8,128)(2,1)S(1)} %broadcast_add_fusion.3), channel_id=1, source_target_pairs={{0,12},{1,13},{2,14},{3,15},{4,0},{5,1},{6,2},{7,3},{8,4},{9,5},{1... | collective-permute-start | bytes 1327112 | tf_op jit(solution)/shard_map/ppermute | solution.py:72
  135.7 26.5 %collective-permute-start.16 = (bf16[4,576,384]{2,1,0:T(8,128)(2,1)S(1)}, bf16[4,576,384]{2,1,0:T(8,128)(2,1)S(1)}, u32[]{:S(2)}, u32[]{:S(2)}) collective-permute-start(bf16[4,576,384]{2,1,0:T(8,128)(2,1)S(1)} %maximum_add_fusion.3), channel_id=1, source_target_pairs={{0,1},{1,0},{2,3},{3,2},{4,5},{5,4},{6,7},{7,6},{8,9},{9,8},{10,11... | collective-permute-start | bytes 5308424 | tf_op jit(solution)/shard_map/ppermute | solution.py:72
  164.4 54.9 %collective-permute-start.17 = (bf16[2,4,576,384]{3,2,1,0:T(8,128)(2,1)}, bf16[2,4,576,384]{3,2,1,0:T(8,128)(2,1)}, u32[]{:S(2)}, u32[]{:S(2)}) collective-permute-start(bf16[2,4,576,384]{3,2,1,0:T(8,128)(2,1)} %pad_maximum_fusion.8), channel_id=1, source_target_pairs={{0,2},{1,3},{2,0},{3,1},{4,6},{5,7},{6,4},{7,5},{8,10},{9,11},{10,... | collective-permute-start | bytes 10616840 | tf_op jit(solution)/shard_map/ppermute | solution.py:72
  165.7 54.1 %collective-permute-start.11 = (bf16[2,4,576,384]{3,2,1,0:T(8,128)(2,1)}, bf16[2,4,576,384]{3,2,1,0:T(8,128)(2,1)}, u32[]{:S(2)}, u32[]{:S(2)}) collective-permute-start(bf16[2,4,576,384]{3,2,1,0:T(8,128)(2,1)} %pad_maximum_fusion.7), channel_id=1, source_target_pairs={{0,16},{16,0},{1,17},{17,1},{2,18},{18,2},{3,19},{19,3},{4,20},{20... | collective-permute-start | bytes 10616840 | tf_op jit(solution)/shard_map/ppermute | solution.py:41
  165.7 54.1 %collective-permute-start.12 = (bf16[2,4,576,384]{3,2,1,0:T(8,128)(2,1)}, bf16[2,4,576,384]{3,2,1,0:T(8,128)(2,1)}, u32[]{:S(2)}, u32[]{:S(2)}) collective-permute-start(bf16[2,4,576,384]{3,2,1,0:T(8,128)(2,1)} %collective-permute-done.10), channel_id=1, source_target_pairs={{0,16},{16,0},{1,17},{17,1},{2,18},{18,2},{3,19},{19,3},{4,20},{20... | collective-permute-start | bytes 10616840 | tf_op jit(solution)/shard_map/ppermute | solution.py:41
  167.2 20.8 %collective-permute-start.1 = (bf16[4,128,768]{2,1,0:T(8,128)(2,1)}, bf16[4,128,768]{2,1,0:T(8,128)(2,1)}, u32[]{:S(2)}, u32[]{:S(2)}) collective-permute-start(bf16[4,128,768]{2,1,0:T(8,128)(2,1)} %dynamic-slice_bitcast_fusion.4), channel_id=1, source_target_pairs={{0,1},{1,0},{2,3},{3,2},{4,5},{5,4},{6,7},{7,6},{8,9},{9,8},{10,11... | collective-permute-start | bytes 2359304 | tf_op jit(solution)/shard_map/ppermute | solution.py:72
  189.3 16.1 %collective-permute-start.4 = (bf16[128,768]{1,0:T(8,128)(2,1)S(1)}, bf16[128,768]{1,0:T(8,128)(2,1)S(1)}, u32[]{:S(2)}, u32[]{:S(2)}) collective-permute-start(bf16[128,768]{1,0:T(8,128)(2,1)S(1)} %get-tuple-element.467), channel_id=1, source_target_pairs={{0,12},{1,13},{2,14},{3,15},{4,0},{5,1},{6,2},{7,3},{8,4},{9,5},{1... | collective-permute-start | bytes 589832 | tf_op jit(solution)/shard_map/ppermute | solution.py:72
  200.1 17.0 %collective-permute-start.3 = (bf16[128,768]{1,0:T(8,128)(2,1)S(1)}, bf16[128,768]{1,0:T(8,128)(2,1)S(1)}, u32[]{:S(2)}, u32[]{:S(2)}) collective-permute-start(bf16[128,768]{1,0:T(8,128)(2,1)S(1)} %get-tuple-element.468), channel_id=1, source_target_pairs={{0,8},{1,9},{2,10},{3,11},{4,12},{5,13},{6,14},{7,15},{8,0},{9,1},... | collective-permute-start | bytes 589832 | tf_op jit(solution)/shard_map/ppermute | solution.py:72
  205.4 13.2 %collective-permute-start.2 = (bf16[128,768]{1,0:T(8,128)(2,1)S(1)}, bf16[128,768]{1,0:T(8,128)(2,1)S(1)}, u32[]{:S(2)}, u32[]{:S(2)}) collective-permute-start(bf16[128,768]{1,0:T(8,128)(2,1)S(1)} %get-tuple-element.466), channel_id=1, source_target_pairs={{0,4},{1,5},{2,6},{3,7},{4,8},{5,9},{6,10},{7,11},{8,12},{9,13},{1... | collective-permute-start | bytes 589832 | tf_op jit(solution)/shard_map/ppermute | solution.py:72
  219.3 28.7 %collective-permute-start.18 = (bf16[2,4,576,384]{3,2,1,0:T(8,128)(2,1)}, bf16[2,4,576,384]{3,2,1,0:T(8,128)(2,1)}, u32[]{:S(2)}, u32[]{:S(2)}) collective-permute-start(bf16[2,4,576,384]{3,2,1,0:T(8,128)(2,1)} %pad_maximum_fusion.8), channel_id=1, source_target_pairs={{0,16},{16,0},{1,17},{17,1},{2,18},{18,2},{3,19},{19,3},{4,20},{20... | collective-permute-start | bytes 10616840 | tf_op jit(solution)/shard_map/ppermute | solution.py:41
  219.3 28.6 %collective-permute-start.19 = (bf16[2,4,576,384]{3,2,1,0:T(8,128)(2,1)}, bf16[2,4,576,384]{3,2,1,0:T(8,128)(2,1)}, u32[]{:S(2)}, u32[]{:S(2)}) collective-permute-start(bf16[2,4,576,384]{3,2,1,0:T(8,128)(2,1)} %collective-permute-done.17), channel_id=1, source_target_pairs={{0,16},{16,0},{1,17},{17,1},{2,18},{18,2},{3,19},{19,3},{4,20},{20... | collective-permute-start | bytes 10616840 | tf_op jit(solution)/shard_map/ppermute | solution.py:41
  276.1 11.3 %collective-permute-start.22 = (bf16[128,768]{1,0:T(8,128)(2,1)S(1)}, bf16[128,768]{1,0:T(8,128)(2,1)S(1)}, u32[]{:S(2)}, u32[]{:S(2)}) collective-permute-start(bf16[128,768]{1,0:T(8,128)(2,1)S(1)} %add_convert_fusion.1), channel_id=1, source_target_pairs={{0,4},{1,5},{2,6},{3,7},{4,8},{5,9},{6,10},{7,11},{8,12},{9,13},{1... | collective-permute-start | bytes 589832 | tf_op jit(solution)/shard_map/ppermute | solution.py:72
  280.5 15.2 %collective-permute-start.21 = (bf16[128,768]{1,0:T(8,128)(2,1)S(1)}, bf16[128,768]{1,0:T(8,128)(2,1)S(1)}, u32[]{:S(2)}, u32[]{:S(2)}) collective-permute-start(bf16[128,768]{1,0:T(8,128)(2,1)S(1)} %add_convert_fusion.1), channel_id=1, source_target_pairs={{0,8},{1,9},{2,10},{3,11},{4,12},{5,13},{6,14},{7,15},{8,0},{9,1},... | collective-permute-start | bytes 589832 | tf_op jit(solution)/shard_map/ppermute | solution.py:72
  282.2 13.6 %collective-permute-start.20 = (bf16[128,768]{1,0:T(8,128)(2,1)S(1)}, bf16[128,768]{1,0:T(8,128)(2,1)S(1)}, u32[]{:S(2)}, u32[]{:S(2)}) collective-permute-start(bf16[128,768]{1,0:T(8,128)(2,1)S(1)} %add_convert_fusion.1), channel_id=1, source_target_pairs={{0,12},{1,13},{2,14},{3,15},{4,0},{5,1},{6,2},{7,3},{8,4},{9,5},{1... | collective-permute-start | bytes 589832 | tf_op jit(solution)/shard_map/ppermute | solution.py:72
  295.8 12.1 %collective-permute-start.23 = (bf16[4,128,768]{2,1,0:T(8,128)(2,1)S(1)}, bf16[4,128,768]{2,1,0:T(8,128)(2,1)S(1)}, u32[]{:S(2)}, u32[]{:S(2)}) collective-permute-start(bf16[4,128,768]{2,1,0:T(8,128)(2,1)S(1)} %get-tuple-element.465), channel_id=1, source_target_pairs={{0,1},{1,0},{2,3},{3,2},{4,5},{5,4},{6,7},{7,6},{8,9},{9,8},{10,11... | collective-permute-start | bytes 2359304 | tf_op jit(solution)/shard_map/ppermute | solution.py:72
  310.1 20.8 %collective-permute-start.24 = (bf16[2,4,128,768]{3,2,1,0:T(8,128)(2,1)}, bf16[2,4,128,768]{3,2,1,0:T(8,128)(2,1)}, u32[]{:S(2)}, u32[]{:S(2)}) collective-permute-start(bf16[2,4,128,768]{3,2,1,0:T(8,128)(2,1)} %pad_maximum_fusion.14), channel_id=1, source_target_pairs={{0,2},{1,3},{2,0},{3,1},{4,6},{5,7},{6,4},{7,5},{8,10},{9,11},{10,... | collective-permute-start | bytes 4718600 | tf_op jit(solution)/shard_map/ppermute | solution.py:72
  372.0 24.0 %all-to-all-start.1 = ((f32[16,3,2048]{2,1,0:T(4,128)}), f32[16,3,2048]{2,1,0:T(4,128)S(1)}, u32[]{:S(2)}, u32[]{:S(2)}) async-start(f32[16,3,2048]{2,1,0:T(4,128)} %broadcast_in_dim.237), calls=%async_computation.1 | async-start | bytes 1048576 | tf_op jit(solution)/shard_map/all_to_all | solution.py:47
  395.9 34.0 %all-to-all-start.3 = ((f16[8,104,768]{2,1,0:T(8,128)(2,1)}), f16[8,104,768]{2,1,0:T(8,128)(2,1)}, u32[]{:S(2)}, u32[]{:S(2)}) async-start(f16[8,104,768]{2,1,0:T(8,128)(2,1)} %bitcast.557), calls=%async_computation.3 | async-start | bytes 2555904 | tf_op jit(solution)/shard_map/all_to_all | solution.py:733
  439.2 65.3 %all-to-all-start.4 = ((bf16[16,128,768]{2,1,0:T(8,128)(2,1)}), bf16[16,128,768]{2,1,0:T(8,128)(2,1)}, u32[]{:S(2)}, u32[]{:S(2)}) async-start(bf16[16,128,768]{2,1,0:T(8,128)(2,1)} %bitcast.537), calls=%async_computation.4 | async-start | bytes 6291456 | tf_op jit(solution)/shard_map/all_to_all | solution.py:880
  443.8 378.9 %all-gather.3.cloned.1.call-start = ((), (), s32[]{:S(2)}) async-start(), calls=%async_computation.11 | async-start | bytes 3342336 | tf_op jit(solution)/shard_map/all_gather | solution.py:903
  445.5 80.2 %collective-permute-start.26 = (bf16[128,5376]{1,0:T(8,128)(2,1)}, bf16[128,5376]{1,0:T(8,128)(2,1)}, u32[]{:S(2)}, u32[]{:S(2)}) collective-permute-start(bf16[128,5376]{1,0:T(8,128)(2,1)} %pad_maximum_fusion.15), channel_id=1, source_target_pairs={{0,16},{16,0},{1,17},{17,1},{2,18},{18,2},{3,19},{19,3},{4,20},{20... | collective-permute-start | bytes 4128776 | tf_op jit(solution)/shard_map/ppermute | solution.py:41
  523.3 11.0 collective-permute-start.25
  555.1 44.9 %collective-permute-start.28 = (f16[4,2,584,384]{3,2,0,1:T(8,128)(2,1)}, f16[4,2,584,384]{3,2,0,1:T(8,128)(2,1)S(1)}, u32[]{:S(2)}, u32[]{:S(2)}) collective-permute-start(f16[4,2,584,384]{3,2,0,1:T(8,128)(2,1)} %bitcast_select_fusion.3), channel_id=1, source_target_pairs={{0,2},{1,3},{2,0},{3,1},{4,6},{5,7},{6,4},{7,5},{8,10},{9,11},{10,... | collective-permute-start | bytes 10764296 | tf_op jit(solution)/shard_map/ppermute | solution.py:72
  561.0 79.7 %collective-permute-start.31 = (bf16[128,5376]{1,0:T(8,128)(2,1)}, bf16[128,5376]{1,0:T(8,128)(2,1)}, u32[]{:S(2)}, u32[]{:S(2)}) collective-permute-start(bf16[128,5376]{1,0:T(8,128)(2,1)} %pad_maximum_fusion.16), channel_id=1, source_target_pairs={{0,16},{16,0},{1,17},{17,1},{2,18},{18,2},{3,19},{19,3},{4,20},{20... | collective-permute-start | bytes 4128776 | tf_op jit(solution)/shard_map/ppermute | solution.py:41
  609.6 23.1 %collective-permute-start.29 = (f16[4,584,384]{2,1,0:T(8,128)(2,1)}, f16[4,584,384]{2,1,0:T(8,128)(2,1)}, u32[]{:S(2)}, u32[]{:S(2)}) collective-permute-start(f16[4,584,384]{2,1,0:T(8,128)(2,1)} %get-tuple-element.424), channel_id=1, source_target_pairs={{0,1},{1,0},{2,3},{3,2},{4,5},{5,4},{6,7},{7,6},{8,9},{9,8},{10,11... | collective-permute-start | bytes 5382152 | tf_op jit(solution)/shard_map/ppermute | solution.py:72
  640.6 13.1 %collective-permute-start.30 = (bf16[128,6912]{1,0:T(8,128)(2,1)}, bf16[128,6912]{1,0:T(8,128)(2,1)}, u32[]{:S(2)}, u32[]{:S(2)}) collective-permute-start(bf16[128,6912]{1,0:T(8,128)(2,1)} %pad_maximum_fusion.13), channel_id=1, source_target_pairs={{0,16},{16,0},{1,17},{17,1},{2,18},{18,2},{3,19},{19,3},{4,20},{20... | collective-permute-start | bytes 5308424 | tf_op jit(solution)/shard_map/ppermute | solution.py:41
  684.2 46.5 %collective-permute-start.32 = (f16[4,2,584,384]{3,2,0,1:T(8,128)(2,1)}, f16[4,2,584,384]{3,2,0,1:T(8,128)(2,1)}, u32[]{:S(2)}, u32[]{:S(2)}) collective-permute-start(f16[4,2,584,384]{3,2,0,1:T(8,128)(2,1)} %bitcast_select_fusion), channel_id=1, source_target_pairs={{0,2},{1,3},{2,0},{3,1},{4,6},{5,7},{6,4},{7,5},{8,10},{9,11},{10,... | collective-permute-start | bytes 10764296 | tf_op jit(solution)/shard_map/ppermute | solution.py:72
  739.7 74.9 %collective-permute-start.33 = (f16[4,584,384]{2,1,0:T(8,128)(2,1)}, f16[4,584,384]{2,1,0:T(8,128)(2,1)}, u32[]{:S(2)}, u32[]{:S(2)}) collective-permute-start(f16[4,584,384]{2,1,0:T(8,128)(2,1)} %get-tuple-element.422), channel_id=1, source_target_pairs={{0,1},{1,0},{2,3},{3,2},{4,5},{5,4},{6,7},{7,6},{8,9},{9,8},{10,11... | collective-permute-start | bytes 5382152 | tf_op jit(solution)/shard_map/ppermute | solution.py:72
  742.6 38.6 %all-to-all-start.5 = ((f32[16,160,48]{1,2,0:T(8,128)}), f32[16,160,48]{1,2,0:T(8,128)S(1)}, u32[]{:S(2)}, u32[]{:S(2)}) async-start(f32[16,160,48]{1,2,0:T(8,128)} %bitcast.132), calls=%async_computation.5 | async-start | bytes 1572864 | tf_op jit(solution)/shard_map/all_to_all | solution.py:906
  755.6 31.8 %collective-permute-start.37 = (f16[584,384]{1,0:T(8,128)(2,1)}, f16[584,384]{1,0:T(8,128)(2,1)S(1)}, u32[]{:S(2)}, u32[]{:S(2)}) collective-permute-start(f16[584,384]{1,0:T(8,128)(2,1)} %get-tuple-element.454), channel_id=1, source_target_pairs={{0,4},{1,5},{2,6},{3,7},{4,8},{5,9},{6,10},{7,11},{8,12},{9,13},{1... | collective-permute-start | bytes 1345544 | tf_op jit(solution)/shard_map/ppermute | solution.py:72
  757.5 52.2 %collective-permute-start.38 = (f16[584,384]{1,0:T(8,128)(2,1)}, f16[584,384]{1,0:T(8,128)(2,1)S(1)}, u32[]{:S(2)}, u32[]{:S(2)}) collective-permute-start(f16[584,384]{1,0:T(8,128)(2,1)} %get-tuple-element.453), channel_id=1, source_target_pairs={{0,8},{1,9},{2,10},{3,11},{4,12},{5,13},{6,14},{7,15},{8,0},{9,1},... | collective-permute-start | bytes 1345544 | tf_op jit(solution)/shard_map/ppermute | solution.py:72
  759.8 51.0 %collective-permute-start.39 = (f16[584,384]{1,0:T(8,128)(2,1)}, f16[584,384]{1,0:T(8,128)(2,1)}, u32[]{:S(2)}, u32[]{:S(2)}) collective-permute-start(f16[584,384]{1,0:T(8,128)(2,1)} %get-tuple-element.452), channel_id=1, source_target_pairs={{0,12},{1,13},{2,14},{3,15},{4,0},{5,1},{6,2},{7,3},{8,4},{9,5},{1... | collective-permute-start | bytes 1345544 | tf_op jit(solution)/shard_map/ppermute | solution.py:72
  843.0 55.8 %collective-permute-start.40 = (f32[3200,768]{1,0:T(8,128)}, f32[3200,768]{1,0:T(8,128)}, u32[]{:S(2)}, u32[]{:S(2)}) collective-permute-start(f32[3200,768]{1,0:T(8,128)} %shard_map.435), channel_id=1, source_target_pairs={{0,16},{16,0},{1,17},{17,1},{2,18},{18,2},{3,19},{19,3},{4,20},{20... | collective-permute-start | bytes 29491208 | tf_op jit(solution)/shard_map/ppermute | solution.py:41
  845.0 22.6 %collective-permute-start.36 = (f16[584,384]{1,0:T(8,128)(2,1)}, f16[584,384]{1,0:T(8,128)(2,1)S(1)}, u32[]{:S(2)}, u32[]{:S(2)}) collective-permute-start(f16[584,384]{1,0:T(8,128)(2,1)} %get-tuple-element.448), channel_id=1, source_target_pairs={{0,12},{1,13},{2,14},{3,15},{4,0},{5,1},{6,2},{7,3},{8,4},{9,5},{1... | collective-permute-start | bytes 1345544 | tf_op jit(solution)/shard_map/ppermute | solution.py:72
  856.6 38.5 %collective-permute-start.35 = (f16[584,384]{1,0:T(8,128)(2,1)}, f16[584,384]{1,0:T(8,128)(2,1)}, u32[]{:S(2)}, u32[]{:S(2)}) collective-permute-start(f16[584,384]{1,0:T(8,128)(2,1)} %get-tuple-element.449), channel_id=1, source_target_pairs={{0,8},{1,9},{2,10},{3,11},{4,12},{5,13},{6,14},{7,15},{8,0},{9,1},... | collective-permute-start | bytes 1345544 | tf_op jit(solution)/shard_map/ppermute | solution.py:72
  856.6 40.4 %collective-permute-start.34 = (f16[584,384]{1,0:T(8,128)(2,1)}, f16[584,384]{1,0:T(8,128)(2,1)}, u32[]{:S(2)}, u32[]{:S(2)}) collective-permute-start(f16[584,384]{1,0:T(8,128)(2,1)} %get-tuple-element.450), channel_id=1, source_target_pairs={{0,4},{1,5},{2,6},{3,7},{4,8},{5,9},{6,10},{7,11},{8,12},{9,13},{1... | collective-permute-start | bytes 1345544 | tf_op jit(solution)/shard_map/ppermute | solution.py:72
  1002.7 20.0 %collective-permute-start.43 = (f32[3,256,256]{2,1,0:T(8,128)}, f32[3,256,256]{2,1,0:T(8,128)}, u32[]{:S(2)}, u32[]{:S(2)}) collective-permute-start(f32[3,256,256]{2,1,0:T(8,128)} %select_add_fusion), channel_id=1, source_target_pairs={{0,1},{1,0},{2,3},{3,2},{4,5},{5,4},{6,7},{7,6},{8,9},{9,8},{10,11... | collective-permute-start | bytes 2359304 | tf_op jit(solution)/shard_map/ppermute | solution.py:41
  1076.9 33.0 %all-to-all-start.9 = ((f16[8,96,768]{2,1,0:T(8,128)(2,1)}), f16[8,96,768]{2,1,0:T(8,128)(2,1)S(1)}, u32[]{:S(2)}, u32[]{:S(2)}) async-start(f16[8,96,768]{2,1,0:T(8,128)(2,1)} %bitcast.206), calls=%async_computation.9 | async-start | bytes 2359296 | tf_op jit(solution)/shard_map/all_to_all | solution.py:744
  (203 other events, 2448.1 us)
Sparse Core Ops, SparseCore 0:
  688.4 88.6 all-gather.2
